TPU v7x, 256 devices: a whole 4x4x8 slice. The times are simulated.
256 devices in a mesh: ctx: 16 (over x, y), tp: 8 (over z), dp: 2 (over core).
Axes of the slice: x: 4, y: 4, z: 8, core: 2. Of those that a mesh axis runs over, the one named last changes fastest.
Arguments:
- projected: bfloat16 [3, 8192, 4096], P(None, ('dp', 'ctx'), 'tp'), parts along dimension 1, may hold values from -6 to 6
- short_taps: float32 [3, 7, 4096], P(None, None, 'tp'), may hold values from -2 to 2
- long_filter: float32 [4096, 4096], P('ctx', 'tp'), may hold values from -2 to 2, as said below
- skip_gain: float32 [4096], P('tp'), may hold values from -1 to 1
- w_out: bfloat16 [4096, 4096], P('tp'), may hold values from -0.125 to 0.125
Outputs:
- hyena_out: bfloat16 [8192, 4096], P(('dp', 'ctx'), 'tp'), parts along dimension 0
There are 2 independent parts, one for each index of `dp`. A program takes and returns all parts, laid end to end along the dimension named above; an argument that names none is the same for every part. Nothing has to cross between parts.
Inputs may be any that keep to these rules, and one draw needn't show every extreme that they name: `long_filter`: taps of each channel's causal filter.
All inputs are finite; a program needn't handle non-finite values.
Results may differ from a plain program's by a relative error of at most 0.014.
Values may be sent and summed in bfloat16 or wider, within the bound.
No kernel may reach another device: no remote copies, remote signals or barrier semaphores. Data moves between devices by JAX's collectives and lax.ppermute only.
A program may use at most 64 MiB of HBM per device.

v0:
```python
import jax
import jax.numpy as jnp
import numpy as np
from jax import lax
from jax.experimental import pallas as pl
from jax.experimental.pallas import tpu as pltpu
from jax.sharding import PartitionSpec as P

TAPS = 7
LANES = 128
BF16 = jnp.bfloat16
F32 = jnp.float32
MIB = 1024 * 1024


def split_table(table):
    high = table.astype(np.float32).astype(jnp.bfloat16)
    low = (table - high.astype(np.float64)).astype(np.float32).astype(jnp.bfloat16)
    return np.stack([high, low])


def dft_tables(blocks, width, channels):
    angle = 2.0 * np.pi * (np.outer(np.arange(width), np.arange(width)) % width) / width
    cos, sin = np.cos(angle), np.sin(angle)
    lanes = np.block([[cos, -sin], [sin, cos]])
    angle = np.pi * (np.outer(2 * np.arange(blocks) + 1, np.arange(blocks)) % (4 * blocks)) / (2 * blocks)
    cos, sin = np.kron(np.cos(angle), np.eye(channels)), np.kron(np.sin(angle), np.eye(channels))
    scale = 1.0 / (blocks * width)
    tables = (np.concatenate([cos, -sin]), lanes, lanes.T, scale * np.concatenate([cos.T, -sin.T]))
    return [split_table(table).reshape(-1, table.shape[1]) for table in tables]


def twiddles(blocks, width):
    angle = 2.0 * np.pi * np.outer(np.arange(blocks) + 0.5, np.arange(width)) / (2 * blocks * width)
    return np.stack([np.cos(angle), -np.sin(angle)]).astype(np.float32)[:, :, None, :]


def split_bf16(values):
    high = values.astype(BF16)
    return high, (values - high.astype(F32)).astype(BF16)


def dot(a, b):
    return jnp.dot(a, b, preferred_element_type=F32)


def prep_kernel(
    parity_ref, projected_hbm, filter_hbm, w_hbm, out_hbm, w_send, inputs, taps_in, turned, held, sems, w_sems
):
    blocks, quad, rows = turned.shape
    group = quad // 4
    width = w_hbm.shape[0]
    chunks = w_send.shape[1] // width
    arrive = [pltpu.make_async_copy(projected_hbm.at[part], inputs.at[part], sems.at[part]) for part in range(3)]
    arrive.append(pltpu.make_async_copy(filter_hbm, taps_in, sems.at[3]))
    for copy in arrive:
        copy.start()
    w_in, w_out = [], []
    for i in range(chunks):
        start = pl.multiple_of((2 * i + 1 - parity_ref[0]) * width, width)
        columns = slice(i * width, (i + 1) * width)
        w_in.append(pltpu.make_async_copy(w_hbm.at[:, pl.ds(start, width)], held.at[:, columns], w_sems.at[i]))
        w_out.append(pltpu.make_async_copy(held.at[:, columns], w_send.at[:, columns], w_sems.at[chunks + i]))
        w_in[i].start()
    leave = []
    for part in range(4):
        arrive[part].wait()
        source = inputs[part] if part < 3 else taps_in[...].astype(BF16)
        lines = slice(part * group, (part + 1) * group)
        turned[:, lines, :] = source.T.reshape(blocks, group, rows)
        leave.append(pltpu.make_async_copy(turned.at[:, lines], out_hbm.at[:, lines], sems.at[4 + part]))
        leave[part].start()
    for i in range(chunks):
        w_in[i].wait()
        w_out[i].start()
    for copy in leave + w_out:
        copy.wait()


def featurize(recv_ref, taps_ref, query, gated, u_high, u_low):
    blocks, quad, width = recv_ref.shape
    group = quad // 4
    tile = 16
    lane = lax.broadcasted_iota(jnp.int32, (tile, LANES), 1)
    first, second = lane < 1, lane < 2
    zeros = jnp.zeros((tile, LANES), F32)
    for part in (1, 2, 0):
        for c0 in range(0, group, tile):
            lines = slice(c0, c0 + tile)
            t = [
                jnp.broadcast_to(taps_ref[lines, part * TAPS + j : part * TAPS + j + 1], (tile, LANES))
                for j in range(TAPS)
            ]
            before = [zeros] * 4
            for s in range(blocks):
                for l0 in range(0, width, LANES):
                    cols = slice(l0, l0 + LANES)
                    now = recv_ref[s, part * group + c0 : part * group + c0 + tile, cols].astype(F32)
                    turn = [pltpu.roll(now, 1, 1)]
                    one = jnp.where(first, before[0], turn[0])
                    turn.append(pltpu.roll(t[6] * now, 2, 1))
                    level = t[4] * now + t[5] * one + jnp.where(second, before[1], turn[1])
                    turn.append(pltpu.roll(level, 2, 1))
                    level = t[2] * now + t[3] * one + jnp.where(second, before[2], turn[2])
                    turn.append(pltpu.roll(level, 2, 1))
                    level = t[0] * now + t[1] * one + jnp.where(second, before[3], turn[3])
                    before = turn
                    if part == 0:
                        query[s, lines, cols] = level
                    elif part == 1:
                        gated[s, lines, cols] = level
                    else:
                        product = gated[s, lines, cols] * level
                        gated[s, lines, cols] = product
                        at = slice(s * group + c0, s * group + c0 + tile)
                        u_high[at, cols], u_low[at, cols] = split_bf16(product)


def conv_kernel(
    recv_ref, taps_ref, tw_ref, tables_hbm, out_hbm, query, gated, u_high, u_low, b_high, b_low, mixed, tables, sems, out_sems
):
    blocks, quad, width = recv_ref.shape
    group = quad // 4
    rows = blocks * group
    step = rows // 2
    per = blocks // 2
    copies, firsts, start = [], [], 0
    for i, size in enumerate((4 * rows, 4 * width, 4 * width, 4 * rows)):
        firsts.append((start, size))
        copies.append(pltpu.make_async_copy(tables_hbm.at[start : start + size], tables.at[start : start + size], sems.at[i]))
        copies[i].start()
        start += size

    def table(which, low, at=None):
        start, size = firsts[which]
        at = slice(0, size // 2) if at is None else at
        start += low * (size // 2)
        return tables[start + at.start : start + at.stop, :]

    featurize(recv_ref, taps_ref, query, gated, u_high, u_low)
    filter_rows = recv_ref[:, 3 * group :, :].reshape(rows, width)

    def turned(re, im, k0, sign):
        tr, ti = tw_ref[0, k0 : k0 + per], sign * tw_ref[1, k0 : k0 + per]
        re, im = re.reshape(per, group, width), im.reshape(per, group, width)
        return (re * tr - im * ti).reshape(step, width), (re * ti + im * tr).reshape(step, width)

    def lanes(re, im, which):
        high, low = split_bf16(jnp.concatenate([re, im], axis=1))
        out = dot(high, table(which, 0)) + dot(low, table(which, 0)) + dot(high, table(which, 1))
        return out[:, :width], out[:, width:]

    for copy in copies:
        copy.wait()
    for k0 in range(0, blocks, per):
        spectra = []
        for high, low in ((filter_rows, None), (u_high[...], u_low[...])):
            parts = []
            for half in range(2):
                at = slice(half * rows + k0 * group, half * rows + k0 * group + step)
                part = dot(table(0, 0, at), high) + dot(table(0, 1, at), high)
                if low is not None:
                    part = part + dot(table(0, 0, at), low)
                parts.append(part)
            spectra.append(lanes(*turned(*parts, k0, 1.0), 1))
        (hr, hi), (ur, ui) = spectra
        re, im = lanes(hr * ur - hi * ui, hr * ui + hi * ur, 2)
        for half, part in enumerate(turned(re, im, k0, -1.0)):
            at = slice(half * rows + k0 * group, half * rows + k0 * group + step)
            b_high[at], b_low[at] = split_bf16(part)

    out_copies = []
    skip = taps_ref[:, 3 * TAPS : 3 * TAPS + 1][None]
    for s0 in range(0, blocks, per):
        total = None
        for half in range(2):
            at = slice(half * rows + s0 * group, half * rows + s0 * group + step)
            from_rows = slice(half * rows, (half + 1) * rows)
            for t, b in ((0, b_high), (0, b_low), (1, b_high)):
                term = dot(table(3, t, at), b[from_rows])
                total = term if total is None else total + term
        span = slice(s0, s0 + per)
        mixed[span] = (query[span] * (total.reshape(per, group, width) + skip * gated[span])).astype(BF16)
        for twin in range(2):
            i = len(out_copies)
            out_copies.append(pltpu.make_async_copy(mixed.at[span], out_hbm.at[twin, span], out_sems.at[i]))
            out_copies[i].start()
    for copy in out_copies:
        copy.wait()


def project_kernel(index_ref, mixed_ref, w_hbm, other_ref, out_ref, own, sems):
    chunks, rows, width = out_ref.shape
    copies = []
    for i in range(chunks):
        start = pl.multiple_of((2 * i + index_ref[1]) * width, width)
        copies.append(
            pltpu.make_async_copy(w_hbm.at[:, pl.ds(start, width)], own.at[:, i * width : (i + 1) * width], sems.at[i])
        )
        copies[i].start()
    mine = index_ref[0]
    first = mixed_ref[mine].reshape(width, rows).T
    second = mixed_ref[1 - mine].reshape(width, rows).T
    for i in range(chunks):
        columns = slice(i * width, (i + 1) * width)
        total = dot(second, other_ref[:, columns])
        copies[i].wait()
        out_ref[i] = (total + dot(first, own[:, columns])).astype(BF16)


def local(projected, short_taps, long_filter, skip_gain, w_out):
    ctx, tp, dp = lax.axis_size("ctx"), lax.axis_size("tp"), lax.axis_size("dp")
    rows, width = projected.shape[1:]
    group = width // ctx
    me_ctx, me_tp, me_dp = lax.axis_index("ctx"), lax.axis_index("tp"), lax.axis_index("dp")

    def partner(z, d):
        first = d + (z - d) % tp // 2 * 2
        return (first + (1 - (z - d) % tp % 2)) % tp

    pair_route = [(z * dp + d, partner(z, d) * dp + d) for z in range(tp) for d in range(dp)]
    pair_groups = [
        [(c * tp + (first + d + b) % tp) * dp + d for b in range(2) for c in range(ctx)]
        for d in range(dp)
        for first in range(0, tp, 2)
    ]
    parity_groups = [list(range(odd, tp, 2)) for odd in range(2)]
    chunks = tp // 2
    parity = (me_tp % 2).astype(jnp.int32)
    place = ((me_tp - me_dp) % tp % 2).astype(jnp.int32)

    vmem = pl.BlockSpec(memory_space=pltpu.VMEM)
    smem = pl.BlockSpec(memory_space=pltpu.SMEM)
    hbm = pl.BlockSpec(memory_space=pl.ANY)
    params = pltpu.CompilerParams(vmem_limit_bytes=60 * MIB)

    send, w_send = pl.pallas_call(
        prep_kernel,
        in_specs=[smem, hbm, hbm, hbm],
        out_specs=[hbm, hbm],
        out_shape=[
            jax.ShapeDtypeStruct((ctx, 4 * group, rows), BF16),
            jax.ShapeDtypeStruct((width, chunks * width), BF16),
        ],
        scratch_shapes=[
            pltpu.VMEM((3, rows, width), BF16),
            pltpu.VMEM((rows, width), F32),
            pltpu.VMEM((ctx, 4 * group, rows), BF16),
            pltpu.VMEM((width, chunks * width), BF16),
            pltpu.SemaphoreType.DMA((8,)),
            pltpu.SemaphoreType.DMA((2 * chunks,)),
        ],
        compiler_params=params,
        name="prep",
    )(parity[None], projected, long_filter, w_out)
    recv = lax.all_to_all(send, "ctx", 0, 0, tiled=True)
    w_other = lax.ppermute(w_send, ("tp", "dp"), pair_route)

    taps = jnp.concatenate([short_taps.reshape(3 * TAPS, width), skip_gain[None, :]], axis=0)
    taps = lax.dynamic_slice_in_dim(taps, me_ctx * group, group, axis=1).T
    tables = np.concatenate(dft_tables(ctx, rows, group))
    mixed = pl.pallas_call(
        conv_kernel,
        in_specs=[vmem, vmem, vmem, hbm],
        out_specs=hbm,
        out_shape=jax.ShapeDtypeStruct((2, ctx, group, rows), BF16),
        scratch_shapes=[
            pltpu.VMEM((ctx, group, rows), F32),
            pltpu.VMEM((ctx, group, rows), F32),
            pltpu.VMEM((ctx * group, rows), BF16),
            pltpu.VMEM((ctx * group, rows), BF16),
            pltpu.VMEM((2 * ctx * group, rows), BF16),
            pltpu.VMEM((2 * ctx * group, rows), BF16),
            pltpu.VMEM((ctx, group, rows), BF16),
            pltpu.VMEM(tables.shape, BF16),
            pltpu.SemaphoreType.DMA((4,)),
            pltpu.SemaphoreType.DMA((4,)),
        ],
        compiler_params=pltpu.CompilerParams(vmem_limit_bytes=52 * MIB),
        name="conv",
    )(recv, taps, jnp.asarray(twiddles(ctx, rows)), jnp.asarray(tables))
    mixed = lax.all_to_all(
        mixed.reshape(2 * ctx, group, rows), ("ctx", "tp", "dp"), 0, 0, tiled=True, axis_index_groups=pair_groups
    ).reshape(2, ctx, group, rows)

    partial = pl.pallas_call(
        project_kernel,
        in_specs=[smem, vmem, hbm, vmem],
        out_specs=vmem,
        out_shape=jax.ShapeDtypeStruct((chunks, rows, width), BF16),
        scratch_shapes=[
            pltpu.VMEM((width, chunks * width), BF16),
            pltpu.SemaphoreType.DMA((chunks,)),
        ],
        compiler_params=params,
        name="project",
    )(jnp.stack([place, parity]), mixed, w_out, w_other)
    gathered = lax.all_to_all(partial, "tp", 0, 0, tiled=True, axis_index_groups=parity_groups)
    return jnp.sum(gathered.astype(F32), axis=0).astype(BF16)


def solution(mesh):
    in_specs = (
        P(None, ("dp", "ctx"), "tp"),
        P(None, None, "tp"),
        P("ctx", "tp"),
        P("tp"),
        P("tp", None),
    )
    out_specs = P(("dp", "ctx"), "tp")
    return jax.shard_map(local, mesh=mesh, in_specs=in_specs, out_specs=out_specs, check_vma=False)
```

profile of v0, /device:TPU:1, one launch (start us, length us, event | category | flops | bytes accessed | tf_op | source)
XLA Modules:
  0.0 119.9 jit_solution(9463289045255337733)
XLA Ops:
  0.0 0.0 copy-start
  0.0 0.0 copy-start.3
  0.0 0.0 copy-start.4
  0.0 3.5 %prep.1 = (bf16[16,128,256]{2,1,0:T(8,128)(2,1)}, bf16[512,2048]{1,0:T(8,128)(2,1)}) custom-call(s32[1]{0:T(128)} %bitcast.1.parity_ref, bf16[3,256,512]{2,1,0:T(8,128)(2,1)} %projected_hbm.1, f32[256,512]{1,0:T(8,128)} %filter_hbm.1, bf16[512,4096]{1,0:T(8,128)(2,1)} %w_hbm.3), custom_call_target="tpu_custom_call" | custom-call | tf_op jit(solution)/shard_map/prep/pallas_call | solution.py:237
  3.5 6.5 %collective-permute-start = (bf16[512,2048]{1,0:T(8,128)(2,1)}, bf16[512,2048]{1,0:T(8,128)(2,1)S(1)}, u32[]{:S(2)}, u32[]{:S(2)}) collective-permute-start(bf16[512,2048]{1,0:T(8,128)(2,1)} %get-tuple-element.8), channel_id=1, source_target_pairs={{0,2},{1,15},{2,0},{3,5},{4,6},{5,3},{6,4},{7,9},{8,10},{9,7},{10,... | collective-permute-start | bytes 6291464 | tf_op jit(solution)/shard_map/ppermute | solution.py:257
  10.0 6.8 %all-to-all-start = ((bf16[16,128,256]{2,1,0:T(8,128)(2,1)}), bf16[16,128,256]{2,1,0:T(8,128)(2,1)S(1)}, u32[]{:S(2)}, u32[]{:S(2)}) async-start(bf16[16,128,256]{2,1,0:T(8,128)(2,1)} %get-tuple-element.7), calls=%async_computation | async-start | bytes 2097152 | tf_op jit(solution)/shard_map/all_to_all | solution.py:256
  16.8 0.0 copy-done.3
  16.8 0.0 copy-done.4
  16.8 0.1 fusion
  16.9 0.1 copy.12
  17.0 15.0 %all-to-all-done.recv_ref = bf16[16,128,256]{2,1,0:T(8,128)(2,1)S(1)} async-done(((bf16[16,128,256]{2,1,0:T(8,128)(2,1)}), bf16[16,128,256]{2,1,0:T(8,128)(2,1)S(1)}, u32[]{:S(2)}, u32[]{:S(2)}) %all-to-all-start) | async-done | bytes 1048608 | tf_op jit(solution)/shard_map/all_to_all | solution.py:256
  32.0 0.0 copy-done
  32.0 32.0 %conv.1 = bf16[2,16,32,256]{3,2,1,0:T(8,128)(2,1)} custom-call(bf16[16,128,256]{2,1,0:T(8,128)(2,1)S(1)} %all-to-all-done.recv_ref, f32[32,22]{1,0:T(8,128)S(1)} %bitcast.6, f32[2,16,1,256]{3,2,1,0:T(1,128)S(1)} %copy-done, bf16[6144,512]{1,0:T(8,128)(2,1)} %constant.53.clone.tables_hbm), custom_call_target="tpu_custom_call" | custom-call | tf_op jit(solution)/shard_map/conv/pallas_call | solution.py:262
  64.0 5.6 %all-to-all-start.1 = ((bf16[32,32,256]{2,1,0:T(8,128)(2,1)}), bf16[32,32,256]{2,1,0:T(8,128)(2,1)S(1)}, u32[]{:S(2)}, u32[]{:S(2)}) async-start(bf16[32,32,256]{2,1,0:T(8,128)(2,1)} %bitcast.4), calls=%async_computation.1 | async-start | bytes 1048576 | tf_op jit(solution)/shard_map/all_to_all | solution.py:282
  69.7 0.6 pad_add_fusion.index_ref
  70.3 10.5 %all-to-all-done.1 = bf16[32,32,256]{2,1,0:T(8,128)(2,1)S(1)} async-done(((bf16[32,32,256]{2,1,0:T(8,128)(2,1)}), bf16[32,32,256]{2,1,0:T(8,128)(2,1)S(1)}, u32[]{:S(2)}, u32[]{:S(2)}) %all-to-all-start.1) | async-done | bytes 524320 | tf_op jit(solution)/shard_map/all_to_all | solution.py:282
  80.8 0.0 copy-start.1
  80.9 0.0 collective-permute-done.other_ref
  80.9 0.0 copy-start.2
  80.9 0.8 copy-done.1
  81.6 0.7 copy-done.2
  82.3 5.7 %project.1 = bf16[4,256,512]{2,1,0:T(8,128)(2,1)} custom-call(s32[2]{0:T(128)} %pad_add_fusion.index_ref, bf16[2,16,32,256]{3,2,1,0:T(8,128)(2,1)} %bitcast.7, bf16[512,4096]{1,0:T(8,128)(2,1)} %w_hbm.3, bf16[512,2048]{1,0:T(8,128)(2,1)} %copy-done.2), custom_call_target="tpu_custom_call" | custom-call | tf_op jit(solution)/shard_map/project/pallas_call | solution.py:286
  88.1 30.9 %all_to_all.15 = bf16[4,256,512]{2,1,0:T(8,128)(2,1)S(1)} all-to-all(bf16[4,256,512]{2,1,0:T(8,128)(2,1)} %project.1), channel_id=1, replica_groups={{0,4,8,12},{2,6,10,14},{1,5,9,13},{3,7,11,15},{16,20,24,28},{18,22,26,3..., dimensions={0} | all-to-all | bytes 2097152 | tf_op jit(solution)/shard_map/all_to_all | solution.py:298
  119.0 0.9 reduce_sum.12
  (1 shorter events, 0.0 us)
Async XLA Ops:
  0.0 32.0 %copy-start = (f32[2,16,1,256]{3,2,1,0:T(1,128)S(1)}, f32[2,16,1,256]{3,2,1,0:T(1,128)}, u32[]{:S(2)}) copy-start(f32[2,16,1,256]{3,2,1,0:T(1,128)} %constant.52.clone.tw_ref) | copy-start | bytes 98308
  0.0 16.8 %copy-start.3 = (f32[3,7,512]{2,1,0:T(8,128)S(1)}, f32[3,7,512]{2,1,0:T(8,128)}, u32[]{:S(2)}) copy-start(f32[3,7,512]{2,1,0:T(8,128)} %param.8) | copy-start | bytes 129028
  0.0 16.8 %copy-start.4 = (f32[512]{0:T(512)S(1)}, f32[512]{0:T(512)}, u32[]{:S(2)}) copy-start(f32[512]{0:T(512)} %param.10) | copy-start | bytes 6148
  3.5 77.4 %collective-permute-start = (bf16[512,2048]{1,0:T(8,128)(2,1)}, bf16[512,2048]{1,0:T(8,128)(2,1)S(1)}, u32[]{:S(2)}, u32[]{:S(2)}) collective-permute-start(bf16[512,2048]{1,0:T(8,128)(2,1)} %get-tuple-element.8), channel_id=1, source_target_pairs={{0,2},{1,15},{2,0},{3,5},{4,6},{5,3},{6,4},{7,9},{8,10},{9,7},{10,... | collective-permute-start | bytes 6291464 | tf_op jit(solution)/shard_map/ppermute | solution.py:257
  10.0 22.0 %all-to-all-start = ((bf16[16,128,256]{2,1,0:T(8,128)(2,1)}), bf16[16,128,256]{2,1,0:T(8,128)(2,1)S(1)}, u32[]{:S(2)}, u32[]{:S(2)}) async-start(bf16[16,128,256]{2,1,0:T(8,128)(2,1)} %get-tuple-element.7), calls=%async_computation | async-start | bytes 2097152 | tf_op jit(solution)/shard_map/all_to_all | solution.py:256
  64.0 16.8 %all-to-all-start.1 = ((bf16[32,32,256]{2,1,0:T(8,128)(2,1)}), bf16[32,32,256]{2,1,0:T(8,128)(2,1)S(1)}, u32[]{:S(2)}, u32[]{:S(2)}) async-start(bf16[32,32,256]{2,1,0:T(8,128)(2,1)} %bitcast.4), calls=%async_computation.1 | async-start | bytes 1048576 | tf_op jit(solution)/shard_map/all_to_all | solution.py:282
  80.8 0.8 copy-start.1
  80.9 1.5 %copy-start.2 = (bf16[512,2048]{1,0:T(8,128)(2,1)}, bf16[512,2048]{1,0:T(8,128)(2,1)S(1)}, u32[]{:S(2)}) copy-start(bf16[512,2048]{1,0:T(8,128)(2,1)S(1)} %collective-permute-done.other_ref) | copy-start | bytes 6291460
where the time goes:
time: 120 us
  Pallas kernels  41.2 us (34%)
  blocking collectives  30.9 us (26%)
  waiting for transfers between devices  25.6 us (21%)
  starting transfers between devices  18.9 us (16%)
  local copies, waits for them, and re-layouts  1.6 us (1%)
  other arithmetic  1.58 us (1%)
    pallas_call x1, Pallas kernels, local(): pl.pallas_call(conv_kernel, in_specs=[vmem, vmem, vmem, hbm], out_specs=h...  32 us
    all_to_all x1, blocking collectives, local(): lax.all_to_all(partial, 'tp', 0, 0, tiled=True, axis_index_groups=parity_...  30.9 us
    all_to_all x1, waiting for transfers between devices, local(): recv = lax.all_to_all(send, 'ctx', 0, 0, tiled=True)  15 us
    all_to_all x1, waiting for transfers between devices, local(): lax.all_to_all(mixed.reshape(2 * ctx, group, rows), ('ctx', 'tp', 'dp'),...  10.5 us
    all_to_all x1, starting transfers between devices, local(): recv = lax.all_to_all(send, 'ctx', 0, 0, tiled=True)  6.75 us
    ppermute x1, starting transfers between devices, local(): w_other = lax.ppermute(w_send, ('tp', 'dp'), pair_route)  6.49 us
    pallas_call x1, Pallas kernels, local(): pl.pallas_call(project_kernel, in_specs=[smem, vmem, hbm, vmem], out_spec...  5.73 us
    all_to_all x1, starting transfers between devices, local(): lax.all_to_all(mixed.reshape(2 * ctx, group, rows), ('ctx', 'tp', 'dp'),...  5.65 us
  transfers between devices with their start and end apart: 3, of which 2 were waited for; matrix products, arithmetic and copies ran while one was open for 1% of the time, Pallas kernels for 27%

commit v1 on v0

v1 whole, which is shorter than its diff:
```python
import math

import jax
import jax.numpy as jnp
import numpy as np
from jax import lax
from jax.experimental import pallas as pl
from jax.experimental.pallas import tpu as pltpu
from jax.sharding import PartitionSpec as P

TAPS = 7
LANES = 128
BF16 = jnp.bfloat16
F32 = jnp.float32
MIB = 1024 * 1024


def split_table(table):
    high = table.astype(np.float32).astype(jnp.bfloat16)
    low = (table - high.astype(np.float64)).astype(np.float32).astype(jnp.bfloat16)
    return np.stack([high, low])


def lane_tables(width):
    angle = 2.0 * np.pi * (np.outer(np.arange(width), np.arange(width)) % width) / width
    cos, sin = np.cos(angle), np.sin(angle)
    forward = np.block([[cos, -sin], [sin, cos]])
    return np.concatenate([split_table(table).reshape(-1, 2 * width) for table in (forward, forward.T)])


def twiddles(blocks, width):
    angle = 2.0 * np.pi * np.outer(np.arange(blocks) + 0.5, np.arange(width)) / (2 * blocks * width)
    return np.stack([np.cos(angle), -np.sin(angle)]).astype(np.float32)[:, :, None, :]


def block_angle(s, k, blocks):
    return math.pi * ((s * (2 * k + 1)) % (4 * blocks)) / (2 * blocks)


def split_bf16(values):
    high = values.astype(BF16)
    return high, (values - high.astype(F32)).astype(BF16)


def dot(a, b):
    return jnp.dot(a, b, preferred_element_type=F32)


def prep_kernel(
    parity_ref, projected_hbm, filter_hbm, w_hbm, out_hbm, w_send, inputs, taps_in, turned, held, sems, w_sems
):
    blocks, quad, rows = turned.shape
    group = quad // 4
    width = w_hbm.shape[0]
    chunks = w_send.shape[1] // width
    arrive = [pltpu.make_async_copy(projected_hbm.at[part], inputs.at[part], sems.at[part]) for part in range(3)]
    arrive.append(pltpu.make_async_copy(filter_hbm, taps_in, sems.at[3]))
    for copy in arrive:
        copy.start()
    w_in, w_out = [], []
    for i in range(chunks):
        start = pl.multiple_of((2 * i + 1 - parity_ref[0]) * width, width)
        columns = slice(i * width, (i + 1) * width)
        w_in.append(pltpu.make_async_copy(w_hbm.at[:, pl.ds(start, width)], held.at[:, columns], w_sems.at[i]))
        w_out.append(pltpu.make_async_copy(held.at[:, columns], w_send.at[:, columns], w_sems.at[chunks + i]))
        w_in[i].start()
    leave = []
    for part in range(4):
        arrive[part].wait()
        source = inputs[part] if part < 3 else taps_in[...].astype(BF16)
        lines = slice(part * group, (part + 1) * group)
        turned[:, lines, :] = source.T.reshape(blocks, group, rows)
        leave.append(pltpu.make_async_copy(turned.at[:, lines], out_hbm.at[:, lines], sems.at[4 + part]))
        leave[part].start()
    for i in range(chunks):
        w_in[i].wait()
        w_out[i].start()
    for copy in leave + w_out:
        copy.wait()


def featurize(recv_ref, taps_ref, query, gated):
    blocks, quad, width = recv_ref.shape
    group = quad // 4
    tile = 16
    batch = blocks
    lane = lax.broadcasted_iota(jnp.int32, (tile, LANES), 1)
    for c0 in range(0, group, tile):
        lines = slice(c0, c0 + tile)
        for part in (1, 2, 0):
            t = [
                jnp.broadcast_to(taps_ref[lines, part * TAPS + j : part * TAPS + j + 1], (tile, LANES))
                for j in range(TAPS)
            ]
            last = [jnp.zeros((tile, LANES), F32)] * 4
            first_row = part * group + c0
            for s0 in range(0, blocks, batch):
                places = [(s, lines, slice(l0, l0 + LANES)) for s in range(s0, s0 + batch) for l0 in range(0, width, LANES)]
                now = [recv_ref[s, first_row : first_row + tile, cols].astype(F32) for s, _, cols in places]
                gates = [gated[at] for at in places] if part == 2 else None

                def shifted(values, amount, which):
                    turns = [pltpu.roll(value, amount, 1) for value in values]
                    moved = [jnp.where(lane < amount, b, a) for b, a in zip([last[which]] + turns[:-1], turns)]
                    last[which] = turns[-1]
                    return moved

                one = shifted(now, 1, 0)
                two = shifted([t[2] * x + t[3] * y for x, y in zip(now, one)], 2, 1)
                four = shifted([t[4] * x + t[5] * y for x, y in zip(now, one)], 4, 2)
                six = shifted([t[6] * x for x in now], 6, 3)
                totals = [t[0] * x + t[1] * y + a + b + c for x, y, a, b, c in zip(now, one, two, four, six)]
                if part == 2:
                    totals = [g * total for g, total in zip(gates, totals)]
                for at, total in zip(places, totals):
                    (query if part == 0 else gated)[at] = total


def over_blocks(values, k, blocks):
    even_c = even_s = odd_c = odd_s = None
    for s, value in enumerate(values):
        c, t = math.cos(block_angle(s, k, blocks)), math.sin(block_angle(s, k, blocks))
        if s == 0:
            even_c = value
            continue
        term_c, term_s = value * c, value * t
        if s % 2 == 0:
            even_c = even_c + term_c
            even_s = term_s if even_s is None else even_s + term_s
        else:
            odd_c = term_c if odd_c is None else odd_c + term_c
            odd_s = term_s if odd_s is None else odd_s + term_s
    return (even_c + odd_c, -(even_s + odd_s)), (even_c - odd_c, even_s - odd_s)


def conv_kernel(
    recv_ref, taps_ref, tw_ref, tables_hbm, out_hbm, query, gated, high, low, spec_h, spec_u, mixed, tables, sems, out_sems
):
    blocks, quad, width = recv_ref.shape
    group = quad // 4
    tile = 16
    load = pltpu.make_async_copy(tables_hbm, tables, sems.at[0])
    load.start()
    featurize(recv_ref, taps_ref, query, gated)

    def table(which, term):
        start = (2 * which + term) * 2 * width
        return tables[start : start + 2 * width, :]

    def store_split(rows, cols, value):
        high[rows, cols], low[rows, cols] = split_bf16(value)

    def lanes(which):
        return dot(high[...], table(which, 0)) + dot(low[...], table(which, 0)) + dot(high[...], table(which, 1))

    def to_odd(block):
        for c0 in range(0, group, tile):
            for l0 in range(0, width, LANES):
                values = [block(s, c0, slice(l0, l0 + LANES)) for s in range(blocks)]
                for k in range(blocks // 2):
                    for kk, (re, im) in zip((k, blocks - 1 - k), over_blocks(values, k, blocks)):
                        tr = tw_ref[0, kk, :, l0 : l0 + LANES]
                        ti = tw_ref[1, kk, :, l0 : l0 + LANES]
                        rows = slice(kk * group + c0, kk * group + c0 + tile)
                        store_split(rows, slice(l0, l0 + LANES), re * tr - im * ti)
                        store_split(rows, slice(width + l0, width + l0 + LANES), re * ti + im * tr)

    to_odd(lambda s, c, p: recv_ref[s, 3 * group + c : 3 * group + c + tile, p].astype(F32))
    load.wait()
    spec_h[...] = lanes(0)
    to_odd(lambda s, c, p: gated[s, c : c + tile, p])
    spec_u[...] = lanes(0)

    hr, hi = spec_h[:, :width], spec_h[:, width:]
    ur, ui = spec_u[:, :width], spec_u[:, width:]
    store_split(slice(None), slice(0, width), hr * ur - hi * ui)
    store_split(slice(None), slice(width, 2 * width), hr * ui + hi * ur)
    spec_h[...] = lanes(1)

    scale = 1.0 / (blocks * width)
    half = blocks // 2
    for c0 in range(0, group, tile):
        skip = taps_ref[c0 : c0 + tile, 3 * TAPS : 3 * TAPS + 1]
        for l0 in range(0, width, LANES):
            reals, imags = [], []
            for k in range(blocks):
                rows = slice(k * group + c0, k * group + c0 + tile)
                tr = tw_ref[0, k, :, l0 : l0 + LANES] * scale
                ti = tw_ref[1, k, :, l0 : l0 + LANES] * scale
                re = spec_h[rows, l0 : l0 + LANES]
                im = spec_h[rows, width + l0 : width + l0 + LANES]
                reals.append(re * tr + im * ti)
                imags.append(im * tr - re * ti)
            sum_re = [reals[k] + reals[blocks - 1 - k] for k in range(half)]
            dif_re = [reals[k] - reals[blocks - 1 - k] for k in range(half)]
            sum_im = [imags[k] + imags[blocks - 1 - k] for k in range(half)]
            dif_im = [imags[k] - imags[blocks - 1 - k] for k in range(half)]
            for s in range(blocks):
                res, ims = (sum_re, dif_im) if s % 2 == 0 else (dif_re, sum_im)
                total = None
                for k in range(half):
                    angle = block_angle(s, k, blocks)
                    term = res[k] if s == 0 else res[k] * math.cos(angle) - ims[k] * math.sin(angle)
                    total = term if total is None else total + term
                at = (s, slice(c0, c0 + tile), slice(l0, l0 + LANES))
                mixed[at] = (query[at] * (total + skip * gated[at])).astype(BF16)
    copies = [pltpu.make_async_copy(mixed, out_hbm.at[twin], out_sems.at[twin]) for twin in range(2)]
    for copy in copies:
        copy.start()
    for copy in copies:
        copy.wait()


def project_kernel(index_ref, mixed_ref, w_hbm, other_ref, out_ref, own, sems):
    chunks, rows, width = out_ref.shape
    copies = []
    for i in range(chunks):
        start = pl.multiple_of((2 * i + index_ref[1]) * width, width)
        copies.append(
            pltpu.make_async_copy(w_hbm.at[:, pl.ds(start, width)], own.at[:, i * width : (i + 1) * width], sems.at[i])
        )
        copies[i].start()
    mine = index_ref[0]
    first = mixed_ref[mine].reshape(width, rows).T
    second = mixed_ref[1 - mine].reshape(width, rows).T
    for i in range(chunks):
        columns = slice(i * width, (i + 1) * width)
        total = dot(second, other_ref[:, columns])
        copies[i].wait()
        out_ref[i] = (total + dot(first, own[:, columns])).astype(BF16)


def local(projected, short_taps, long_filter, skip_gain, w_out):
    ctx, tp, dp = lax.axis_size("ctx"), lax.axis_size("tp"), lax.axis_size("dp")
    rows, width = projected.shape[1:]
    group = width // ctx
    me_ctx, me_tp, me_dp = lax.axis_index("ctx"), lax.axis_index("tp"), lax.axis_index("dp")

    def partner(z, d):
        first = d + (z - d) % tp // 2 * 2
        return (first + (1 - (z - d) % tp % 2)) % tp

    pair_route = [(z * dp + d, partner(z, d) * dp + d) for z in range(tp) for d in range(dp)]
    pair_groups = [
        [(c * tp + (first + d + b) % tp) * dp + d for b in range(2) for c in range(ctx)]
        for d in range(dp)
        for first in range(0, tp, 2)
    ]
    parity_groups = [list(range(odd, tp, 2)) for odd in range(2)]
    chunks = tp // 2
    parity = (me_tp % 2).astype(jnp.int32)
    place = ((me_tp - me_dp) % tp % 2).astype(jnp.int32)

    vmem = pl.BlockSpec(memory_space=pltpu.VMEM)
    smem = pl.BlockSpec(memory_space=pltpu.SMEM)
    hbm = pl.BlockSpec(memory_space=pl.ANY)
    params = pltpu.CompilerParams(vmem_limit_bytes=60 * MIB)

    send, w_send = pl.pallas_call(
        prep_kernel,
        in_specs=[smem, hbm, hbm, hbm],
        out_specs=[hbm, hbm],
        out_shape=[
            jax.ShapeDtypeStruct((ctx, 4 * group, rows), BF16),
            jax.ShapeDtypeStruct((width, chunks * width), BF16),
        ],
        scratch_shapes=[
            pltpu.VMEM((3, rows, width), BF16),
            pltpu.VMEM((rows, width), F32),
            pltpu.VMEM((ctx, 4 * group, rows), BF16),
            pltpu.VMEM((width, chunks * width), BF16),
            pltpu.SemaphoreType.DMA((8,)),
            pltpu.SemaphoreType.DMA((2 * chunks,)),
        ],
        compiler_params=params,
        name="prep",
    )(parity[None], projected, long_filter, w_out)
    recv = lax.all_to_all(send, "ctx", 0, 0, tiled=True)
    w_other = lax.ppermute(w_send, ("tp", "dp"), pair_route)

    taps = jnp.concatenate([short_taps.reshape(3 * TAPS, width), skip_gain[None, :]], axis=0)
    taps = lax.dynamic_slice_in_dim(taps, me_ctx * group, group, axis=1).T
    tables = lane_tables(rows)
    mixed = pl.pallas_call(
        conv_kernel,
        in_specs=[vmem, vmem, vmem, hbm],
        out_specs=hbm,
        out_shape=jax.ShapeDtypeStruct((2, ctx, group, rows), BF16),
        scratch_shapes=[
            pltpu.VMEM((ctx, group, rows), F32),
            pltpu.VMEM((ctx, group, rows), F32),
            pltpu.VMEM((ctx * group, 2 * rows), BF16),
            pltpu.VMEM((ctx * group, 2 * rows), BF16),
            pltpu.VMEM((ctx * group, 2 * rows), F32),
            pltpu.VMEM((ctx * group, 2 * rows), F32),
            pltpu.VMEM((ctx, group, rows), BF16),
            pltpu.VMEM(tables.shape, BF16),
            pltpu.SemaphoreType.DMA((1,)),
            pltpu.SemaphoreType.DMA((2,)),
        ],
        compiler_params=pltpu.CompilerParams(vmem_limit_bytes=52 * MIB),
        name="conv",
    )(recv, taps, jnp.asarray(twiddles(ctx, rows)), jnp.asarray(tables))
    mixed = lax.all_to_all(
        mixed.reshape(2 * ctx, group, rows), ("ctx", "tp", "dp"), 0, 0, tiled=True, axis_index_groups=pair_groups
    ).reshape(2, ctx, group, rows)

    partial = pl.pallas_call(
        project_kernel,
        in_specs=[smem, vmem, hbm, vmem],
        out_specs=vmem,
        out_shape=jax.ShapeDtypeStruct((chunks, rows, width), BF16),
        scratch_shapes=[
            pltpu.VMEM((width, chunks * width), BF16),
            pltpu.SemaphoreType.DMA((chunks,)),
        ],
        compiler_params=pltpu.CompilerParams(vmem_limit_bytes=48 * MIB),
        name="project",
    )(jnp.stack([place, parity]), mixed, w_out, w_other)
    gathered = lax.all_to_all(partial, "tp", 0, 0, tiled=True, axis_index_groups=parity_groups)
    return jnp.sum(gathered.astype(F32), axis=0).astype(BF16)


def solution(mesh):
    in_specs = (
        P(None, ("dp", "ctx"), "tp"),
        P(None, None, "tp"),
        P("ctx", "tp"),
        P("tp"),
        P("tp", None),
    )
    out_specs = P(("dp", "ctx"), "tp")
    return jax.shard_map(local, mesh=mesh, in_specs=in_specs, out_specs=out_specs, check_vma=False)
```

time: 120 us -> 92.7 us (0.77)
  Pallas kernels: 41.2 us -> 15.4 us
  local copies, waits for them, and re-layouts: 1.6 us -> 0.11 us
    pallas_call x1, Pallas kernels: 32 us -> 8.39 us  [local(): pl.pallas_call(conv_kernel, in_specs=[vmem, vmem, vmem, hbm], out_specs=h...]
    pallas_call x1, Pallas kernels: 5.73 us -> 3.52 us  [local(): pl.pallas_call(project_kernel, in_specs=[smem, vmem, hbm, vmem], out_spec...]
    unnamed x11 -> x7, local copies, waits for them, and re-layouts: 1.59 us -> 0.11 us
  transfers between devices with their start and end apart: 3 -> 3, of which waited for: 2 -> 2; matrix products, arithmetic and copies ran while one was open for 1% -> 0% of each run, Pallas kernels for 27% -> 9%
where the time goes in v1:
time: 92.7 us; the launch traced here: 92.3 us
  blocking collectives  30.7 us (33%)
  waiting for transfers between devices  26.1 us (28%)
  starting transfers between devices  18.9 us (20%)
  Pallas kernels  15.4 us (17%)
  other arithmetic  1.06 us (1%)
    all_to_all x1, blocking collectives, local(): lax.all_to_all(partial, 'tp', 0, 0, tiled=True, axis_index_groups=parity_...  30.7 us
    all_to_all x1, waiting for transfers between devices, local(): recv = lax.all_to_all(send, 'ctx', 0, 0, tiled=True)  15 us
    all_to_all x1, waiting for transfers between devices, local(): lax.all_to_all(mixed.reshape(2 * ctx, group, rows), ('ctx', 'tp', 'dp'),...  11.1 us
    pallas_call x1, Pallas kernels, local(): pl.pallas_call(conv_kernel, in_specs=[vmem, vmem, vmem, hbm], out_specs=h...  8.39 us
    all_to_all x1, starting transfers between devices, local(): recv = lax.all_to_all(send, 'ctx', 0, 0, tiled=True)  6.75 us
    ppermute x1, starting transfers between devices, local(): w_other = lax.ppermute(w_send, ('tp', 'dp'), pair_route)  6.5 us
    all_to_all x1, starting transfers between devices, local(): lax.all_to_all(mixed.reshape(2 * ctx, group, rows), ('ctx', 'tp', 'dp'),...  5.65 us
    pallas_call x1, Pallas kernels, local(): pl.pallas_call(project_kernel, in_specs=[smem, vmem, hbm, vmem], out_spec...  3.52 us
  transfers between devices with their start and end apart: 3, of which 2 were waited for; matrix products, arithmetic and copies ran while one was open for 0% of the time, Pallas kernels for 9%

profile of v1, /device:TPU:1, one launch (start us, length us, event | category | flops | bytes accessed | tf_op | source)
XLA Modules:
  0.0 92.3 jit_solution(10613860542753598101)
XLA Ops:
  0.0 3.5 %prep.1 = (bf16[16,128,256]{2,1,0:T(8,128)(2,1)}, bf16[512,2048]{1,0:T(8,128)(2,1)}) custom-call(s32[1]{0:T(128)} %bitcast.1.parity_ref, bf16[3,256,512]{2,1,0:T(8,128)(2,1)} %projected_hbm.1, f32[256,512]{1,0:T(8,128)} %filter_hbm.1, bf16[512,4096]{1,0:T(8,128)(2,1)} %w_hbm.3), custom_call_target="tpu_custom_call" | custom-call | tf_op jit(solution)/shard_map/prep/pallas_call | solution.py:259
  3.5 0.0 copy-start.1
  3.5 0.0 copy-start.2
  3.5 0.0 copy-start
  3.5 6.5 %collective-permute-start = (bf16[512,2048]{1,0:T(8,128)(2,1)}, bf16[512,2048]{1,0:T(8,128)(2,1)S(1)}, u32[]{:S(2)}, u32[]{:S(2)}) collective-permute-start(bf16[512,2048]{1,0:T(8,128)(2,1)} %get-tuple-element.8), channel_id=1, source_target_pairs={{0,2},{1,15},{2,0},{3,5},{4,6},{5,3},{6,4},{7,9},{8,10},{9,7},{10,... | collective-permute-start | bytes 6291464 | tf_op jit(solution)/shard_map/ppermute | solution.py:279
  10.0 6.8 %all-to-all-start = ((bf16[16,128,256]{2,1,0:T(8,128)(2,1)}), bf16[16,128,256]{2,1,0:T(8,128)(2,1)S(1)}, u32[]{:S(2)}, u32[]{:S(2)}) async-start(bf16[16,128,256]{2,1,0:T(8,128)(2,1)} %get-tuple-element.7), calls=%async_computation | async-start | bytes 2097152 | tf_op jit(solution)/shard_map/all_to_all | solution.py:278
  16.8 0.0 copy-done.1
  16.8 0.0 copy-done.2
  16.8 0.1 fusion
  16.9 0.1 copy.12
  17.0 15.0 %all-to-all-done.recv_ref = bf16[16,128,256]{2,1,0:T(8,128)(2,1)S(1)} async-done(((bf16[16,128,256]{2,1,0:T(8,128)(2,1)}), bf16[16,128,256]{2,1,0:T(8,128)(2,1)S(1)}, u32[]{:S(2)}, u32[]{:S(2)}) %all-to-all-start) | async-done | bytes 1048608 | tf_op jit(solution)/shard_map/all_to_all | solution.py:278
  32.0 0.0 copy-done
  32.0 8.4 %conv.1 = bf16[2,16,32,256]{3,2,1,0:T(8,128)(2,1)} custom-call(bf16[16,128,256]{2,1,0:T(8,128)(2,1)S(1)} %all-to-all-done.recv_ref, f32[32,22]{1,0:T(8,128)S(1)} %bitcast.7, f32[2,16,1,256]{3,2,1,0:T(1,128)S(1)} %copy-done, bf16[2048,512]{1,0:T(8,128)(2,1)} %constant.53.clone.tables_hbm), custom_call_target="tpu_custom_call" | custom-call | tf_op jit(solution)/shard_map/conv/pallas_call | solution.py:284
  40.4 5.7 %all-to-all-start.1 = ((bf16[32,32,256]{2,1,0:T(8,128)(2,1)}), bf16[32,32,256]{2,1,0:T(8,128)(2,1)S(1)}, u32[]{:S(2)}, u32[]{:S(2)}) async-start(bf16[32,32,256]{2,1,0:T(8,128)(2,1)} %bitcast.4), calls=%async_computation.1 | async-start | bytes 1048576 | tf_op jit(solution)/shard_map/all_to_all | solution.py:304
  46.1 0.1 pad_add_fusion.index_ref
  46.2 11.1 %all-to-all-done.1 = bf16[32,32,256]{2,1,0:T(8,128)(2,1)S(1)} async-done(((bf16[32,32,256]{2,1,0:T(8,128)(2,1)}), bf16[32,32,256]{2,1,0:T(8,128)(2,1)S(1)}, u32[]{:S(2)}, u32[]{:S(2)}) %all-to-all-start.1) | async-done | bytes 524320 | tf_op jit(solution)/shard_map/all_to_all | solution.py:304
  57.2 0.0 collective-permute-done.other_ref
  57.2 3.5 %project.1 = bf16[4,256,512]{2,1,0:T(8,128)(2,1)S(1)} custom-call(s32[2]{0:T(128)S(1)} %pad_add_fusion.index_ref, bf16[2,16,32,256]{3,2,1,0:T(8,128)(2,1)S(1)} %bitcast.6, bf16[512,4096]{1,0:T(8,128)(2,1)} %w_hbm.3, bf16[512,2048]{1,0:T(8,128)(2,1)S(1)} %collective-permute-done.other_ref), custom_call_target="tpu_custom_call" | custom-call | tf_op jit(solution)/shard_map/project/pallas_call | solution.py:308
  60.8 30.7 %all_to_all.15 = bf16[4,256,512]{2,1,0:T(8,128)(2,1)S(1)} all-to-all(bf16[4,256,512]{2,1,0:T(8,128)(2,1)S(1)} %project.1), channel_id=1, replica_groups={{0,4,8,12},{2,6,10,14},{1,5,9,13},{3,7,11,15},{16,20,24,28},{18,22,26,3..., dimensions={0} | all-to-all | bytes 2097152 | tf_op jit(solution)/shard_map/all_to_all | solution.py:320
  91.4 0.9 reduce_sum.12
  (1 shorter events, 0.0 us)
Async XLA Ops:
  3.5 13.3 %copy-start.1 = (f32[3,7,512]{2,1,0:T(8,128)S(1)}, f32[3,7,512]{2,1,0:T(8,128)}, u32[]{:S(2)}) copy-start(f32[3,7,512]{2,1,0:T(8,128)} %param.8) | copy-start | bytes 129028
  3.5 13.3 %copy-start.2 = (f32[512]{0:T(512)S(1)}, f32[512]{0:T(512)}, u32[]{:S(2)}) copy-start(f32[512]{0:T(512)} %param.10) | copy-start | bytes 6148
  3.5 28.5 %copy-start = (f32[2,16,1,256]{3,2,1,0:T(1,128)S(1)}, f32[2,16,1,256]{3,2,1,0:T(1,128)}, u32[]{:S(2)}) copy-start(f32[2,16,1,256]{3,2,1,0:T(1,128)} %constant.52.clone.tw_ref) | copy-start | bytes 98308
  3.5 53.7 %collective-permute-start = (bf16[512,2048]{1,0:T(8,128)(2,1)}, bf16[512,2048]{1,0:T(8,128)(2,1)S(1)}, u32[]{:S(2)}, u32[]{:S(2)}) collective-permute-start(bf16[512,2048]{1,0:T(8,128)(2,1)} %get-tuple-element.8), channel_id=1, source_target_pairs={{0,2},{1,15},{2,0},{3,5},{4,6},{5,3},{6,4},{7,9},{8,10},{9,7},{10,... | collective-permute-start | bytes 6291464 | tf_op jit(solution)/shard_map/ppermute | solution.py:279
  10.0 22.0 %all-to-all-start = ((bf16[16,128,256]{2,1,0:T(8,128)(2,1)}), bf16[16,128,256]{2,1,0:T(8,128)(2,1)S(1)}, u32[]{:S(2)}, u32[]{:S(2)}) async-start(bf16[16,128,256]{2,1,0:T(8,128)(2,1)} %get-tuple-element.7), calls=%async_computation | async-start | bytes 2097152 | tf_op jit(solution)/shard_map/all_to_all | solution.py:278
  40.4 16.8 %all-to-all-start.1 = ((bf16[32,32,256]{2,1,0:T(8,128)(2,1)}), bf16[32,32,256]{2,1,0:T(8,128)(2,1)S(1)}, u32[]{:S(2)}, u32[]{:S(2)}) async-start(bf16[32,32,256]{2,1,0:T(8,128)(2,1)} %bitcast.4), calls=%async_computation.1 | async-start | bytes 1048576 | tf_op jit(solution)/shard_map/all_to_all | solution.py:304

commit v2 on v1

--- a/solution.py
+++ b/solution.py
@@ -46,8 +46,13 @@
     return jnp.dot(a, b, preferred_element_type=F32)
 
 
+def column_start(first, i, w_hbm):
+    width = w_hbm.shape[0]
+    return pl.multiple_of(lax.rem(first + i, w_hbm.shape[1] // width) * width, width)
+
+
 def prep_kernel(
-    parity_ref, projected_hbm, filter_hbm, w_hbm, out_hbm, w_send, inputs, taps_in, turned, held, sems, w_sems
+    index_ref, projected_hbm, filter_hbm, w_hbm, out_hbm, w_send, inputs, taps_in, turned, held, sems, w_sems
 ):
     blocks, quad, rows = turned.shape
     group = quad // 4
@@ -59,7 +64,7 @@
         copy.start()
     w_in, w_out = [], []
     for i in range(chunks):
-        start = pl.multiple_of((2 * i + 1 - parity_ref[0]) * width, width)
+        start = column_start(index_ref[2], i, w_hbm)
         columns = slice(i * width, (i + 1) * width)
         w_in.append(pltpu.make_async_copy(w_hbm.at[:, pl.ds(start, width)], held.at[:, columns], w_sems.at[i]))
         w_out.append(pltpu.make_async_copy(held.at[:, columns], w_send.at[:, columns], w_sems.at[chunks + i]))
@@ -215,7 +220,7 @@
     chunks, rows, width = out_ref.shape
     copies = []
     for i in range(chunks):
-        start = pl.multiple_of((2 * i + index_ref[1]) * width, width)
+        start = column_start(index_ref[1], i, w_hbm)
         copies.append(
             pltpu.make_async_copy(w_hbm.at[:, pl.ds(start, width)], own.at[:, i * width : (i + 1) * width], sems.at[i])
         )
@@ -236,20 +241,23 @@
     group = width // ctx
     me_ctx, me_tp, me_dp = lax.axis_index("ctx"), lax.axis_index("tp"), lax.axis_index("dp")
 
-    def partner(z, d):
-        first = d + (z - d) % tp // 2 * 2
-        return (first + (1 - (z - d) % tp % 2)) % tp
-
-    pair_route = [(z * dp + d, partner(z, d) * dp + d) for z in range(tp) for d in range(dp)]
+    half = tp // 2
+
+    def plane(r, d):
+        return (r + 2 * d) % tp
+
+    pair_route = [(plane(r, d) * dp + d, plane(tp - 1 - r, d) * dp + d) for r in range(tp) for d in range(dp)]
     pair_groups = [
-        [(c * tp + (first + d + b) % tp) * dp + d for b in range(2) for c in range(ctx)]
+        [(c * tp + plane(r, d)) * dp + d for r in (first, tp - 1 - first) for c in range(ctx)]
         for d in range(dp)
-        for first in range(0, tp, 2)
+        for first in range(half)
     ]
-    parity_groups = [list(range(odd, tp, 2)) for odd in range(2)]
-    chunks = tp // 2
-    parity = (me_tp % 2).astype(jnp.int32)
-    place = ((me_tp - me_dp) % tp % 2).astype(jnp.int32)
+    quad_groups = [[plane(q * half + i, d) * dp + d for i in range(half)] for d in range(dp) for q in range(2)]
+    chunks = half
+    place = lax.rem(me_tp - 2 * me_dp + 2 * tp, tp) // half
+    own_first = lax.rem(place * half + 2 * me_dp, tp)
+    other_first = lax.rem((1 - place) * half + 2 * me_dp, tp)
+    index = jnp.stack([place, own_first, other_first]).astype(jnp.int32)
 
     vmem = pl.BlockSpec(memory_space=pltpu.VMEM)
     smem = pl.BlockSpec(memory_space=pltpu.SMEM)
@@ -274,7 +282,7 @@
         ],
         compiler_params=params,
         name="prep",
-    )(parity[None], projected, long_filter, w_out)
+    )(index, projected, long_filter, w_out)
     recv = lax.all_to_all(send, "ctx", 0, 0, tiled=True)
     w_other = lax.ppermute(w_send, ("tp", "dp"), pair_route)
 
@@ -316,8 +324,8 @@
         ],
         compiler_params=pltpu.CompilerParams(vmem_limit_bytes=48 * MIB),
         name="project",
-    )(jnp.stack([place, parity]), mixed, w_out, w_other)
-    gathered = lax.all_to_all(partial, "tp", 0, 0, tiled=True, axis_index_groups=parity_groups)
+    )(index, mixed, w_out, w_other)
+    gathered = lax.all_to_all(partial, ("tp", "dp"), 0, 0, tiled=True, axis_index_groups=quad_groups)
     return jnp.sum(gathered.astype(F32), axis=0).astype(BF16)
 
 

time: 92.7 us -> 96.8 us (1.044)
  blocking collectives: 30.7 us -> 52.9 us
  waiting for transfers between devices: 26.1 us -> 14.5 us
  starting transfers between devices: 18.9 us -> 12 us
    all_to_all x1 -> x2, blocking collectives: 30.7 us -> 52.9 us  [the longest x1 28.6 us: local(): lax.all_to_all(mixed.reshape(2 * ctx, group, rows), ('ctx', 'tp', 'dp'),...]
    all_to_all x1 -> x0, waiting for transfers between devices: 11.1 us -> none  [local(): lax.all_to_all(mixed.reshape(2 * ctx, group, rows), ('ctx', 'tp', 'dp'),...]
    all_to_all x1 -> x0, starting transfers between devices: 5.65 us -> none  [local(): lax.all_to_all(mixed.reshape(2 * ctx, group, rows), ('ctx', 'tp', 'dp'),...]
    ppermute x1, starting transfers between devices: 6.5 us -> 5.26 us  [local(): w_other = lax.ppermute(w_send, ('tp', 'dp'), pair_route)]
  transfers between devices with their start and end apart: 3 -> 2, of which waited for: 2 -> 1; matrix products, arithmetic and copies ran while one was open for 0% -> 0% of each run, Pallas kernels for 9% -> 8%
where the time goes in v2:
time: 96.8 us; the launch traced here: 96.5 us
  blocking collectives  52.9 us (55%)
  Pallas kernels  15.3 us (16%)
  waiting for transfers between devices  14.5 us (15%)
  starting transfers between devices  12 us (12%)
  other arithmetic  1.64 us (2%)
    all_to_all x1, blocking collectives, local(): lax.all_to_all(mixed.reshape(2 * ctx, group, rows), ('ctx', 'tp', 'dp'),...  28.6 us
    all_to_all x1, blocking collectives, local(): lax.all_to_all(partial, ('tp', 'dp'), 0, 0, tiled=True, axis_index_groups...  24.3 us
    all_to_all x1, waiting for transfers between devices, local(): recv = lax.all_to_all(send, 'ctx', 0, 0, tiled=True)  14.4 us
    pallas_call x1, Pallas kernels, local(): pl.pallas_call(conv_kernel, in_specs=[vmem, vmem, vmem, hbm], out_specs=h...  7.63 us
    all_to_all x1, starting transfers between devices, local(): recv = lax.all_to_all(send, 'ctx', 0, 0, tiled=True)  6.75 us
    ppermute x1, starting transfers between devices, local(): w_other = lax.ppermute(w_send, ('tp', 'dp'), pair_route)  5.26 us
    pallas_call x1, Pallas kernels, local(): pl.pallas_call(prep_kernel, in_specs=[smem, hbm, hbm, hbm], out_specs=[hb...  4.12 us
    pallas_call x1, Pallas kernels, local(): pl.pallas_call(project_kernel, in_specs=[smem, vmem, hbm, vmem], out_spec...  3.52 us
  transfers between devices with their start and end apart: 2, of which 1 were waited for; matrix products, arithmetic and copies ran while one was open for 0% of the time, Pallas kernels for 8%

profile of v2, /device:TPU:1, one launch (start us, length us, event | category | flops | bytes accessed | tf_op | source)
XLA Modules:
  0.0 96.5 jit_solution(9670299092867609577)
XLA Ops:
  0.0 0.7 pad_add_fusion.index_ref
  0.7 4.1 %prep.1 = (bf16[16,128,256]{2,1,0:T(8,128)(2,1)}, bf16[512,2048]{1,0:T(8,128)(2,1)}) custom-call(s32[3]{0:T(128)} %pad_add_fusion.index_ref, bf16[3,256,512]{2,1,0:T(8,128)(2,1)} %projected_hbm.1, f32[256,512]{1,0:T(8,128)} %filter_hbm.1, bf16[512,4096]{1,0:T(8,128)(2,1)} %w_hbm.3), custom_call_target="tpu_custom_call" | custom-call | tf_op jit(solution)/shard_map/prep/pallas_call | solution.py:267
  4.8 0.0 copy-start.2
  4.8 0.0 copy-start.3
  4.8 0.0 copy-start
  4.8 5.3 %collective-permute-start = (bf16[512,2048]{1,0:T(8,128)(2,1)}, bf16[512,2048]{1,0:T(8,128)(2,1)S(1)}, u32[]{:S(2)}, u32[]{:S(2)}) collective-permute-start(bf16[512,2048]{1,0:T(8,128)(2,1)} %get-tuple-element.8), channel_id=1, source_target_pairs={{0,14},{5,3},{2,12},{7,1},{4,10},{9,15},{6,8},{11,13},{8,6},{13,11... | collective-permute-start | bytes 6291464 | tf_op jit(solution)/shard_map/ppermute | solution.py:287
  10.1 6.8 %all-to-all-start = ((bf16[16,128,256]{2,1,0:T(8,128)(2,1)}), bf16[16,128,256]{2,1,0:T(8,128)(2,1)S(1)}, u32[]{:S(2)}, u32[]{:S(2)}) async-start(bf16[16,128,256]{2,1,0:T(8,128)(2,1)} %get-tuple-element.7), calls=%async_computation | async-start | bytes 2097152 | tf_op jit(solution)/shard_map/all_to_all | solution.py:286
  16.8 0.0 copy-done.2
  16.9 0.0 copy-done.3
  16.9 0.1 fusion
  17.0 0.1 copy.12
  17.1 14.4 %all-to-all-done.recv_ref = bf16[16,128,256]{2,1,0:T(8,128)(2,1)S(1)} async-done(((bf16[16,128,256]{2,1,0:T(8,128)(2,1)}), bf16[16,128,256]{2,1,0:T(8,128)(2,1)S(1)}, u32[]{:S(2)}, u32[]{:S(2)}) %all-to-all-start) | async-done | bytes 1048608 | tf_op jit(solution)/shard_map/all_to_all | solution.py:286
  31.5 0.0 copy-done
  31.5 0.0 copy-start.1
  31.5 7.6 %conv.1 = bf16[2,16,32,256]{3,2,1,0:T(8,128)(2,1)S(1)} custom-call(bf16[16,128,256]{2,1,0:T(8,128)(2,1)S(1)} %all-to-all-done.recv_ref, f32[32,22]{1,0:T(8,128)S(1)} %bitcast.9, f32[2,16,1,256]{3,2,1,0:T(1,128)S(1)} %copy-done, bf16[2048,512]{1,0:T(8,128)(2,1)} %constant.55.clone.tables_hbm), custom_call_target="tpu_custom_call" | custom-call | tf_op jit(solution)/shard_map/conv/pallas_call | solution.py:292
  39.1 28.6 %all_to_all.15 = bf16[32,32,256]{2,1,0:T(8,128)(2,1)S(1)} all-to-all(bf16[32,32,256]{2,1,0:T(8,128)(2,1)S(1)} %bitcast.8), channel_id=1, replica_groups={{0,16,32,48,64,80,96,112,128,144,160,176,192,208,224,240,14,30,46,62,78..., dimensions={0} | all-to-all | bytes 1048576 | tf_op jit(solution)/shard_map/all_to_all | solution.py:312
  67.7 0.0 collective-permute-done.other_ref
  67.7 0.0 copy-done.1
  67.7 3.5 %project.1 = bf16[4,256,512]{2,1,0:T(8,128)(2,1)S(1)} custom-call(s32[3]{0:T(128)S(1)} %copy-done.1, bf16[2,16,32,256]{3,2,1,0:T(8,128)(2,1)S(1)} %bitcast.7, bf16[512,4096]{1,0:T(8,128)(2,1)} %w_hbm.3, bf16[512,2048]{1,0:T(8,128)(2,1)S(1)} %collective-permute-done.other_ref), custom_call_target="tpu_custom_call" | custom-call | tf_op jit(solution)/shard_map/project/pallas_call | solution.py:316
  71.2 24.3 %all_to_all.16 = bf16[4,256,512]{2,1,0:T(8,128)(2,1)S(1)} all-to-all(bf16[4,256,512]{2,1,0:T(8,128)(2,1)S(1)} %project.1), channel_id=1, replica_groups={{0,2,4,6},{8,10,12,14},{5,7,9,11},{13,15,1,3},{16,18,20,22},{24,26,28,3..., dimensions={0} | all-to-all | bytes 2097152 | tf_op jit(solution)/shard_map/all_to_all | solution.py:328
  95.6 0.9 reduce_sum.12
  (1 shorter events, 0.0 us)
Async XLA Ops:
  4.8 12.1 %copy-start.2 = (f32[3,7,512]{2,1,0:T(8,128)S(1)}, f32[3,7,512]{2,1,0:T(8,128)}, u32[]{:S(2)}) copy-start(f32[3,7,512]{2,1,0:T(8,128)} %param.8) | copy-start | bytes 129028
  4.8 12.1 %copy-start.3 = (f32[512]{0:T(512)S(1)}, f32[512]{0:T(512)}, u32[]{:S(2)}) copy-start(f32[512]{0:T(512)} %param.10) | copy-start | bytes 6148
  4.8 26.7 %copy-start = (f32[2,16,1,256]{3,2,1,0:T(1,128)S(1)}, f32[2,16,1,256]{3,2,1,0:T(1,128)}, u32[]{:S(2)}) copy-start(f32[2,16,1,256]{3,2,1,0:T(1,128)} %constant.54.clone.tw_ref) | copy-start | bytes 98308
  4.8 62.9 %collective-permute-start = (bf16[512,2048]{1,0:T(8,128)(2,1)}, bf16[512,2048]{1,0:T(8,128)(2,1)S(1)}, u32[]{:S(2)}, u32[]{:S(2)}) collective-permute-start(bf16[512,2048]{1,0:T(8,128)(2,1)} %get-tuple-element.8), channel_id=1, source_target_pairs={{0,14},{5,3},{2,12},{7,1},{4,10},{9,15},{6,8},{11,13},{8,6},{13,11... | collective-permute-start | bytes 6291464 | tf_op jit(solution)/shard_map/ppermute | solution.py:287
  10.1 21.4 %all-to-all-start = ((bf16[16,128,256]{2,1,0:T(8,128)(2,1)}), bf16[16,128,256]{2,1,0:T(8,128)(2,1)S(1)}, u32[]{:S(2)}, u32[]{:S(2)}) async-start(bf16[16,128,256]{2,1,0:T(8,128)(2,1)} %get-tuple-element.7), calls=%async_computation | async-start | bytes 2097152 | tf_op jit(solution)/shard_map/all_to_all | solution.py:286
  31.5 36.2 %copy-start.1 = (s32[3]{0:T(128)S(1)}, s32[3]{0:T(128)}, u32[]{:S(2)}) copy-start(s32[3]{0:T(128)} %pad_add_fusion.index_ref) | copy-start | bytes 40

commit v3 on v1

--- a/solution.py
+++ b/solution.py
@@ -1,3 +1,4 @@
+import functools
 import math
 
 import jax
@@ -46,8 +47,18 @@
     return jnp.dot(a, b, preferred_element_type=F32)
 
 
+def column_start(place_ref, i, w_hbm, other=False):
+    width = w_hbm.shape[0]
+    chunks = w_hbm.shape[1] // width
+    core, ring = lax.rem(place_ref[0], 2), place_ref[0] // 2
+    mine = ring // 2
+    side = (lax.rem(ring, 2) + (2 * mine >= chunks // 2).astype(jnp.int32) + int(other)) % 2
+    upper = (2 * jnp.asarray(i, jnp.int32) >= chunks // 2).astype(jnp.int32)
+    return pl.multiple_of(lax.rem(2 * i + lax.rem(side + upper, 2) + core, chunks) * width, width)
+
+
 def prep_kernel(
-    parity_ref, projected_hbm, filter_hbm, w_hbm, out_hbm, w_send, inputs, taps_in, turned, held, sems, w_sems
+    place_ref, projected_hbm, filter_hbm, w_hbm, out_hbm, w_send, inputs, taps_in, turned, held, sems, w_sems
 ):
     blocks, quad, rows = turned.shape
     group = quad // 4
@@ -59,7 +70,7 @@
         copy.start()
     w_in, w_out = [], []
     for i in range(chunks):
-        start = pl.multiple_of((2 * i + 1 - parity_ref[0]) * width, width)
+        start = column_start(place_ref, i, w_hbm, other=True)
         columns = slice(i * width, (i + 1) * width)
         w_in.append(pltpu.make_async_copy(w_hbm.at[:, pl.ds(start, width)], held.at[:, columns], w_sems.at[i]))
         w_out.append(pltpu.make_async_copy(held.at[:, columns], w_send.at[:, columns], w_sems.at[chunks + i]))
@@ -211,23 +222,35 @@
         copy.wait()
 
 
-def project_kernel(index_ref, mixed_ref, w_hbm, other_ref, out_ref, own, sems):
-    chunks, rows, width = out_ref.shape
+def project_kernel(steps, first, place_ref, mixed_ref, w_hbm, other_ref, *refs):
+    outs, (own, sems) = refs[:-2], refs[-2:]
+    width = w_hbm.shape[0]
+    index = place_ref[0] // 4
     copies = []
-    for i in range(chunks):
-        start = pl.multiple_of((2 * i + index_ref[1]) * width, width)
-        copies.append(
-            pltpu.make_async_copy(w_hbm.at[:, pl.ds(start, width)], own.at[:, i * width : (i + 1) * width], sems.at[i])
-        )
-        copies[i].start()
-    mine = index_ref[0]
-    first = mixed_ref[mine].reshape(width, rows).T
-    second = mixed_ref[1 - mine].reshape(width, rows).T
-    for i in range(chunks):
-        columns = slice(i * width, (i + 1) * width)
-        total = dot(second, other_ref[:, columns])
-        copies[i].wait()
-        out_ref[i] = (total + dot(first, own[:, columns])).astype(BF16)
+    for n, step in enumerate(steps):
+        start = column_start(place_ref, index ^ step, w_hbm)
+        copies.append(pltpu.make_async_copy(w_hbm.at[:, pl.ds(start, width)], own.at[n], sems.at[n]))
+        copies[n].start()
+    if first:
+        turned = outs[-1]
+        rows = turned.shape[1]
+        mine = lax.rem(place_ref[0] // 2, 2)
+        turned[0] = mixed_ref[mine].reshape(width, rows).T
+        turned[1] = mixed_ref[1 - mine].reshape(width, rows).T
+    else:
+        turned = mixed_ref
+    for n, step in enumerate(steps):
+        start = pl.multiple_of((index ^ step) * width, width)
+        total = dot(turned[1], other_ref[:, pl.ds(start, width)])
+        copies[n].wait()
+        outs[n][...] = (total + dot(turned[0], own[n])).astype(outs[n].dtype)
+
+
+def sum_kernel(own_ref, *refs):
+    total = own_ref[...]
+    for ref in refs[:-1]:
+        total = total + ref[...].astype(F32)
+    refs[-1][...] = total.astype(BF16)
 
 
 def local(projected, short_taps, long_filter, skip_gain, w_out):
@@ -236,20 +259,18 @@
     group = width // ctx
     me_ctx, me_tp, me_dp = lax.axis_index("ctx"), lax.axis_index("tp"), lax.axis_index("dp")
 
-    def partner(z, d):
-        first = d + (z - d) % tp // 2 * 2
-        return (first + (1 - (z - d) % tp % 2)) % tp
-
-    pair_route = [(z * dp + d, partner(z, d) * dp + d) for z in range(tp) for d in range(dp)]
-    pair_groups = [
-        [(c * tp + (first + d + b) % tp) * dp + d for b in range(2) for c in range(ctx)]
-        for d in range(dp)
-        for first in range(0, tp, 2)
-    ]
-    parity_groups = [list(range(odd, tp, 2)) for odd in range(2)]
     chunks = tp // 2
-    parity = (me_tp % 2).astype(jnp.int32)
-    place = ((me_tp - me_dp) % tp % 2).astype(jnp.int32)
+
+    def quad_place(q, i):
+        return 2 * i + (q + (2 * i >= tp // 2)) % 2
+
+    def device(r, d):
+        return (r + d) % tp * dp + d
+
+    pair_route = [(device(r, d), device(r ^ 1, d)) for r in range(tp) for d in range(dp)]
+    pair_groups = [[c * tp * dp + device(r, d) for r in (2 * i, 2 * i + 1) for c in range(ctx)] for d in range(dp) for i in range(chunks)]
+    quads = [[device(quad_place(q, i), d) for i in range(chunks)] for d in range(dp) for q in range(2)]
+    place = (lax.rem(me_tp - me_dp + tp, tp) * 2 + me_dp).astype(jnp.int32)[None]
 
     vmem = pl.BlockSpec(memory_space=pltpu.VMEM)
     smem = pl.BlockSpec(memory_space=pltpu.SMEM)
@@ -274,7 +295,7 @@
         ],
         compiler_params=params,
         name="prep",
-    )(parity[None], projected, long_filter, w_out)
+    )(place, projected, long_filter, w_out)
     recv = lax.all_to_all(send, "ctx", 0, 0, tiled=True)
     w_other = lax.ppermute(w_send, ("tp", "dp"), pair_route)
 
@@ -305,20 +326,35 @@
         mixed.reshape(2 * ctx, group, rows), ("ctx", "tp", "dp"), 0, 0, tiled=True, axis_index_groups=pair_groups
     ).reshape(2, ctx, group, rows)
 
-    partial = pl.pallas_call(
-        project_kernel,
-        in_specs=[smem, vmem, hbm, vmem],
-        out_specs=vmem,
-        out_shape=jax.ShapeDtypeStruct((chunks, rows, width), BF16),
-        scratch_shapes=[
-            pltpu.VMEM((width, chunks * width), BF16),
-            pltpu.SemaphoreType.DMA((chunks,)),
-        ],
+    def project(steps, operand, kind):
+        first = operand is mixed
+        block = jax.ShapeDtypeStruct((rows, width), kind)
+        extra = [jax.ShapeDtypeStruct((2, rows, width), BF16)] if first else []
+        return pl.pallas_call(
+            functools.partial(project_kernel, steps, first),
+            in_specs=[smem, vmem, hbm, vmem],
+            out_specs=[vmem for _ in steps] + [vmem] * len(extra),
+            out_shape=[block] * len(steps) + extra,
+            scratch_shapes=[pltpu.VMEM((len(steps), width, width), BF16), pltpu.SemaphoreType.DMA((len(steps),))],
+            compiler_params=pltpu.CompilerParams(vmem_limit_bytes=48 * MIB),
+            name="project",
+        )(place, operand, w_out, w_other)
+
+    def passed(block, step):
+        return lax.ppermute(block, ("tp", "dp"), [(quad[i], quad[i ^ step]) for quad in quads for i in range(chunks)])
+
+    far, turned = project((3,), mixed, BF16)
+    parts = [passed(far, 3)]
+    near = project((1, 2), turned, BF16)
+    parts += [passed(block, step) for block, step in zip(near, (1, 2))]
+    (own,) = project((0,), turned, F32)
+    return pl.pallas_call(
+        sum_kernel,
+        in_specs=[vmem] * 4,
+        out_shape=jax.ShapeDtypeStruct((rows, width), BF16),
         compiler_params=pltpu.CompilerParams(vmem_limit_bytes=48 * MIB),
-        name="project",
-    )(jnp.stack([place, parity]), mixed, w_out, w_other)
-    gathered = lax.all_to_all(partial, "tp", 0, 0, tiled=True, axis_index_groups=parity_groups)
-    return jnp.sum(gathered.astype(F32), axis=0).astype(BF16)
+        name="sum",
+    )(own, *parts)
 
 
 def solution(mesh):

time: 92.7 us -> 84.9 us (0.916)
  blocking collectives: 30.7 us -> 16.6 us
  waiting for transfers between devices: 26.1 us -> 34.1 us
  starting transfers between devices: 18.9 us -> 17 us
  Pallas kernels: 15.4 us -> 16.5 us
  other arithmetic: 1.06 us -> 0.08 us
    ppermute x0 -> x3, waiting for transfers between devices: none -> 19.1 us  [passed(): lax.ppermute(block, ('tp', 'dp'), [(quad[i], quad[i ^ step]) for quad in...]
    all_to_all x1, blocking collectives: 30.7 us -> 16.6 us  [local(): lax.all_to_all(mixed.reshape(2 * ctx, group, rows), ('ctx', 'tp', 'dp'),...]
    all_to_all x1 -> x0, waiting for transfers between devices: 11.1 us -> none  [local(): lax.all_to_all(mixed.reshape(2 * ctx, group, rows), ('ctx', 'tp', 'dp'),...]
    all_to_all x1 -> x0, starting transfers between devices: 5.65 us -> none  [local(): lax.all_to_all(mixed.reshape(2 * ctx, group, rows), ('ctx', 'tp', 'dp'),...]
    ppermute x0 -> x3, starting transfers between devices: none -> 3.71 us  [passed(): lax.ppermute(block, ('tp', 'dp'), [(quad[i], quad[i ^ step]) for quad in...]
    pallas_call x1 -> x4, Pallas kernels: 3.52 us -> 5.91 us  [the longest x3 5.09 us: project(): pl.pallas_call(functools.partial(project_kernel, steps, first), in_specs=...]
  transfers between devices with their start and end apart: 3 -> 5, of which waited for: 2 -> 4; matrix products, arithmetic and copies ran while one was open for 0% -> 0% of each run, Pallas kernels for 9% -> 13%
where the time goes in v3:
time: 84.9 us; the launch traced here: 84.5 us
  waiting for transfers between devices  34.1 us (40%)
  starting transfers between devices  17 us (20%)
  blocking collectives  16.6 us (20%)
  Pallas kernels  16.5 us (19%)
    ppermute x3, waiting for transfers between devices, passed(): lax.ppermute(block, ('tp', 'dp'), [(quad[i], quad[i ^ step]) for quad in...  19.1 us
    all_to_all x1, blocking collectives, local(): lax.all_to_all(mixed.reshape(2 * ctx, group, rows), ('ctx', 'tp', 'dp'),...  16.6 us
    all_to_all x1, waiting for transfers between devices, local(): recv = lax.all_to_all(send, 'ctx', 0, 0, tiled=True)  15 us
    pallas_call x1, Pallas kernels, local(): pl.pallas_call(conv_kernel, in_specs=[vmem, vmem, vmem, hbm], out_specs=h...  7.62 us
    all_to_all x1, starting transfers between devices, local(): recv = lax.all_to_all(send, 'ctx', 0, 0, tiled=True)  6.75 us
    ppermute x1, starting transfers between devices, local(): w_other = lax.ppermute(w_send, ('tp', 'dp'), pair_route)  6.49 us
    pallas_call x3, Pallas kernels, project(): pl.pallas_call(functools.partial(project_kernel, steps, first), in_specs=...  5.09 us
    ppermute x3, starting transfers between devices, passed(): lax.ppermute(block, ('tp', 'dp'), [(quad[i], quad[i ^ step]) for quad in...  3.71 us
  transfers between devices with their start and end apart: 5, of which 4 were waited for; matrix products, arithmetic and copies ran while one was open for 0% of the time, Pallas kernels for 13%

profile of v3, /device:TPU:1, one launch (start us, length us, event | category | flops | bytes accessed | tf_op | source)
XLA Modules:
  0.0 84.5 jit_solution(8482840770568316853)
XLA Ops:
  0.0 3.0 %prep.1 = (bf16[16,128,256]{2,1,0:T(8,128)(2,1)}, bf16[512,2048]{1,0:T(8,128)(2,1)}) custom-call(s32[1]{0:T(128)} %bitcast.place_ref, bf16[3,256,512]{2,1,0:T(8,128)(2,1)} %projected_hbm.1, f32[256,512]{1,0:T(8,128)} %filter_hbm.1, bf16[512,4096]{1,0:T(8,128)(2,1)} %w_hbm.7), custom_call_target="tpu_custom_call" | custom-call | tf_op jit(solution)/shard_map/prep/pallas_call | solution.py:280
  3.0 0.0 copy-start.1
  3.0 0.0 copy-start.2
  3.0 0.0 copy-start
  3.1 6.5 %collective-permute-start = (bf16[512,2048]{1,0:T(8,128)(2,1)}, bf16[512,2048]{1,0:T(8,128)(2,1)S(1)}, u32[]{:S(2)}, u32[]{:S(2)}) collective-permute-start(bf16[512,2048]{1,0:T(8,128)(2,1)} %get-tuple-element.12), channel_id=1, source_target_pairs={{0,2},{3,5},{2,0},{5,3},{4,6},{7,9},{6,4},{9,7},{8,10},{11,13},{10... | collective-permute-start | bytes 6291464 | tf_op jit(solution)/shard_map/ppermute | solution.py:300
  9.5 6.8 %all-to-all-start = ((bf16[16,128,256]{2,1,0:T(8,128)(2,1)}), bf16[16,128,256]{2,1,0:T(8,128)(2,1)S(1)}, u32[]{:S(2)}, u32[]{:S(2)}) async-start(bf16[16,128,256]{2,1,0:T(8,128)(2,1)} %get-tuple-element.11), calls=%async_computation | async-start | bytes 2097152 | tf_op jit(solution)/shard_map/all_to_all | solution.py:299
  16.3 0.0 copy-done.1
  16.3 0.0 copy-done.2
  16.3 0.1 fusion
  16.4 0.1 copy.12
  16.5 15.0 %all-to-all-done.recv_ref = bf16[16,128,256]{2,1,0:T(8,128)(2,1)S(1)} async-done(((bf16[16,128,256]{2,1,0:T(8,128)(2,1)}), bf16[16,128,256]{2,1,0:T(8,128)(2,1)S(1)}, u32[]{:S(2)}, u32[]{:S(2)}) %all-to-all-start) | async-done | bytes 1048608 | tf_op jit(solution)/shard_map/all_to_all | solution.py:299
  31.5 7.6 %conv.1 = bf16[2,16,32,256]{3,2,1,0:T(8,128)(2,1)S(1)} custom-call(bf16[16,128,256]{2,1,0:T(8,128)(2,1)S(1)} %all-to-all-done.recv_ref, f32[32,22]{1,0:T(8,128)S(1)} %bitcast.7, f32[2,16,1,256]{3,2,1,0:T(1,128)S(1)} %copy-done, bf16[2048,512]{1,0:T(8,128)(2,1)} %constant.31.clone.tables_hbm), custom_call_target="tpu_custom_call" | custom-call | tf_op jit(solution)/shard_map/conv/pallas_call | solution.py:305
  39.2 16.6 %all_to_all.10 = bf16[32,32,256]{2,1,0:T(8,128)(2,1)S(1)} all-to-all(bf16[32,32,256]{2,1,0:T(8,128)(2,1)S(1)} %bitcast.5), channel_id=1, replica_groups={{0,16,32,48,64,80,96,112,128,144,160,176,192,208,224,240,2,18,34,50,66,..., dimensions={0} | all-to-all | bytes 1048576 | tf_op jit(solution)/shard_map/all_to_all | solution.py:325
  55.8 0.0 collective-permute-done.other_ref
  55.8 1.5 %project.3 = (bf16[256,512]{1,0:T(8,128)(2,1)S(1)}, bf16[2,256,512]{2,1,0:T(8,128)(2,1)S(1)}) custom-call(s32[1]{0:T(128)} %bitcast.place_ref, bf16[2,16,32,256]{3,2,1,0:T(8,128)(2,1)S(1)} %bitcast.6, bf16[512,4096]{1,0:T(8,128)(2,1)} %w_hbm.7, bf16[512,2048]{1,0:T(8,128)(2,1)S(1)} %collective-permute-done.other_ref), custom_call_target="tpu_custom_call" | custom-call | tf_op jit(solution)/shard_map/project/pallas_call | solution.py:333
  57.3 0.1 collective-permute-start.1
  57.4 2.0 %project.5 = (bf16[256,512]{1,0:T(8,128)(2,1)S(1)}, bf16[256,512]{1,0:T(8,128)(2,1)S(1)}) custom-call(s32[1]{0:T(128)} %bitcast.place_ref, bf16[2,256,512]{2,1,0:T(8,128)(2,1)S(1)} %get-tuple-element.13.mixed_ref, bf16[512,4096]{1,0:T(8,128)(2,1)} %w_hbm.7, bf16[512,2048]{1,0:T(8,128)(2,1)S(1)} %collective-permute-done.other_ref), custom_call_target="tpu_custom_call" | custom-call | tf_op jit(solution)/shard_map/project/pallas_call | solution.py:333
  59.5 2.3 %collective-permute-start.2 = (bf16[256,512]{1,0:T(8,128)(2,1)S(1)}, bf16[256,512]{1,0:T(8,128)(2,1)S(1)}, u32[]{:S(2)}, u32[]{:S(2)}) collective-permute-start(bf16[256,512]{1,0:T(8,128)(2,1)S(1)} %get-tuple-element.15), channel_id=1, source_target_pairs={{0,4},{4,0},{10,14},{14,10},{2,6},{6,2},{8,12},{12,8},{3,7},{7,3},... | collective-permute-start | bytes 786440 | tf_op jit(solution)/shard_map/ppermute | solution.py:344
  61.8 1.3 %collective-permute-start.3 = (bf16[256,512]{1,0:T(8,128)(2,1)S(1)}, bf16[256,512]{1,0:T(8,128)(2,1)S(1)}, u32[]{:S(2)}, u32[]{:S(2)}) collective-permute-start(bf16[256,512]{1,0:T(8,128)(2,1)S(1)} %get-tuple-element.16), channel_id=1, source_target_pairs={{0,10},{4,14},{10,0},{14,4},{2,8},{6,12},{8,2},{12,6},{3,13},{7,1}... | collective-permute-start | bytes 786440 | tf_op jit(solution)/shard_map/ppermute | solution.py:344
  63.1 1.5 %project.4.own_ref = f32[256,512]{1,0:T(8,128)S(1)} custom-call(s32[1]{0:T(128)} %bitcast.place_ref, bf16[2,256,512]{2,1,0:T(8,128)(2,1)S(1)} %get-tuple-element.13.mixed_ref, bf16[512,4096]{1,0:T(8,128)(2,1)} %w_hbm.7, bf16[512,2048]{1,0:T(8,128)(2,1)S(1)} %collective-permute-done.other_ref), custom_call_target="tpu_custom_call" | custom-call | tf_op jit(solution)/shard_map/project/pallas_call | solution.py:333
  64.6 6.9 %collective-permute-done.1.refs_0_ = bf16[256,512]{1,0:T(8,128)(2,1)S(1)} collective-permute-done((bf16[256,512]{1,0:T(8,128)(2,1)S(1)}, bf16[256,512]{1,0:T(8,128)(2,1)S(1)}, u32[]{:S(2)}, u32[]{:S(2)}) %collective-permute-start.1) | collective-permute-done | bytes 262176 | tf_op jit(solution)/shard_map/ppermute | solution.py:344
  71.5 1.9 %collective-permute-done.2.refs_1_ = bf16[256,512]{1,0:T(8,128)(2,1)S(1)} collective-permute-done((bf16[256,512]{1,0:T(8,128)(2,1)S(1)}, bf16[256,512]{1,0:T(8,128)(2,1)S(1)}, u32[]{:S(2)}, u32[]{:S(2)}) %collective-permute-start.2) | collective-permute-done | bytes 262176 | tf_op jit(solution)/shard_map/ppermute | solution.py:344
  73.3 10.3 %collective-permute-done.3.refs_2_ = bf16[256,512]{1,0:T(8,128)(2,1)S(1)} collective-permute-done((bf16[256,512]{1,0:T(8,128)(2,1)S(1)}, bf16[256,512]{1,0:T(8,128)(2,1)S(1)}, u32[]{:S(2)}, u32[]{:S(2)}) %collective-permute-start.3) | collective-permute-done | bytes 262176 | tf_op jit(solution)/shard_map/ppermute | solution.py:344
  83.7 0.8 sum.1
  (2 shorter events, 0.0 us)
Async XLA Ops:
  3.0 13.3 %copy-start.1 = (f32[3,7,512]{2,1,0:T(8,128)S(1)}, f32[3,7,512]{2,1,0:T(8,128)}, u32[]{:S(2)}) copy-start(f32[3,7,512]{2,1,0:T(8,128)} %param.8) | copy-start | bytes 129028
  3.0 13.3 %copy-start.2 = (f32[512]{0:T(512)S(1)}, f32[512]{0:T(512)}, u32[]{:S(2)}) copy-start(f32[512]{0:T(512)} %param.10) | copy-start | bytes 6148
  3.0 28.5 %copy-start = (f32[2,16,1,256]{3,2,1,0:T(1,128)S(1)}, f32[2,16,1,256]{3,2,1,0:T(1,128)}, u32[]{:S(2)}) copy-start(f32[2,16,1,256]{3,2,1,0:T(1,128)} %constant.30.clone.tw_ref) | copy-start | bytes 98308
  3.1 52.7 %collective-permute-start = (bf16[512,2048]{1,0:T(8,128)(2,1)}, bf16[512,2048]{1,0:T(8,128)(2,1)S(1)}, u32[]{:S(2)}, u32[]{:S(2)}) collective-permute-start(bf16[512,2048]{1,0:T(8,128)(2,1)} %get-tuple-element.12), channel_id=1, source_target_pairs={{0,2},{3,5},{2,0},{5,3},{4,6},{7,9},{6,4},{9,7},{8,10},{11,13},{10... | collective-permute-start | bytes 6291464 | tf_op jit(solution)/shard_map/ppermute | solution.py:300
  9.5 22.0 %all-to-all-start = ((bf16[16,128,256]{2,1,0:T(8,128)(2,1)}), bf16[16,128,256]{2,1,0:T(8,128)(2,1)S(1)}, u32[]{:S(2)}, u32[]{:S(2)}) async-start(bf16[16,128,256]{2,1,0:T(8,128)(2,1)} %get-tuple-element.11), calls=%async_computation | async-start | bytes 2097152 | tf_op jit(solution)/shard_map/all_to_all | solution.py:299
  57.3 14.2 %collective-permute-start.1 = (bf16[256,512]{1,0:T(8,128)(2,1)S(1)}, bf16[256,512]{1,0:T(8,128)(2,1)S(1)}, u32[]{:S(2)}, u32[]{:S(2)}) collective-permute-start(bf16[256,512]{1,0:T(8,128)(2,1)S(1)} %get-tuple-element.14), channel_id=1, source_target_pairs={{0,14},{4,10},{10,4},{14,0},{2,12},{6,8},{8,6},{12,2},{3,1},{7,13}... | collective-permute-start | bytes 786440 | tf_op jit(solution)/shard_map/ppermute | solution.py:344
  59.5 13.9 %collective-permute-start.2 = (bf16[256,512]{1,0:T(8,128)(2,1)S(1)}, bf16[256,512]{1,0:T(8,128)(2,1)S(1)}, u32[]{:S(2)}, u32[]{:S(2)}) collective-permute-start(bf16[256,512]{1,0:T(8,128)(2,1)S(1)} %get-tuple-element.15), channel_id=1, source_target_pairs={{0,4},{4,0},{10,14},{14,10},{2,6},{6,2},{8,12},{12,8},{3,7},{7,3},... | collective-permute-start | bytes 786440 | tf_op jit(solution)/shard_map/ppermute | solution.py:344
  61.8 21.9 %collective-permute-start.3 = (bf16[256,512]{1,0:T(8,128)(2,1)S(1)}, bf16[256,512]{1,0:T(8,128)(2,1)S(1)}, u32[]{:S(2)}, u32[]{:S(2)}) collective-permute-start(bf16[256,512]{1,0:T(8,128)(2,1)S(1)} %get-tuple-element.16), channel_id=1, source_target_pairs={{0,10},{4,14},{10,0},{14,4},{2,8},{6,12},{8,2},{12,6},{3,13},{7,1}... | collective-permute-start | bytes 786440 | tf_op jit(solution)/shard_map/ppermute | solution.py:344

commit v4 on v3

--- a/solution.py
+++ b/solution.py
@@ -11,6 +11,7 @@
 
 TAPS = 7
 LANES = 128
+HALO = 16
 BF16 = jnp.bfloat16
 F32 = jnp.float32
 MIB = 1024 * 1024
@@ -57,15 +58,13 @@
     return pl.multiple_of(lax.rem(2 * i + lax.rem(side + upper, 2) + core, chunks) * width, width)
 
 
-def prep_kernel(
-    place_ref, projected_hbm, filter_hbm, w_hbm, out_hbm, w_send, inputs, taps_in, turned, held, sems, w_sems
-):
-    blocks, quad, rows = turned.shape
-    group = quad // 4
+def prep_kernel(place_ref, projected_hbm, filter_hbm, w_hbm, out_hbm, w_send, inputs, taps_in, turned, held, sems, w_sems):
+    blocks, lines, rows = turned.shape
+    group = lines // 3
     width = w_hbm.shape[0]
     chunks = w_send.shape[1] // width
-    arrive = [pltpu.make_async_copy(projected_hbm.at[part], inputs.at[part], sems.at[part]) for part in range(3)]
-    arrive.append(pltpu.make_async_copy(filter_hbm, taps_in, sems.at[3]))
+    arrive = [pltpu.make_async_copy(projected_hbm.at[1 + part], inputs.at[part], sems.at[part]) for part in range(2)]
+    arrive.append(pltpu.make_async_copy(filter_hbm, taps_in, sems.at[2]))
     for copy in arrive:
         copy.start()
     w_in, w_out = [], []
@@ -76,12 +75,12 @@
         w_out.append(pltpu.make_async_copy(held.at[:, columns], w_send.at[:, columns], w_sems.at[chunks + i]))
         w_in[i].start()
     leave = []
-    for part in range(4):
+    for part in range(3):
         arrive[part].wait()
-        source = inputs[part] if part < 3 else taps_in[...].astype(BF16)
-        lines = slice(part * group, (part + 1) * group)
-        turned[:, lines, :] = source.T.reshape(blocks, group, rows)
-        leave.append(pltpu.make_async_copy(turned.at[:, lines], out_hbm.at[:, lines], sems.at[4 + part]))
+        source = inputs[part] if part < 2 else taps_in[...].astype(BF16)
+        at = slice(part * group, (part + 1) * group)
+        turned[:, at, :] = source.T.reshape(blocks, group, rows)
+        leave.append(pltpu.make_async_copy(turned.at[:, at], out_hbm.at[:, at], sems.at[3 + part]))
         leave[part].start()
     for i in range(chunks):
         w_in[i].wait()
@@ -90,21 +89,32 @@
         copy.wait()
 
 
-def featurize(recv_ref, taps_ref, query, gated):
-    blocks, quad, width = recv_ref.shape
-    group = quad // 4
+def query_kernel(now_ref, before_ref, taps_ref, out_ref, whole):
+    rows = out_ref.shape[0]
+    halo = before_ref.shape[0]
+    whole[:halo] = before_ref[...].astype(F32)
+    whole[halo:] = now_ref[...].astype(F32)
+    total = taps_ref[0, 0:1, :] * whole[halo:]
+    for j in range(1, TAPS):
+        total = total + taps_ref[0, j : j + 1, :] * whole[pl.ds(halo - j, rows), :]
+    out_ref[...] = total
+
+
+def featurize(recv_ref, taps_ref, gated):
+    blocks, lines_all, width = recv_ref.shape
+    group = lines_all // 3
     tile = 16
     batch = blocks
     lane = lax.broadcasted_iota(jnp.int32, (tile, LANES), 1)
     for c0 in range(0, group, tile):
         lines = slice(c0, c0 + tile)
-        for part in (1, 2, 0):
+        for part in (1, 2):
             t = [
                 jnp.broadcast_to(taps_ref[lines, part * TAPS + j : part * TAPS + j + 1], (tile, LANES))
                 for j in range(TAPS)
             ]
             last = [jnp.zeros((tile, LANES), F32)] * 4
-            first_row = part * group + c0
+            first_row = (part - 1) * group + c0
             for s0 in range(0, blocks, batch):
                 places = [(s, lines, slice(l0, l0 + LANES)) for s in range(s0, s0 + batch) for l0 in range(0, width, LANES)]
                 now = [recv_ref[s, first_row : first_row + tile, cols].astype(F32) for s, _, cols in places]
@@ -124,7 +134,7 @@
                 if part == 2:
                     totals = [g * total for g, total in zip(gates, totals)]
                 for at, total in zip(places, totals):
-                    (query if part == 0 else gated)[at] = total
+                    gated[at] = total
 
 
 def over_blocks(values, k, blocks):
@@ -145,14 +155,14 @@
 
 
 def conv_kernel(
-    recv_ref, taps_ref, tw_ref, tables_hbm, out_hbm, query, gated, high, low, spec_h, spec_u, mixed, tables, sems, out_sems
+    recv_ref, taps_ref, tw_ref, tables_hbm, out_ref, gated, high, low, spec_h, spec_u, tables, sems
 ):
-    blocks, quad, width = recv_ref.shape
-    group = quad // 4
+    blocks, lines_all, width = recv_ref.shape
+    group = lines_all // 3
     tile = 16
     load = pltpu.make_async_copy(tables_hbm, tables, sems.at[0])
     load.start()
-    featurize(recv_ref, taps_ref, query, gated)
+    featurize(recv_ref, taps_ref, gated)
 
     def table(which, term):
         start = (2 * which + term) * 2 * width
@@ -176,7 +186,7 @@
                         store_split(rows, slice(l0, l0 + LANES), re * tr - im * ti)
                         store_split(rows, slice(width + l0, width + l0 + LANES), re * ti + im * tr)
 
-    to_odd(lambda s, c, p: recv_ref[s, 3 * group + c : 3 * group + c + tile, p].astype(F32))
+    to_odd(lambda s, c, p: recv_ref[s, 2 * group + c : 2 * group + c + tile, p].astype(F32))
     load.wait()
     spec_h[...] = lanes(0)
     to_odd(lambda s, c, p: gated[s, c : c + tile, p])
@@ -214,36 +224,34 @@
                     term = res[k] if s == 0 else res[k] * math.cos(angle) - ims[k] * math.sin(angle)
                     total = term if total is None else total + term
                 at = (s, slice(c0, c0 + tile), slice(l0, l0 + LANES))
-                mixed[at] = (query[at] * (total + skip * gated[at])).astype(BF16)
-    copies = [pltpu.make_async_copy(mixed, out_hbm.at[twin], out_sems.at[twin]) for twin in range(2)]
-    for copy in copies:
-        copy.start()
-    for copy in copies:
-        copy.wait()
-
-
-def project_kernel(steps, first, place_ref, mixed_ref, w_hbm, other_ref, *refs):
-    outs, (own, sems) = refs[:-2], refs[-2:]
+                out_ref[at] = (total + skip * gated[at]).astype(BF16)
+
+
+def mix_kernel(conv_ref, query_ref, out_ref):
+    rows, width = query_ref.shape
+    turned = conv_ref[...].reshape(width, rows).T
+    out_ref[...] = (query_ref[...] * turned.astype(F32)).astype(BF16)
+
+
+def own_kernel(place_ref, mixed_ref, w_hbm, out_ref, own, sems):
     width = w_hbm.shape[0]
     index = place_ref[0] // 4
     copies = []
-    for n, step in enumerate(steps):
+    for step in range(own.shape[0]):
         start = column_start(place_ref, index ^ step, w_hbm)
-        copies.append(pltpu.make_async_copy(w_hbm.at[:, pl.ds(start, width)], own.at[n], sems.at[n]))
-        copies[n].start()
-    if first:
-        turned = outs[-1]
-        rows = turned.shape[1]
-        mine = lax.rem(place_ref[0] // 2, 2)
-        turned[0] = mixed_ref[mine].reshape(width, rows).T
-        turned[1] = mixed_ref[1 - mine].reshape(width, rows).T
-    else:
-        turned = mixed_ref
-    for n, step in enumerate(steps):
+        copies.append(pltpu.make_async_copy(w_hbm.at[:, pl.ds(start, width)], own.at[step], sems.at[step]))
+        copies[step].start()
+    for step in reversed(range(own.shape[0])):
+        copies[step].wait()
+        out_ref[step] = dot(mixed_ref[...], own[step])
+
+
+def other_kernel(steps, place_ref, mixed_ref, own_ref, other_ref, *outs):
+    width = other_ref.shape[0]
+    index = place_ref[0] // 4
+    for step, out in zip(steps, outs):
         start = pl.multiple_of((index ^ step) * width, width)
-        total = dot(turned[1], other_ref[:, pl.ds(start, width)])
-        copies[n].wait()
-        outs[n][...] = (total + dot(turned[0], own[n])).astype(outs[n].dtype)
+        out[...] = (own_ref[step] + dot(mixed_ref[...], other_ref[:, pl.ds(start, width)])).astype(out.dtype)
 
 
 def sum_kernel(own_ref, *refs):
@@ -268,7 +276,6 @@
         return (r + d) % tp * dp + d
 
     pair_route = [(device(r, d), device(r ^ 1, d)) for r in range(tp) for d in range(dp)]
-    pair_groups = [[c * tp * dp + device(r, d) for r in (2 * i, 2 * i + 1) for c in range(ctx)] for d in range(dp) for i in range(chunks)]
     quads = [[device(quad_place(q, i), d) for i in range(chunks)] for d in range(dp) for q in range(2)]
     place = (lax.rem(me_tp - me_dp + tp, tp) * 2 + me_dp).astype(jnp.int32)[None]
 
@@ -282,15 +289,15 @@
         in_specs=[smem, hbm, hbm, hbm],
         out_specs=[hbm, hbm],
         out_shape=[
-            jax.ShapeDtypeStruct((ctx, 4 * group, rows), BF16),
+            jax.ShapeDtypeStruct((ctx, 3 * group, rows), BF16),
             jax.ShapeDtypeStruct((width, chunks * width), BF16),
         ],
         scratch_shapes=[
-            pltpu.VMEM((3, rows, width), BF16),
+            pltpu.VMEM((2, rows, width), BF16),
             pltpu.VMEM((rows, width), F32),
-            pltpu.VMEM((ctx, 4 * group, rows), BF16),
+            pltpu.VMEM((ctx, 3 * group, rows), BF16),
             pltpu.VMEM((width, chunks * width), BF16),
-            pltpu.SemaphoreType.DMA((8,)),
+            pltpu.SemaphoreType.DMA((6,)),
             pltpu.SemaphoreType.DMA((2 * chunks,)),
         ],
         compiler_params=params,
@@ -299,55 +306,72 @@
     recv = lax.all_to_all(send, "ctx", 0, 0, tiled=True)
     w_other = lax.ppermute(w_send, ("tp", "dp"), pair_route)
 
+    before = lax.ppermute(projected[0, rows - HALO :], "ctx", [(i, i + 1) for i in range(ctx - 1)])
+    query = pl.pallas_call(
+        query_kernel,
+        in_specs=[vmem] * 3,
+        out_specs=vmem,
+        out_shape=jax.ShapeDtypeStruct((rows, width), F32),
+        scratch_shapes=[pltpu.VMEM((HALO + rows, width), F32)],
+        compiler_params=pltpu.CompilerParams(vmem_limit_bytes=48 * MIB),
+        name="query",
+    )(projected[0], before, short_taps)
+
     taps = jnp.concatenate([short_taps.reshape(3 * TAPS, width), skip_gain[None, :]], axis=0)
     taps = lax.dynamic_slice_in_dim(taps, me_ctx * group, group, axis=1).T
+    taps, query = lax.optimization_barrier((taps, query))
     tables = lane_tables(rows)
-    mixed = pl.pallas_call(
+    conv = pl.pallas_call(
         conv_kernel,
         in_specs=[vmem, vmem, vmem, hbm],
-        out_specs=hbm,
-        out_shape=jax.ShapeDtypeStruct((2, ctx, group, rows), BF16),
+        out_specs=vmem,
+        out_shape=jax.ShapeDtypeStruct((ctx, group, rows), BF16),
         scratch_shapes=[
-            pltpu.VMEM((ctx, group, rows), F32),
             pltpu.VMEM((ctx, group, rows), F32),
             pltpu.VMEM((ctx * group, 2 * rows), BF16),
             pltpu.VMEM((ctx * group, 2 * rows), BF16),
             pltpu.VMEM((ctx * group, 2 * rows), F32),
             pltpu.VMEM((ctx * group, 2 * rows), F32),
-            pltpu.VMEM((ctx, group, rows), BF16),
             pltpu.VMEM(tables.shape, BF16),
             pltpu.SemaphoreType.DMA((1,)),
-            pltpu.SemaphoreType.DMA((2,)),
         ],
         compiler_params=pltpu.CompilerParams(vmem_limit_bytes=52 * MIB),
         name="conv",
     )(recv, taps, jnp.asarray(twiddles(ctx, rows)), jnp.asarray(tables))
-    mixed = lax.all_to_all(
-        mixed.reshape(2 * ctx, group, rows), ("ctx", "tp", "dp"), 0, 0, tiled=True, axis_index_groups=pair_groups
-    ).reshape(2, ctx, group, rows)
-
-    def project(steps, operand, kind):
-        first = operand is mixed
-        block = jax.ShapeDtypeStruct((rows, width), kind)
-        extra = [jax.ShapeDtypeStruct((2, rows, width), BF16)] if first else []
+    conv = lax.all_to_all(conv, "ctx", 0, 0, tiled=True)
+
+    small = pltpu.CompilerParams(vmem_limit_bytes=48 * MIB)
+    block = jax.ShapeDtypeStruct((rows, width), BF16)
+    mixed = pl.pallas_call(
+        mix_kernel, in_specs=[vmem, vmem], out_specs=vmem, out_shape=block, compiler_params=small, name="mix"
+    )(conv, query)
+    mixed_other = lax.ppermute(mixed, ("tp", "dp"), pair_route)
+    own_sums = pl.pallas_call(
+        own_kernel,
+        in_specs=[smem, vmem, hbm],
+        out_specs=vmem,
+        out_shape=jax.ShapeDtypeStruct((chunks, rows, width), F32),
+        scratch_shapes=[pltpu.VMEM((chunks, width, width), BF16), pltpu.SemaphoreType.DMA((chunks,))],
+        compiler_params=small,
+        name="own",
+    )(place, mixed, w_out)
+
+    def project(steps, kind):
         return pl.pallas_call(
-            functools.partial(project_kernel, steps, first),
-            in_specs=[smem, vmem, hbm, vmem],
-            out_specs=[vmem for _ in steps] + [vmem] * len(extra),
-            out_shape=[block] * len(steps) + extra,
-            scratch_shapes=[pltpu.VMEM((len(steps), width, width), BF16), pltpu.SemaphoreType.DMA((len(steps),))],
-            compiler_params=pltpu.CompilerParams(vmem_limit_bytes=48 * MIB),
-            name="project",
-        )(place, operand, w_out, w_other)
+            functools.partial(other_kernel, steps),
+            in_specs=[smem, vmem, vmem, vmem],
+            out_specs=[vmem] * len(steps),
+            out_shape=[jax.ShapeDtypeStruct((rows, width), kind)] * len(steps),
+            compiler_params=small,
+            name="other",
+        )(place, mixed_other, own_sums, w_other)
 
     def passed(block, step):
         return lax.ppermute(block, ("tp", "dp"), [(quad[i], quad[i ^ step]) for quad in quads for i in range(chunks)])
 
-    far, turned = project((3,), mixed, BF16)
-    parts = [passed(far, 3)]
-    near = project((1, 2), turned, BF16)
-    parts += [passed(block, step) for block, step in zip(near, (1, 2))]
-    (own,) = project((0,), turned, F32)
+    parts = [passed(block, step) for step, block in zip((3,), project((3,), BF16))]
+    parts += [passed(block, step) for step, block in zip((1, 2), project((1, 2), BF16))]
+    (own,) = project((0,), F32)
     return pl.pallas_call(
         sum_kernel,
         in_specs=[vmem] * 4,

time: 84.9 us -> 80 us (0.942)
  the two profiles are of different devices: /device:TPU:1 before, /device:TPU:32 now
where the time goes in v4:
time: 80 us; the launch traced here: 79.6 us
  waiting for transfers between devices  28.4 us (36%)
  starting transfers between devices  20.6 us (26%)
  Pallas kernels  14.5 us (18%)
  blocking collectives  12.3 us (15%)
  local copies, waits for them, and re-layouts  3.46 us (4%)
    ppermute x3, waiting for transfers between devices, passed(): lax.ppermute(block, ('tp', 'dp'), [(quad[i], quad[i ^ step]) for quad in...  18.8 us
    all_to_all x1, blocking collectives, local(): conv = lax.all_to_all(conv, 'ctx', 0, 0, tiled=True)  12.3 us
    ppermute x3, starting transfers between devices, passed(): lax.ppermute(block, ('tp', 'dp'), [(quad[i], quad[i ^ step]) for quad in...  6.67 us
    pallas_call x1, Pallas kernels, local(): pl.pallas_call(conv_kernel, in_specs=[vmem, vmem, vmem, hbm], out_specs=v...  6.19 us
    all_to_all x1, starting transfers between devices, local(): recv = lax.all_to_all(send, 'ctx', 0, 0, tiled=True)  5.3 us
    ppermute x1, waiting for transfers between devices, local(): lax.ppermute(projected[0, rows - HALO:], 'ctx', [(i, i + 1) for i in rang...  4.15 us
    all_to_all x1, waiting for transfers between devices, local(): recv = lax.all_to_all(send, 'ctx', 0, 0, tiled=True)  3.87 us
    ppermute x1, starting transfers between devices, local(): lax.ppermute(projected[0, rows - HALO:], 'ctx', [(i, i + 1) for i in rang...  3.81 us
  transfers between devices with their start and end apart: 7, of which 6 were waited for; matrix products, arithmetic and copies ran while one was open for 3% of the time, Pallas kernels for 13%

profile of v4, /device:TPU:32, one launch (start us, length us, event | category | flops | bytes accessed | tf_op | source)
XLA Modules:
  0.0 79.6 jit_solution(15966156719942378841)
XLA Ops:
  0.0 2.9 %prep.1 = (bf16[16,96,256]{2,1,0:T(8,128)(2,1)}, bf16[512,2048]{1,0:T(8,128)(2,1)}) custom-call(s32[1]{0:T(128)} %bitcast.place_ref, bf16[3,256,512]{2,1,0:T(8,128)(2,1)} %projected_hbm.1, f32[256,512]{1,0:T(8,128)} %filter_hbm.1, bf16[512,4096]{1,0:T(8,128)(2,1)} %w_hbm.3), custom_call_target="tpu_custom_call" | custom-call | tf_op jit(solution)/shard_map/prep/pallas_call | solution.py:287
  2.9 1.9 %collective-permute-start.2 = (bf16[512,2048]{1,0:T(8,128)(2,1)}, bf16[512,2048]{1,0:T(8,128)(2,1)S(1)}, u32[]{:S(2)}, u32[]{:S(2)}) collective-permute-start(bf16[512,2048]{1,0:T(8,128)(2,1)} %get-tuple-element.14), channel_id=1, source_target_pairs={{0,2},{3,5},{2,0},{5,3},{4,6},{7,9},{6,4},{9,7},{8,10},{11,13},{10... | collective-permute-start | bytes 6291464 | tf_op jit(solution)/shard_map/ppermute | solution.py:307
  4.8 5.3 %all-to-all-start = ((bf16[16,96,256]{2,1,0:T(8,128)(2,1)}), bf16[16,96,256]{2,1,0:T(8,128)(2,1)S(1)}, u32[]{:S(2)}, u32[]{:S(2)}) async-start(bf16[16,96,256]{2,1,0:T(8,128)(2,1)} %get-tuple-element.11), calls=%async_computation | async-start | bytes 1572864 | tf_op jit(solution)/shard_map/all_to_all | solution.py:306
  10.1 0.7 slice_bitcast_fusion.1
  10.9 3.8 %collective-permute-start = (bf16[16,512]{1,0:T(8,128)(2,1)S(1)}, bf16[16,512]{1,0:T(8,128)(2,1)S(1)}, u32[]{:S(2)}, u32[]{:S(2)}) collective-permute-start(bf16[16,512]{1,0:T(8,128)(2,1)S(1)} %slice_bitcast_fusion.1), channel_id=1, source_target_pairs={{0,16},{16,32},{32,48},{48,64},{64,80},{80,96},{96,112},{112,128},... | collective-permute-start | bytes 49160 | tf_op jit(solution)/shard_map/ppermute | solution.py:309
  14.7 1.7 %slice_bitcast_fusion.now_ref = bf16[256,512]{1,0:T(8,128)(2,1)} fusion(bf16[3,256,512]{2,1,0:T(8,128)(2,1)} %projected_hbm.1), kind=kLoop, calls=%fused_computation | loop fusion | bytes 524288 | tf_op jit(solution)/shard_map/squeeze | solution.py:318
  16.5 4.2 %collective-permute-done.before_ref = bf16[16,512]{1,0:T(8,128)(2,1)S(1)} collective-permute-done((bf16[16,512]{1,0:T(8,128)(2,1)S(1)}, bf16[16,512]{1,0:T(8,128)(2,1)S(1)}, u32[]{:S(2)}, u32[]{:S(2)}) %collective-permute-start) | collective-permute-done | bytes 16416 | tf_op jit(solution)/shard_map/ppermute | solution.py:309
  20.7 0.9 %copy-done = bf16[256,512]{1,0:T(8,128)(2,1)S(1)} copy-done((bf16[256,512]{1,0:T(8,128)(2,1)S(1)}, bf16[256,512]{1,0:T(8,128)(2,1)}, u32[]{:S(2)}) %copy-start) | copy-done | bytes 262168
  21.6 0.7 query.1.query_ref
  22.4 3.9 %all-to-all-done.recv_ref = bf16[16,96,256]{2,1,0:T(8,128)(2,1)S(1)} async-done(((bf16[16,96,256]{2,1,0:T(8,128)(2,1)}), bf16[16,96,256]{2,1,0:T(8,128)(2,1)S(1)}, u32[]{:S(2)}, u32[]{:S(2)}) %all-to-all-start) | async-done | bytes 786464 | tf_op jit(solution)/shard_map/all_to_all | solution.py:306
  26.3 6.2 %conv.1 = bf16[16,32,256]{2,1,0:T(8,128)(2,1)S(1)} custom-call(bf16[16,96,256]{2,1,0:T(8,128)(2,1)S(1)} %all-to-all-done.recv_ref, f32[32,22]{1,0:T(8,128)S(1)} %bitcast.7, f32[2,16,1,256]{3,2,1,0:T(1,128)S(1)} %copy-done.2, bf16[2048,512]{1,0:T(8,128)(2,1)} %constant.31.clone.tables_hbm), custom_call_target="tpu_custom_call" | custom-call | tf_op jit(solution)/shard_map/conv/pallas_call | solution.py:324
  32.5 12.3 %all_to_all.10.conv_ref = bf16[16,32,256]{2,1,0:T(8,128)(2,1)S(1)} all-to-all(bf16[16,32,256]{2,1,0:T(8,128)(2,1)S(1)} %conv.1), channel_id=1, replica_groups=mesh['ctx'=16,'tp'=8,'dp'=2] {'ctx'}, dimensions={0} | all-to-all | bytes 524288 | tf_op jit(solution)/shard_map/all_to_all | solution.py:341
  44.9 2.9 %collective-permute-start.1 = (bf16[256,512]{1,0:T(8,128)(2,1)S(1)}, bf16[256,512]{1,0:T(8,128)(2,1)S(1)}, u32[]{:S(2)}, u32[]{:S(2)}) collective-permute-start(bf16[256,512]{1,0:T(8,128)(2,1)S(1)} %mix.1.mixed_ref), channel_id=1, source_target_pairs={{0,2},{3,5},{2,0},{5,3},{4,6},{7,9},{6,4},{9,7},{8,10},{11,13},{10... | collective-permute-start | bytes 786440 | tf_op jit(solution)/shard_map/ppermute | solution.py:348
  47.9 2.8 %own.1.own_ref = f32[4,256,512]{2,1,0:T(8,128)S(1)} custom-call(s32[1]{0:T(128)} %bitcast.place_ref, bf16[256,512]{1,0:T(8,128)(2,1)S(1)} %mix.1.mixed_ref, bf16[512,4096]{1,0:T(8,128)(2,1)} %w_hbm.3), custom_call_target="tpu_custom_call" | custom-call | tf_op jit(solution)/shard_map/own/pallas_call | solution.py:349
  50.6 1.6 %collective-permute-done.1.mixed_ref = bf16[256,512]{1,0:T(8,128)(2,1)S(1)} collective-permute-done((bf16[256,512]{1,0:T(8,128)(2,1)S(1)}, bf16[256,512]{1,0:T(8,128)(2,1)S(1)}, u32[]{:S(2)}, u32[]{:S(2)}) %collective-permute-start.1) | collective-permute-done | bytes 262176 | tf_op jit(solution)/shard_map/ppermute | solution.py:348
  52.2 0.3 other.4
  52.5 4.5 %collective-permute-start.3 = (bf16[256,512]{1,0:T(8,128)(2,1)S(1)}, bf16[256,512]{1,0:T(8,128)(2,1)S(1)}, u32[]{:S(2)}, u32[]{:S(2)}) collective-permute-start(bf16[256,512]{1,0:T(8,128)(2,1)S(1)} %other.4), channel_id=1, source_target_pairs={{0,14},{4,10},{10,4},{14,0},{2,12},{6,8},{8,6},{12,2},{3,1},{7,13}... | collective-permute-start | bytes 786440 | tf_op jit(solution)/shard_map/ppermute | solution.py:370
  57.0 0.4 other.5
  57.5 0.4 collective-permute-start.4
  57.8 1.8 %collective-permute-start.5 = (bf16[256,512]{1,0:T(8,128)(2,1)S(1)}, bf16[256,512]{1,0:T(8,128)(2,1)S(1)}, u32[]{:S(2)}, u32[]{:S(2)}) collective-permute-start(bf16[256,512]{1,0:T(8,128)(2,1)S(1)} %get-tuple-element.16), channel_id=1, source_target_pairs={{0,10},{4,14},{10,0},{14,4},{2,8},{6,12},{8,2},{12,6},{3,13},{7,1}... | collective-permute-start | bytes 786440 | tf_op jit(solution)/shard_map/ppermute | solution.py:370
  59.9 11.9 %collective-permute-done.3.refs_0_ = bf16[256,512]{1,0:T(8,128)(2,1)S(1)} collective-permute-done((bf16[256,512]{1,0:T(8,128)(2,1)S(1)}, bf16[256,512]{1,0:T(8,128)(2,1)S(1)}, u32[]{:S(2)}, u32[]{:S(2)}) %collective-permute-start.3) | collective-permute-done | bytes 262176 | tf_op jit(solution)/shard_map/ppermute | solution.py:370
  71.9 2.3 %collective-permute-done.4.refs_1_ = bf16[256,512]{1,0:T(8,128)(2,1)S(1)} collective-permute-done((bf16[256,512]{1,0:T(8,128)(2,1)S(1)}, bf16[256,512]{1,0:T(8,128)(2,1)S(1)}, u32[]{:S(2)}, u32[]{:S(2)}) %collective-permute-start.4) | collective-permute-done | bytes 262176 | tf_op jit(solution)/shard_map/ppermute | solution.py:370
  74.2 4.6 %collective-permute-done.5.refs_2_ = bf16[256,512]{1,0:T(8,128)(2,1)S(1)} collective-permute-done((bf16[256,512]{1,0:T(8,128)(2,1)S(1)}, bf16[256,512]{1,0:T(8,128)(2,1)S(1)}, u32[]{:S(2)}, u32[]{:S(2)}) %collective-permute-start.5) | collective-permute-done | bytes 262176 | tf_op jit(solution)/shard_map/ppermute | solution.py:370
  78.7 0.8 %sum.1 = bf16[256,512]{1,0:T(8,128)(2,1)} custom-call(f32[256,512]{1,0:T(8,128)S(1)} %other.3.own_ref, bf16[256,512]{1,0:T(8,128)(2,1)S(1)} %collective-permute-done.3.refs_0_, bf16[256,512]{1,0:T(8,128)(2,1)S(1)} %collective-permute-done.4.refs_1_, bf16[256,512]{1,0:T(8,128)(2,1)S(1)} %collective-permute-done.5.refs_2_), custom_call_target="tpu_custom_call" | custom-call | tf_op jit(solution)/shard_map/sum/pallas_call | solution.py:375
  (13 shorter events, 0.6 us)
Async XLA Ops:
  0.0 14.7 %copy-start.1 = (f32[3,7,512]{2,1,0:T(8,128)S(1)}, f32[3,7,512]{2,1,0:T(8,128)}, u32[]{:S(2)}) copy-start(f32[3,7,512]{2,1,0:T(8,128)} %taps_ref.1) | copy-start | bytes 129028
  2.9 13.5 %copy-start.3 = (f32[512]{0:T(512)S(1)}, f32[512]{0:T(512)}, u32[]{:S(2)}) copy-start(f32[512]{0:T(512)} %param.10) | copy-start | bytes 6148
  2.9 23.4 %copy-start.2 = (f32[2,16,1,256]{3,2,1,0:T(1,128)S(1)}, f32[2,16,1,256]{3,2,1,0:T(1,128)}, u32[]{:S(2)}) copy-start(f32[2,16,1,256]{3,2,1,0:T(1,128)} %constant.30.clone.tw_ref) | copy-start | bytes 98308
  2.9 49.3 %collective-permute-start.2 = (bf16[512,2048]{1,0:T(8,128)(2,1)}, bf16[512,2048]{1,0:T(8,128)(2,1)S(1)}, u32[]{:S(2)}, u32[]{:S(2)}) collective-permute-start(bf16[512,2048]{1,0:T(8,128)(2,1)} %get-tuple-element.14), channel_id=1, source_target_pairs={{0,2},{3,5},{2,0},{5,3},{4,6},{7,9},{6,4},{9,7},{8,10},{11,13},{10... | collective-permute-start | bytes 6291464 | tf_op jit(solution)/shard_map/ppermute | solution.py:307
  4.8 21.5 %all-to-all-start = ((bf16[16,96,256]{2,1,0:T(8,128)(2,1)}), bf16[16,96,256]{2,1,0:T(8,128)(2,1)S(1)}, u32[]{:S(2)}, u32[]{:S(2)}) async-start(bf16[16,96,256]{2,1,0:T(8,128)(2,1)} %get-tuple-element.11), calls=%async_computation | async-start | bytes 1572864 | tf_op jit(solution)/shard_map/all_to_all | solution.py:306
  10.9 9.8 %collective-permute-start = (bf16[16,512]{1,0:T(8,128)(2,1)S(1)}, bf16[16,512]{1,0:T(8,128)(2,1)S(1)}, u32[]{:S(2)}, u32[]{:S(2)}) collective-permute-start(bf16[16,512]{1,0:T(8,128)(2,1)S(1)} %slice_bitcast_fusion.1), channel_id=1, source_target_pairs={{0,16},{16,32},{32,48},{48,64},{64,80},{80,96},{96,112},{112,128},... | collective-permute-start | bytes 49160 | tf_op jit(solution)/shard_map/ppermute | solution.py:309
  20.7 0.9 %copy-start = (bf16[256,512]{1,0:T(8,128)(2,1)S(1)}, bf16[256,512]{1,0:T(8,128)(2,1)}, u32[]{:S(2)}) copy-start(bf16[256,512]{1,0:T(8,128)(2,1)} %slice_bitcast_fusion.now_ref) | copy-start | bytes 786436
  44.9 7.3 %collective-permute-start.1 = (bf16[256,512]{1,0:T(8,128)(2,1)S(1)}, bf16[256,512]{1,0:T(8,128)(2,1)S(1)}, u32[]{:S(2)}, u32[]{:S(2)}) collective-permute-start(bf16[256,512]{1,0:T(8,128)(2,1)S(1)} %mix.1.mixed_ref), channel_id=1, source_target_pairs={{0,2},{3,5},{2,0},{5,3},{4,6},{7,9},{6,4},{9,7},{8,10},{11,13},{10... | collective-permute-start | bytes 786440 | tf_op jit(solution)/shard_map/ppermute | solution.py:348
  52.5 19.4 %collective-permute-start.3 = (bf16[256,512]{1,0:T(8,128)(2,1)S(1)}, bf16[256,512]{1,0:T(8,128)(2,1)S(1)}, u32[]{:S(2)}, u32[]{:S(2)}) collective-permute-start(bf16[256,512]{1,0:T(8,128)(2,1)S(1)} %other.4), channel_id=1, source_target_pairs={{0,14},{4,10},{10,4},{14,0},{2,12},{6,8},{8,6},{12,2},{3,1},{7,13}... | collective-permute-start | bytes 786440 | tf_op jit(solution)/shard_map/ppermute | solution.py:370
  57.5 16.7 %collective-permute-start.4 = (bf16[256,512]{1,0:T(8,128)(2,1)S(1)}, bf16[256,512]{1,0:T(8,128)(2,1)S(1)}, u32[]{:S(2)}, u32[]{:S(2)}) collective-permute-start(bf16[256,512]{1,0:T(8,128)(2,1)S(1)} %get-tuple-element.15), channel_id=1, source_target_pairs={{0,4},{4,0},{10,14},{14,10},{2,6},{6,2},{8,12},{12,8},{3,7},{7,3},... | collective-permute-start | bytes 786440 | tf_op jit(solution)/shard_map/ppermute | solution.py:370
  57.8 20.9 %collective-permute-start.5 = (bf16[256,512]{1,0:T(8,128)(2,1)S(1)}, bf16[256,512]{1,0:T(8,128)(2,1)S(1)}, u32[]{:S(2)}, u32[]{:S(2)}) collective-permute-start(bf16[256,512]{1,0:T(8,128)(2,1)S(1)} %get-tuple-element.16), channel_id=1, source_target_pairs={{0,10},{4,14},{10,0},{14,4},{2,8},{6,12},{8,2},{12,6},{3,13},{7,1}... | collective-permute-start | bytes 786440 | tf_op jit(solution)/shard_map/ppermute | solution.py:370

commit v5 on v4

--- a/solution.py
+++ b/solution.py
@@ -58,14 +58,17 @@
     return pl.multiple_of(lax.rem(2 * i + lax.rem(side + upper, 2) + core, chunks) * width, width)
 
 
-def prep_kernel(place_ref, projected_hbm, filter_hbm, w_hbm, out_hbm, w_send, inputs, taps_in, turned, held, sems, w_sems):
+def prep_kernel(
+    place_ref, projected_hbm, filter_hbm, w_hbm, out_hbm, w_send, tail_ref, inputs, taps_in, turned, held, sems, w_sems
+):
     blocks, lines, rows = turned.shape
     group = lines // 3
     width = w_hbm.shape[0]
     chunks = w_send.shape[1] // width
     arrive = [pltpu.make_async_copy(projected_hbm.at[1 + part], inputs.at[part], sems.at[part]) for part in range(2)]
     arrive.append(pltpu.make_async_copy(filter_hbm, taps_in, sems.at[2]))
-    for copy in arrive:
+    tail = pltpu.make_async_copy(projected_hbm.at[0, rows - HALO :], tail_ref, sems.at[6])
+    for copy in [*arrive, tail]:
         copy.start()
     w_in, w_out = [], []
     for i in range(chunks):
@@ -85,14 +88,17 @@
     for i in range(chunks):
         w_in[i].wait()
         w_out[i].start()
-    for copy in leave + w_out:
+    for copy in [*leave, *w_out, tail]:
         copy.wait()
 
 
-def query_kernel(now_ref, before_ref, taps_ref, out_ref, whole):
+def query_kernel(projected_hbm, before_ref, taps_ref, out_ref, now_ref, whole, sem):
     rows = out_ref.shape[0]
     halo = before_ref.shape[0]
+    copy = pltpu.make_async_copy(projected_hbm.at[0], now_ref, sem.at[0])
+    copy.start()
     whole[:halo] = before_ref[...].astype(F32)
+    copy.wait()
     whole[halo:] = now_ref[...].astype(F32)
     total = taps_ref[0, 0:1, :] * whole[halo:]
     for j in range(1, TAPS):
@@ -284,20 +290,21 @@
     hbm = pl.BlockSpec(memory_space=pl.ANY)
     params = pltpu.CompilerParams(vmem_limit_bytes=60 * MIB)
 
-    send, w_send = pl.pallas_call(
+    send, w_send, tail = pl.pallas_call(
         prep_kernel,
         in_specs=[smem, hbm, hbm, hbm],
-        out_specs=[hbm, hbm],
+        out_specs=[hbm, hbm, vmem],
         out_shape=[
             jax.ShapeDtypeStruct((ctx, 3 * group, rows), BF16),
             jax.ShapeDtypeStruct((width, chunks * width), BF16),
+            jax.ShapeDtypeStruct((HALO, width), BF16),
         ],
         scratch_shapes=[
             pltpu.VMEM((2, rows, width), BF16),
             pltpu.VMEM((rows, width), F32),
             pltpu.VMEM((ctx, 3 * group, rows), BF16),
             pltpu.VMEM((width, chunks * width), BF16),
-            pltpu.SemaphoreType.DMA((6,)),
+            pltpu.SemaphoreType.DMA((7,)),
             pltpu.SemaphoreType.DMA((2 * chunks,)),
         ],
         compiler_params=params,
@@ -306,20 +313,24 @@
     recv = lax.all_to_all(send, "ctx", 0, 0, tiled=True)
     w_other = lax.ppermute(w_send, ("tp", "dp"), pair_route)
 
-    before = lax.ppermute(projected[0, rows - HALO :], "ctx", [(i, i + 1) for i in range(ctx - 1)])
+    taps = jnp.concatenate([short_taps.reshape(3 * TAPS, width), skip_gain[None, :]], axis=0)
+    taps = lax.dynamic_slice_in_dim(taps, me_ctx * group, group, axis=1).T
+    before = lax.ppermute(tail, "ctx", [(i, i + 1) for i in range(ctx - 1)])
+    taps, before = lax.optimization_barrier((taps, before))
     query = pl.pallas_call(
         query_kernel,
-        in_specs=[vmem] * 3,
+        in_specs=[hbm, vmem, vmem],
         out_specs=vmem,
         out_shape=jax.ShapeDtypeStruct((rows, width), F32),
-        scratch_shapes=[pltpu.VMEM((HALO + rows, width), F32)],
-        compiler_params=pltpu.CompilerParams(vmem_limit_bytes=48 * MIB),
+        scratch_shapes=[
+            pltpu.VMEM((rows, width), BF16),
+            pltpu.VMEM((HALO + rows, width), F32),
+            pltpu.SemaphoreType.DMA((1,)),
+        ],
+        compiler_params=pltpu.CompilerParams(vmem_limit_bytes=50 * MIB),
         name="query",
-    )(projected[0], before, short_taps)
-
-    taps = jnp.concatenate([short_taps.reshape(3 * TAPS, width), skip_gain[None, :]], axis=0)
-    taps = lax.dynamic_slice_in_dim(taps, me_ctx * group, group, axis=1).T
-    taps, query = lax.optimization_barrier((taps, query))
+    )(projected, before, short_taps)
+
     tables = lane_tables(rows)
     conv = pl.pallas_call(
         conv_kernel,

time: 80 us -> 80.3 us (level)
  the two profiles are of different devices: /device:TPU:32 before, /device:TPU:1 now
where the time goes in v5:
time: 80.3 us; the launch traced here: 78.9 us
  waiting for transfers between devices  36.2 us (45%)
  starting transfers between devices  25.4 us (32%)
  Pallas kernels  15.9 us (20%)
  local copies, waits for them, and re-layouts  1.23 us (2%)
    ppermute x3, waiting for transfers between devices, passed(): lax.ppermute(block, ('tp', 'dp'), [(quad[i], quad[i ^ step]) for quad in...  17.7 us
    pallas_call x1, Pallas kernels, local(): pl.pallas_call(conv_kernel, in_specs=[vmem, vmem, vmem, hbm], out_specs=v...  6.89 us
    all_to_all x1, starting transfers between devices, local(): recv = lax.all_to_all(send, 'ctx', 0, 0, tiled=True)  6.75 us
    ppermute x1, starting transfers between devices, local(): w_other = lax.ppermute(w_send, ('tp', 'dp'), pair_route)  6.49 us
    all_to_all x1, waiting for transfers between devices, local(): conv = lax.all_to_all(conv, 'ctx', 0, 0, tiled=True)  6.1 us
    all_to_all x1, waiting for transfers between devices, local(): recv = lax.all_to_all(send, 'ctx', 0, 0, tiled=True)  5.54 us
    ppermute x3, starting transfers between devices, passed(): lax.ppermute(block, ('tp', 'dp'), [(quad[i], quad[i ^ step]) for quad in...  5.11 us
    all_to_all x1, starting transfers between devices, local(): conv = lax.all_to_all(conv, 'ctx', 0, 0, tiled=True)  3.55 us
  transfers between devices with their start and end apart: 8, of which 7 were waited for; matrix products, arithmetic and copies ran while one was open for 0% of the time, Pallas kernels for 14%

profile of v5, /device:TPU:1, one launch (start us, length us, event | category | flops | bytes accessed | tf_op | source)
XLA Modules:
  0.0 78.9 jit_solution(7421663396821354194)
XLA Ops:
  0.0 3.5 %prep.1 = (bf16[16,96,256]{2,1,0:T(8,128)(2,1)}, bf16[512,2048]{1,0:T(8,128)(2,1)}, bf16[16,512]{1,0:T(8,128)(2,1)}) custom-call(s32[1]{0:T(128)} %bitcast.place_ref, bf16[3,256,512]{2,1,0:T(8,128)(2,1)} %projected_hbm.3, f32[256,512]{1,0:T(8,128)} %filter_hbm.1, bf16[512,4096]{1,0:T(8,128)(2,1)} %w_hbm.3), custom_call_target="tpu_custom_call" | custom-call | tf_op jit(solution)/shard_map/prep/pallas_call | solution.py:293
  3.5 6.5 %collective-permute-start.2 = (bf16[512,2048]{1,0:T(8,128)(2,1)}, bf16[512,2048]{1,0:T(8,128)(2,1)S(1)}, u32[]{:S(2)}, u32[]{:S(2)}) collective-permute-start(bf16[512,2048]{1,0:T(8,128)(2,1)} %get-tuple-element.16), channel_id=1, source_target_pairs={{0,2},{3,5},{2,0},{5,3},{4,6},{7,9},{6,4},{9,7},{8,10},{11,13},{10... | collective-permute-start | bytes 6291464 | tf_op jit(solution)/shard_map/ppermute | solution.py:314
  10.0 6.8 %all-to-all-start = ((bf16[16,96,256]{2,1,0:T(8,128)(2,1)}), bf16[16,96,256]{2,1,0:T(8,128)(2,1)S(1)}, u32[]{:S(2)}, u32[]{:S(2)}) async-start(bf16[16,96,256]{2,1,0:T(8,128)(2,1)} %get-tuple-element.12), calls=%async_computation | async-start | bytes 1572864 | tf_op jit(solution)/shard_map/all_to_all | solution.py:313
  16.8 3.3 %collective-permute-start = (bf16[16,512]{1,0:T(8,128)(2,1)}, bf16[16,512]{1,0:T(8,128)(2,1)S(1)}, u32[]{:S(2)}, u32[]{:S(2)}) collective-permute-start(bf16[16,512]{1,0:T(8,128)(2,1)} %get-tuple-element.13), channel_id=1, source_target_pairs={{0,16},{16,32},{32,48},{48,64},{64,80},{80,96},{96,112},{112,128},... | collective-permute-start | bytes 49160 | tf_op jit(solution)/shard_map/ppermute | solution.py:318
  20.3 3.3 %collective-permute-done.before_ref = bf16[16,512]{1,0:T(8,128)(2,1)S(1)} collective-permute-done((bf16[16,512]{1,0:T(8,128)(2,1)}, bf16[16,512]{1,0:T(8,128)(2,1)S(1)}, u32[]{:S(2)}, u32[]{:S(2)}) %collective-permute-start) | collective-permute-done | bytes 16416 | tf_op jit(solution)/shard_map/ppermute | solution.py:318
  23.6 5.5 %all-to-all-done.recv_ref = bf16[16,96,256]{2,1,0:T(8,128)(2,1)S(1)} async-done(((bf16[16,96,256]{2,1,0:T(8,128)(2,1)}), bf16[16,96,256]{2,1,0:T(8,128)(2,1)S(1)}, u32[]{:S(2)}, u32[]{:S(2)}) %all-to-all-start) | async-done | bytes 786464 | tf_op jit(solution)/shard_map/all_to_all | solution.py:313
  29.1 6.9 %conv.1 = bf16[16,32,256]{2,1,0:T(8,128)(2,1)} custom-call(bf16[16,96,256]{2,1,0:T(8,128)(2,1)S(1)} %all-to-all-done.recv_ref, f32[32,22]{1,0:T(8,128)S(1)} %bitcast.3, f32[2,16,1,256]{3,2,1,0:T(1,128)S(1)} %copy-done.2, bf16[2048,512]{1,0:T(8,128)(2,1)} %constant.31.clone.tables_hbm), custom_call_target="tpu_custom_call" | custom-call | tf_op jit(solution)/shard_map/conv/pallas_call | solution.py:335
  36.0 3.5 %all-to-all-start.1 = ((bf16[16,32,256]{2,1,0:T(8,128)(2,1)}), bf16[16,32,256]{2,1,0:T(8,128)(2,1)S(1)}, u32[]{:S(2)}, u32[]{:S(2)}) async-start(bf16[16,32,256]{2,1,0:T(8,128)(2,1)} %conv.1), calls=%async_computation.1 | async-start | bytes 524288 | tf_op jit(solution)/shard_map/all_to_all | solution.py:352
  39.6 1.1 %copy-done = bf16[3,256,512]{2,1,0:T(8,128)(2,1)S(1)} copy-done((bf16[3,256,512]{2,1,0:T(8,128)(2,1)S(1)}, bf16[3,256,512]{2,1,0:T(8,128)(2,1)}, u32[]{:S(2)}) %copy-start) | copy-done | bytes 786456
  40.7 0.8 query.1.query_ref
  41.5 6.1 %all-to-all-done.1.conv_ref = bf16[16,32,256]{2,1,0:T(8,128)(2,1)S(1)} async-done(((bf16[16,32,256]{2,1,0:T(8,128)(2,1)}), bf16[16,32,256]{2,1,0:T(8,128)(2,1)S(1)}, u32[]{:S(2)}, u32[]{:S(2)}) %all-to-all-start.1) | async-done | bytes 262176 | tf_op jit(solution)/shard_map/all_to_all | solution.py:352
  47.6 0.1 mix.1.mixed_ref
  47.7 0.2 collective-permute-start.1
  47.9 2.8 %own.1.own_ref = f32[4,256,512]{2,1,0:T(8,128)S(1)} custom-call(s32[1]{0:T(128)} %bitcast.place_ref, bf16[256,512]{1,0:T(8,128)(2,1)S(1)} %mix.1.mixed_ref, bf16[512,4096]{1,0:T(8,128)(2,1)} %w_hbm.3), custom_call_target="tpu_custom_call" | custom-call | tf_op jit(solution)/shard_map/own/pallas_call | solution.py:360
  50.7 3.5 %collective-permute-done.1.mixed_ref = bf16[256,512]{1,0:T(8,128)(2,1)S(1)} collective-permute-done((bf16[256,512]{1,0:T(8,128)(2,1)S(1)}, bf16[256,512]{1,0:T(8,128)(2,1)S(1)}, u32[]{:S(2)}, u32[]{:S(2)}) %collective-permute-start.1) | collective-permute-done | bytes 262176 | tf_op jit(solution)/shard_map/ppermute | solution.py:359
  54.2 0.3 other.4
  54.5 0.1 collective-permute-start.3
  54.6 0.5 other.5
  55.1 5.0 %collective-permute-start.4 = (bf16[256,512]{1,0:T(8,128)(2,1)S(1)}, bf16[256,512]{1,0:T(8,128)(2,1)S(1)}, u32[]{:S(2)}, u32[]{:S(2)}) collective-permute-start(bf16[256,512]{1,0:T(8,128)(2,1)S(1)} %get-tuple-element.17), channel_id=1, source_target_pairs={{0,4},{4,0},{10,14},{14,10},{2,6},{6,2},{8,12},{12,8},{3,7},{7,3},... | collective-permute-start | bytes 786440 | tf_op jit(solution)/shard_map/ppermute | solution.py:381
  60.1 0.3 other.3.own_ref
  60.4 1.6 %collective-permute-done.3.refs_0_ = bf16[256,512]{1,0:T(8,128)(2,1)S(1)} collective-permute-done((bf16[256,512]{1,0:T(8,128)(2,1)S(1)}, bf16[256,512]{1,0:T(8,128)(2,1)S(1)}, u32[]{:S(2)}, u32[]{:S(2)}) %collective-permute-start.3) | collective-permute-done | bytes 262176 | tf_op jit(solution)/shard_map/ppermute | solution.py:381
  62.1 13.4 %collective-permute-done.4.refs_1_ = bf16[256,512]{1,0:T(8,128)(2,1)S(1)} collective-permute-done((bf16[256,512]{1,0:T(8,128)(2,1)S(1)}, bf16[256,512]{1,0:T(8,128)(2,1)S(1)}, u32[]{:S(2)}, u32[]{:S(2)}) %collective-permute-start.4) | collective-permute-done | bytes 262176 | tf_op jit(solution)/shard_map/ppermute | solution.py:381
  75.5 2.6 %collective-permute-done.5.refs_2_ = bf16[256,512]{1,0:T(8,128)(2,1)S(1)} collective-permute-done((bf16[256,512]{1,0:T(8,128)(2,1)S(1)}, bf16[256,512]{1,0:T(8,128)(2,1)S(1)}, u32[]{:S(2)}, u32[]{:S(2)}) %collective-permute-start.5) | collective-permute-done | bytes 262176 | tf_op jit(solution)/shard_map/ppermute | solution.py:381
  78.1 0.8 %sum.1 = bf16[256,512]{1,0:T(8,128)(2,1)} custom-call(f32[256,512]{1,0:T(8,128)S(1)} %other.3.own_ref, bf16[256,512]{1,0:T(8,128)(2,1)S(1)} %collective-permute-done.3.refs_0_, bf16[256,512]{1,0:T(8,128)(2,1)S(1)} %collective-permute-done.4.refs_1_, bf16[256,512]{1,0:T(8,128)(2,1)S(1)} %collective-permute-done.5.refs_2_), custom_call_target="tpu_custom_call" | custom-call | tf_op jit(solution)/shard_map/sum/pallas_call | solution.py:386
  (12 shorter events, 0.2 us)
Async XLA Ops:
  0.0 20.1 %copy-start.1 = (f32[3,7,512]{2,1,0:T(8,128)S(1)}, f32[3,7,512]{2,1,0:T(8,128)}, u32[]{:S(2)}) copy-start(f32[3,7,512]{2,1,0:T(8,128)} %taps_ref.1) | copy-start | bytes 129028
  0.0 20.1 %copy-start.3 = (f32[512]{0:T(512)S(1)}, f32[512]{0:T(512)}, u32[]{:S(2)}) copy-start(f32[512]{0:T(512)} %param.10) | copy-start | bytes 6148
  0.0 29.1 %copy-start.2 = (f32[2,16,1,256]{3,2,1,0:T(1,128)S(1)}, f32[2,16,1,256]{3,2,1,0:T(1,128)}, u32[]{:S(2)}) copy-start(f32[2,16,1,256]{3,2,1,0:T(1,128)} %constant.30.clone.tw_ref) | copy-start | bytes 98308
  3.5 50.7 %collective-permute-start.2 = (bf16[512,2048]{1,0:T(8,128)(2,1)}, bf16[512,2048]{1,0:T(8,128)(2,1)S(1)}, u32[]{:S(2)}, u32[]{:S(2)}) collective-permute-start(bf16[512,2048]{1,0:T(8,128)(2,1)} %get-tuple-element.16), channel_id=1, source_target_pairs={{0,2},{3,5},{2,0},{5,3},{4,6},{7,9},{6,4},{9,7},{8,10},{11,13},{10... | collective-permute-start | bytes 6291464 | tf_op jit(solution)/shard_map/ppermute | solution.py:314
  10.0 19.1 %all-to-all-start = ((bf16[16,96,256]{2,1,0:T(8,128)(2,1)}), bf16[16,96,256]{2,1,0:T(8,128)(2,1)S(1)}, u32[]{:S(2)}, u32[]{:S(2)}) async-start(bf16[16,96,256]{2,1,0:T(8,128)(2,1)} %get-tuple-element.12), calls=%async_computation | async-start | bytes 1572864 | tf_op jit(solution)/shard_map/all_to_all | solution.py:313
  16.8 6.8 %collective-permute-start = (bf16[16,512]{1,0:T(8,128)(2,1)}, bf16[16,512]{1,0:T(8,128)(2,1)S(1)}, u32[]{:S(2)}, u32[]{:S(2)}) collective-permute-start(bf16[16,512]{1,0:T(8,128)(2,1)} %get-tuple-element.13), channel_id=1, source_target_pairs={{0,16},{16,32},{32,48},{48,64},{64,80},{80,96},{96,112},{112,128},... | collective-permute-start | bytes 49160 | tf_op jit(solution)/shard_map/ppermute | solution.py:318
  36.0 11.6 %all-to-all-start.1 = ((bf16[16,32,256]{2,1,0:T(8,128)(2,1)}), bf16[16,32,256]{2,1,0:T(8,128)(2,1)S(1)}, u32[]{:S(2)}, u32[]{:S(2)}) async-start(bf16[16,32,256]{2,1,0:T(8,128)(2,1)} %conv.1), calls=%async_computation.1 | async-start | bytes 524288 | tf_op jit(solution)/shard_map/all_to_all | solution.py:352
  39.6 1.1 %copy-start = (bf16[3,256,512]{2,1,0:T(8,128)(2,1)S(1)}, bf16[3,256,512]{2,1,0:T(8,128)(2,1)}, u32[]{:S(2)}) copy-start(bf16[3,256,512]{2,1,0:T(8,128)(2,1)} %projected_hbm.3) | copy-start | bytes 2359300
  47.7 6.5 %collective-permute-start.1 = (bf16[256,512]{1,0:T(8,128)(2,1)S(1)}, bf16[256,512]{1,0:T(8,128)(2,1)S(1)}, u32[]{:S(2)}, u32[]{:S(2)}) collective-permute-start(bf16[256,512]{1,0:T(8,128)(2,1)S(1)} %mix.1.mixed_ref), channel_id=1, source_target_pairs={{0,2},{3,5},{2,0},{5,3},{4,6},{7,9},{6,4},{9,7},{8,10},{11,13},{10... | collective-permute-start | bytes 786440 | tf_op jit(solution)/shard_map/ppermute | solution.py:359
  54.5 7.5 %collective-permute-start.3 = (bf16[256,512]{1,0:T(8,128)(2,1)S(1)}, bf16[256,512]{1,0:T(8,128)(2,1)S(1)}, u32[]{:S(2)}, u32[]{:S(2)}) collective-permute-start(bf16[256,512]{1,0:T(8,128)(2,1)S(1)} %other.4), channel_id=1, source_target_pairs={{0,14},{4,10},{10,4},{14,0},{2,12},{6,8},{8,6},{12,2},{3,1},{7,13}... | collective-permute-start | bytes 786440 | tf_op jit(solution)/shard_map/ppermute | solution.py:381
  55.1 20.4 %collective-permute-start.4 = (bf16[256,512]{1,0:T(8,128)(2,1)S(1)}, bf16[256,512]{1,0:T(8,128)(2,1)S(1)}, u32[]{:S(2)}, u32[]{:S(2)}) collective-permute-start(bf16[256,512]{1,0:T(8,128)(2,1)S(1)} %get-tuple-element.17), channel_id=1, source_target_pairs={{0,4},{4,0},{10,14},{14,10},{2,6},{6,2},{8,12},{12,8},{3,7},{7,3},... | collective-permute-start | bytes 786440 | tf_op jit(solution)/shard_map/ppermute | solution.py:381
  60.1 18.0 %collective-permute-start.5 = (bf16[256,512]{1,0:T(8,128)(2,1)S(1)}, bf16[256,512]{1,0:T(8,128)(2,1)S(1)}, u32[]{:S(2)}, u32[]{:S(2)}) collective-permute-start(bf16[256,512]{1,0:T(8,128)(2,1)S(1)} %get-tuple-element.18), channel_id=1, source_target_pairs={{0,10},{4,14},{10,0},{14,4},{2,8},{6,12},{8,2},{12,6},{3,13},{7,1}... | collective-permute-start | bytes 786440 | tf_op jit(solution)/shard_map/ppermute | solution.py:381

commit v6 on v4

--- a/solution.py
+++ b/solution.py
@@ -12,6 +12,7 @@
 TAPS = 7
 LANES = 128
 HALO = 16
+EDGE_LANES = 64
 BF16 = jnp.bfloat16
 F32 = jnp.float32
 MIB = 1024 * 1024
@@ -58,13 +59,20 @@
     return pl.multiple_of(lax.rem(2 * i + lax.rem(side + upper, 2) + core, chunks) * width, width)
 
 
-def prep_kernel(place_ref, projected_hbm, filter_hbm, w_hbm, out_hbm, w_send, inputs, taps_in, turned, held, sems, w_sems):
-    blocks, lines, rows = turned.shape
-    group = lines // 3
-    width = w_hbm.shape[0]
+def prep_kernel(
+    place_ref, projected_hbm, filter_hbm, taps_hbm, w_hbm, out_hbm, w_send,
+    inputs, filter_in, taps, whole, edges, turned, held, sems, w_sems,
+):
+    blocks, group, _ = turned.shape
+    rows, width = inputs.shape[1:]
+    halo = TAPS - 1
     chunks = w_send.shape[1] // width
-    arrive = [pltpu.make_async_copy(projected_hbm.at[1 + part], inputs.at[part], sems.at[part]) for part in range(2)]
-    arrive.append(pltpu.make_async_copy(filter_hbm, taps_in, sems.at[2]))
+    arrive = [
+        pltpu.make_async_copy(filter_hbm, filter_in, sems.at[0]),
+        pltpu.make_async_copy(taps_hbm, taps, sems.at[1]),
+        pltpu.make_async_copy(projected_hbm.at[1], inputs.at[0], sems.at[2]),
+        pltpu.make_async_copy(projected_hbm.at[2], inputs.at[1], sems.at[3]),
+    ]
     for copy in arrive:
         copy.start()
     w_in, w_out = [], []
@@ -75,13 +83,31 @@
         w_out.append(pltpu.make_async_copy(held.at[:, columns], w_send.at[:, columns], w_sems.at[chunks + i]))
         w_in[i].start()
     leave = []
-    for part in range(3):
-        arrive[part].wait()
-        source = inputs[part] if part < 2 else taps_in[...].astype(BF16)
-        at = slice(part * group, (part + 1) * group)
-        turned[:, at, :] = source.T.reshape(blocks, group, rows)
-        leave.append(pltpu.make_async_copy(turned.at[:, at], out_hbm.at[:, at], sems.at[3 + part]))
-        leave[part].start()
+
+    def store(values, lanes):
+        turned[:, :, lanes] = values.astype(BF16).T.reshape(blocks, group, -1)
+        leave.append(pltpu.make_async_copy(turned.at[:, :, lanes], out_hbm.at[:, :, lanes], sems.at[4 + len(leave)]))
+        leave[-1].start()
+
+    arrive[0].wait()
+    store(filter_in[...], slice(rows, 2 * rows))
+    arrive[1].wait()
+    edges[...] = jnp.zeros_like(edges)
+    gated = None
+    for part in range(2):
+        arrive[2 + part].wait()
+        now = whole.at[part]
+        now[:8] = jnp.zeros((8, width), F32)
+        now[8:] = inputs[part].astype(F32)
+        first = part * EDGE_LANES
+        edges[first : first + halo] = now[rows + 8 - halo : rows + 8]
+        edges[first + halo : first + 2 * halo] = now[8 : 8 + halo]
+        total = taps[1 + part, 0:1, :] * now[8:]
+        for j in range(1, TAPS):
+            total = total + taps[1 + part, j : j + 1, :] * now[8 - j : 8 - j + rows]
+        gated = total if gated is None else gated * total
+    store(edges[...], slice(2 * rows, 2 * rows + LANES))
+    store(gated, slice(0, rows))
     for i in range(chunks):
         w_in[i].wait()
         w_out[i].start()
@@ -100,41 +126,33 @@
     out_ref[...] = total
 
 
-def featurize(recv_ref, taps_ref, gated):
-    blocks, lines_all, width = recv_ref.shape
-    group = lines_all // 3
+def complete(recv_ref, taps_ref, gated):
+    blocks, group, lanes_all = recv_ref.shape
+    width = (lanes_all - LANES) // 2
+    halo = TAPS - 1
     tile = 16
-    batch = blocks
     lane = lax.broadcasted_iota(jnp.int32, (tile, LANES), 1)
+    value_side = lane >= EDGE_LANES
+    tail = (lane < halo) | (value_side & (lane < EDGE_LANES + halo))
     for c0 in range(0, group, tile):
         lines = slice(c0, c0 + tile)
-        for part in (1, 2):
-            t = [
-                jnp.broadcast_to(taps_ref[lines, part * TAPS + j : part * TAPS + j + 1], (tile, LANES))
-                for j in range(TAPS)
-            ]
-            last = [jnp.zeros((tile, LANES), F32)] * 4
-            first_row = (part - 1) * group + c0
-            for s0 in range(0, blocks, batch):
-                places = [(s, lines, slice(l0, l0 + LANES)) for s in range(s0, s0 + batch) for l0 in range(0, width, LANES)]
-                now = [recv_ref[s, first_row : first_row + tile, cols].astype(F32) for s, _, cols in places]
-                gates = [gated[at] for at in places] if part == 2 else None
-
-                def shifted(values, amount, which):
-                    turns = [pltpu.roll(value, amount, 1) for value in values]
-                    moved = [jnp.where(lane < amount, b, a) for b, a in zip([last[which]] + turns[:-1], turns)]
-                    last[which] = turns[-1]
-                    return moved
-
-                one = shifted(now, 1, 0)
-                two = shifted([t[2] * x + t[3] * y for x, y in zip(now, one)], 2, 1)
-                four = shifted([t[4] * x + t[5] * y for x, y in zip(now, one)], 4, 2)
-                six = shifted([t[6] * x for x in now], 6, 3)
-                totals = [t[0] * x + t[1] * y + a + b + c for x, y, a, b, c in zip(now, one, two, four, six)]
-                if part == 2:
-                    totals = [g * total for g, total in zip(gates, totals)]
-                for at, total in zip(places, totals):
-                    gated[at] = total
+        t = []
+        for j in range(TAPS):
+            key, value = (taps_ref[lines, part * TAPS + j : part * TAPS + j + 1] for part in (1, 2))
+            t.append(jnp.where(value_side, jnp.broadcast_to(value, lane.shape), jnp.broadcast_to(key, lane.shape)))
+        packs = [recv_ref[s, lines, 2 * width :].astype(F32) for s in range(blocks)]
+        starts = [recv_ref[s, lines, :LANES].astype(F32) for s in range(blocks)]
+        rests = [recv_ref[s, lines, LANES:width].astype(F32) for s in range(blocks)]
+        spans = [jnp.where(tail, b, a) for b, a in zip([jnp.zeros_like(packs[0])] + packs[:-1], packs)]
+        totals = [t[0] * span for span in spans]
+        for j in range(1, TAPS):
+            totals = [total + t[j] * pltpu.roll(span, j, 1) for total, span in zip(totals, spans)]
+        firsts = [total * pltpu.roll(total, EDGE_LANES, 1) for total in totals]
+        firsts = [pltpu.roll(first, LANES - halo, 1) for first in firsts]
+        starts = [jnp.where(lane < halo, first, start) for first, start in zip(firsts, starts)]
+        for s in range(blocks):
+            gated[s, lines, :LANES] = starts[s]
+            gated[s, lines, LANES:width] = rests[s]
 
 
 def over_blocks(values, k, blocks):
@@ -157,12 +175,12 @@
 def conv_kernel(
     recv_ref, taps_ref, tw_ref, tables_hbm, out_ref, gated, high, low, spec_h, spec_u, tables, sems
 ):
-    blocks, lines_all, width = recv_ref.shape
-    group = lines_all // 3
+    blocks, group, lanes_all = recv_ref.shape
+    width = (lanes_all - LANES) // 2
     tile = 16
     load = pltpu.make_async_copy(tables_hbm, tables, sems.at[0])
     load.start()
-    featurize(recv_ref, taps_ref, gated)
+    complete(recv_ref, taps_ref, gated)
 
     def table(which, term):
         start = (2 * which + term) * 2 * width
@@ -186,7 +204,7 @@
                         store_split(rows, slice(l0, l0 + LANES), re * tr - im * ti)
                         store_split(rows, slice(width + l0, width + l0 + LANES), re * ti + im * tr)
 
-    to_odd(lambda s, c, p: recv_ref[s, 2 * group + c : 2 * group + c + tile, p].astype(F32))
+    to_odd(lambda s, c, p: recv_ref[s, c : c + tile, width + p.start : width + p.stop].astype(F32))
     load.wait()
     spec_h[...] = lanes(0)
     to_odd(lambda s, c, p: gated[s, c : c + tile, p])
@@ -286,23 +304,26 @@
 
     send, w_send = pl.pallas_call(
         prep_kernel,
-        in_specs=[smem, hbm, hbm, hbm],
+        in_specs=[smem, hbm, hbm, hbm, hbm],
         out_specs=[hbm, hbm],
         out_shape=[
-            jax.ShapeDtypeStruct((ctx, 3 * group, rows), BF16),
+            jax.ShapeDtypeStruct((ctx, group, 2 * rows + LANES), BF16),
             jax.ShapeDtypeStruct((width, chunks * width), BF16),
         ],
         scratch_shapes=[
             pltpu.VMEM((2, rows, width), BF16),
             pltpu.VMEM((rows, width), F32),
-            pltpu.VMEM((ctx, 3 * group, rows), BF16),
+            pltpu.VMEM(short_taps.shape, F32),
+            pltpu.VMEM((2, 8 + rows, width), F32),
+            pltpu.VMEM((LANES, width), F32),
+            pltpu.VMEM((ctx, group, 2 * rows + LANES), BF16),
             pltpu.VMEM((width, chunks * width), BF16),
-            pltpu.SemaphoreType.DMA((6,)),
+            pltpu.SemaphoreType.DMA((7,)),
             pltpu.SemaphoreType.DMA((2 * chunks,)),
         ],
         compiler_params=params,
         name="prep",
-    )(place, projected, long_filter, w_out)
+    )(place, projected, long_filter, short_taps, w_out)
     recv = lax.all_to_all(send, "ctx", 0, 0, tiled=True)
     w_other = lax.ppermute(w_send, ("tp", "dp"), pair_route)
 
@@ -369,8 +390,8 @@
     def passed(block, step):
         return lax.ppermute(block, ("tp", "dp"), [(quad[i], quad[i ^ step]) for quad in quads for i in range(chunks)])
 
-    parts = [passed(block, step) for step, block in zip((3,), project((3,), BF16))]
-    parts += [passed(block, step) for step, block in zip((1, 2), project((1, 2), BF16))]
+    parts = [passed(block, step) for step, block in zip((2,), project((2,), BF16))]
+    parts += [passed(block, step) for step, block in zip((3, 1), project((3, 1), BF16))]
     (own,) = project((0,), F32)
     return pl.pallas_call(
         sum_kernel,

time: 80 us -> 80.2 us (level)
  the two profiles are of different devices: /device:TPU:32 before, /device:TPU:8 now
where the time goes in v6:
time: 80.2 us; the launch traced here: 79.6 us
  waiting for transfers between devices  23.2 us (29%)
  starting transfers between devices  19.5 us (24%)
  blocking collectives  16.8 us (21%)
  Pallas kernels  15.2 us (19%)
  local copies, waits for them, and re-layouts  4.67 us (6%)
    ppermute x3, waiting for transfers between devices, passed(): lax.ppermute(block, ('tp', 'dp'), [(quad[i], quad[i ^ step]) for quad in...  17.3 us
    all_to_all x1, blocking collectives, local(): conv = lax.all_to_all(conv, 'ctx', 0, 0, tiled=True)  16.8 us
    all_to_all x1, starting transfers between devices, local(): recv = lax.all_to_all(send, 'ctx', 0, 0, tiled=True)  7.39 us
    ppermute x3, starting transfers between devices, passed(): lax.ppermute(block, ('tp', 'dp'), [(quad[i], quad[i ^ step]) for quad in...  6.66 us
    pallas_call x1, Pallas kernels, local(): pl.pallas_call(conv_kernel, in_specs=[vmem, vmem, vmem, hbm], out_specs=v...  5.55 us
    pallas_call x1, Pallas kernels, local(): pl.pallas_call(prep_kernel, in_specs=[smem, hbm, hbm, hbm, hbm], out_spec...  4.13 us
    ppermute x1, waiting for transfers between devices, local(): mixed_other = lax.ppermute(mixed, ('tp', 'dp'), pair_route)  3.54 us
    ppermute x1, starting transfers between devices, local(): lax.ppermute(projected[0, rows - HALO:], 'ctx', [(i, i + 1) for i in rang...  3.36 us
  transfers between devices with their start and end apart: 7, of which 6 were waited for; matrix products, arithmetic and copies ran while one was open for 2% of the time, Pallas kernels for 13%

profile of v6, /device:TPU:8, one launch (start us, length us, event | category | flops | bytes accessed | tf_op | source)
XLA Modules:
  0.0 79.6 jit_solution(16076017170527132254)
XLA Ops:
  0.0 4.1 %prep.1 = (bf16[16,32,640]{2,1,0:T(8,128)(2,1)}, bf16[512,2048]{1,0:T(8,128)(2,1)}) custom-call(s32[1]{0:T(128)} %bitcast.place_ref, bf16[3,256,512]{2,1,0:T(8,128)(2,1)} %projected_hbm.1, f32[256,512]{1,0:T(8,128)} %filter_hbm.1, f32[3,7,512]{2,1,0:T(8,128)} %taps_ref.1, bf16[512,4096]{1,0:T(8,128)(2,1)} %w_hbm.3), custom_call_target="tpu_custom_call" | custom-call | tf_op jit(solution)/shard_map/prep/pallas_call | solution.py:305
  4.1 2.0 %collective-permute-start.2 = (bf16[512,2048]{1,0:T(8,128)(2,1)}, bf16[512,2048]{1,0:T(8,128)(2,1)S(1)}, u32[]{:S(2)}, u32[]{:S(2)}) collective-permute-start(bf16[512,2048]{1,0:T(8,128)(2,1)} %get-tuple-element.14), channel_id=1, source_target_pairs={{0,2},{3,5},{2,0},{5,3},{4,6},{7,9},{6,4},{9,7},{8,10},{11,13},{10... | collective-permute-start | bytes 6291464 | tf_op jit(solution)/shard_map/ppermute | solution.py:328
  6.1 7.4 %all-to-all-start = ((bf16[16,32,640]{2,1,0:T(8,128)(2,1)}), bf16[16,32,640]{2,1,0:T(8,128)(2,1)S(1)}, u32[]{:S(2)}, u32[]{:S(2)}) async-start(bf16[16,32,640]{2,1,0:T(8,128)(2,1)} %get-tuple-element.11), calls=%async_computation | async-start | bytes 1310720 | tf_op jit(solution)/shard_map/all_to_all | solution.py:327
  13.5 0.7 slice_bitcast_fusion.1
  14.3 3.4 %collective-permute-start = (bf16[16,512]{1,0:T(8,128)(2,1)S(1)}, bf16[16,512]{1,0:T(8,128)(2,1)S(1)}, u32[]{:S(2)}, u32[]{:S(2)}) collective-permute-start(bf16[16,512]{1,0:T(8,128)(2,1)S(1)} %slice_bitcast_fusion.1), channel_id=1, source_target_pairs={{0,16},{16,32},{32,48},{48,64},{64,80},{80,96},{96,112},{112,128},... | collective-permute-start | bytes 49160 | tf_op jit(solution)/shard_map/ppermute | solution.py:330
  17.7 1.0 %slice_bitcast_fusion.now_ref = bf16[256,512]{1,0:T(8,128)(2,1)S(1)} fusion(bf16[3,256,512]{2,1,0:T(8,128)(2,1)} %projected_hbm.1), kind=kLoop, calls=%fused_computation | loop fusion | bytes 524288 | tf_op jit(solution)/shard_map/squeeze | solution.py:339
  18.8 2.2 %collective-permute-done.before_ref = bf16[16,512]{1,0:T(8,128)(2,1)S(1)} collective-permute-done((bf16[16,512]{1,0:T(8,128)(2,1)S(1)}, bf16[16,512]{1,0:T(8,128)(2,1)S(1)}, u32[]{:S(2)}, u32[]{:S(2)}) %collective-permute-start) | collective-permute-done | bytes 16416 | tf_op jit(solution)/shard_map/ppermute | solution.py:330
  21.0 0.6 copy-done.3
  21.6 0.8 copy-done.1
  22.4 0.7 copy-done.4
  23.1 0.7 query.1.query_ref
  24.1 0.8 copy-done.2
  24.8 5.6 %conv.1 = bf16[16,32,256]{2,1,0:T(8,128)(2,1)S(1)} custom-call(bf16[16,32,640]{2,1,0:T(8,128)(2,1)S(1)} %all-to-all-done.recv_ref, f32[32,22]{1,0:T(8,128)S(1)} %bitcast.7, f32[2,16,1,256]{3,2,1,0:T(1,128)S(1)} %copy-done.2, bf16[2048,512]{1,0:T(8,128)(2,1)} %constant.31.clone.tables_hbm), custom_call_target="tpu_custom_call" | custom-call | tf_op jit(solution)/shard_map/conv/pallas_call | solution.py:345
  30.4 16.8 %all_to_all.10.conv_ref = bf16[16,32,256]{2,1,0:T(8,128)(2,1)S(1)} all-to-all(bf16[16,32,256]{2,1,0:T(8,128)(2,1)S(1)} %conv.1), channel_id=1, replica_groups=mesh['ctx'=16,'tp'=8,'dp'=2] {'ctx'}, dimensions={0} | all-to-all | bytes 524288 | tf_op jit(solution)/shard_map/all_to_all | solution.py:362
  47.5 2.8 %own.1.own_ref = f32[4,256,512]{2,1,0:T(8,128)S(1)} custom-call(s32[1]{0:T(128)} %bitcast.place_ref, bf16[256,512]{1,0:T(8,128)(2,1)S(1)} %mix.1.mixed_ref, bf16[512,4096]{1,0:T(8,128)(2,1)} %w_hbm.3), custom_call_target="tpu_custom_call" | custom-call | tf_op jit(solution)/shard_map/own/pallas_call | solution.py:370
  50.3 3.5 %collective-permute-done.1.mixed_ref = bf16[256,512]{1,0:T(8,128)(2,1)S(1)} collective-permute-done((bf16[256,512]{1,0:T(8,128)(2,1)S(1)}, bf16[256,512]{1,0:T(8,128)(2,1)S(1)}, u32[]{:S(2)}, u32[]{:S(2)}) %collective-permute-start.1) | collective-permute-done | bytes 262176 | tf_op jit(solution)/shard_map/ppermute | solution.py:369
  53.8 0.3 other.4
  54.1 4.1 %collective-permute-start.3 = (bf16[256,512]{1,0:T(8,128)(2,1)S(1)}, bf16[256,512]{1,0:T(8,128)(2,1)S(1)}, u32[]{:S(2)}, u32[]{:S(2)}) collective-permute-start(bf16[256,512]{1,0:T(8,128)(2,1)S(1)} %other.4), channel_id=1, source_target_pairs={{0,10},{4,14},{10,0},{14,4},{2,8},{6,12},{8,2},{12,6},{3,13},{7,1}... | collective-permute-start | bytes 786440 | tf_op jit(solution)/shard_map/ppermute | solution.py:391
  58.3 0.4 other.5
  58.8 2.4 %collective-permute-start.5 = (bf16[256,512]{1,0:T(8,128)(2,1)S(1)}, bf16[256,512]{1,0:T(8,128)(2,1)S(1)}, u32[]{:S(2)}, u32[]{:S(2)}) collective-permute-start(bf16[256,512]{1,0:T(8,128)(2,1)S(1)} %get-tuple-element.16), channel_id=1, source_target_pairs={{0,4},{4,0},{10,14},{14,10},{2,6},{6,2},{8,12},{12,8},{3,7},{7,3},... | collective-permute-start | bytes 786440 | tf_op jit(solution)/shard_map/ppermute | solution.py:391
  61.6 11.3 %collective-permute-done.3.refs_0_ = bf16[256,512]{1,0:T(8,128)(2,1)S(1)} collective-permute-done((bf16[256,512]{1,0:T(8,128)(2,1)S(1)}, bf16[256,512]{1,0:T(8,128)(2,1)S(1)}, u32[]{:S(2)}, u32[]{:S(2)}) %collective-permute-start.3) | collective-permute-done | bytes 262176 | tf_op jit(solution)/shard_map/ppermute | solution.py:391
  72.8 5.7 %collective-permute-done.4.refs_1_ = bf16[256,512]{1,0:T(8,128)(2,1)S(1)} collective-permute-done((bf16[256,512]{1,0:T(8,128)(2,1)S(1)}, bf16[256,512]{1,0:T(8,128)(2,1)S(1)}, u32[]{:S(2)}, u32[]{:S(2)}) %collective-permute-start.4) | collective-permute-done | bytes 262176 | tf_op jit(solution)/shard_map/ppermute | solution.py:391
  78.5 0.3 collective-permute-done.5.refs_2_
  78.8 0.8 %sum.1 = bf16[256,512]{1,0:T(8,128)(2,1)} custom-call(f32[256,512]{1,0:T(8,128)S(1)} %other.3.own_ref, bf16[256,512]{1,0:T(8,128)(2,1)S(1)} %collective-permute-done.3.refs_0_, bf16[256,512]{1,0:T(8,128)(2,1)S(1)} %collective-permute-done.4.refs_1_, bf16[256,512]{1,0:T(8,128)(2,1)S(1)} %collective-permute-done.5.refs_2_), custom_call_target="tpu_custom_call" | custom-call | tf_op jit(solution)/shard_map/sum/pallas_call | solution.py:396
  (17 shorter events, 1.0 us)
Async XLA Ops:
  0.0 17.6 %copy-start = (f32[3,7,512]{2,1,0:T(8,128)S(1)}, f32[3,7,512]{2,1,0:T(8,128)}, u32[]{:S(2)}) copy-start(f32[3,7,512]{2,1,0:T(8,128)} %taps_ref.1) | copy-start | bytes 129028
  0.0 18.6 %copy-start.5 = (f32[512]{0:T(512)S(1)}, f32[512]{0:T(512)}, u32[]{:S(2)}) copy-start(f32[512]{0:T(512)} %param.10) | copy-start | bytes 6148
  4.1 49.7 %collective-permute-start.2 = (bf16[512,2048]{1,0:T(8,128)(2,1)}, bf16[512,2048]{1,0:T(8,128)(2,1)S(1)}, u32[]{:S(2)}, u32[]{:S(2)}) collective-permute-start(bf16[512,2048]{1,0:T(8,128)(2,1)} %get-tuple-element.14), channel_id=1, source_target_pairs={{0,2},{3,5},{2,0},{5,3},{4,6},{7,9},{6,4},{9,7},{8,10},{11,13},{10... | collective-permute-start | bytes 6291464 | tf_op jit(solution)/shard_map/ppermute | solution.py:328
  6.1 17.9 %all-to-all-start = ((bf16[16,32,640]{2,1,0:T(8,128)(2,1)}), bf16[16,32,640]{2,1,0:T(8,128)(2,1)S(1)}, u32[]{:S(2)}, u32[]{:S(2)}) async-start(bf16[16,32,640]{2,1,0:T(8,128)(2,1)} %get-tuple-element.11), calls=%async_computation | async-start | bytes 1310720 | tf_op jit(solution)/shard_map/all_to_all | solution.py:327
  14.3 6.7 %collective-permute-start = (bf16[16,512]{1,0:T(8,128)(2,1)S(1)}, bf16[16,512]{1,0:T(8,128)(2,1)S(1)}, u32[]{:S(2)}, u32[]{:S(2)}) collective-permute-start(bf16[16,512]{1,0:T(8,128)(2,1)S(1)} %slice_bitcast_fusion.1), channel_id=1, source_target_pairs={{0,16},{16,32},{32,48},{48,64},{64,80},{80,96},{96,112},{112,128},... | collective-permute-start | bytes 49160 | tf_op jit(solution)/shard_map/ppermute | solution.py:330
  21.0 0.6 copy-start.3
  21.6 0.8 %copy-start.1 = (f32[3,7,512]{2,1,0:T(8,128)S(1)}, f32[3,7,512]{2,1,0:T(8,128)}, u32[]{:S(2)}) copy-start(f32[3,7,512]{2,1,0:T(8,128)} %taps_ref.1) | copy-start | bytes 129028
  22.4 0.7 copy-start.4
  24.1 0.8 copy-start.2
  47.4 6.5 %collective-permute-start.1 = (bf16[256,512]{1,0:T(8,128)(2,1)S(1)}, bf16[256,512]{1,0:T(8,128)(2,1)S(1)}, u32[]{:S(2)}, u32[]{:S(2)}) collective-permute-start(bf16[256,512]{1,0:T(8,128)(2,1)S(1)} %mix.1.mixed_ref), channel_id=1, source_target_pairs={{0,2},{3,5},{2,0},{5,3},{4,6},{7,9},{6,4},{9,7},{8,10},{11,13},{10... | collective-permute-start | bytes 786440 | tf_op jit(solution)/shard_map/ppermute | solution.py:369
  54.1 18.7 %collective-permute-start.3 = (bf16[256,512]{1,0:T(8,128)(2,1)S(1)}, bf16[256,512]{1,0:T(8,128)(2,1)S(1)}, u32[]{:S(2)}, u32[]{:S(2)}) collective-permute-start(bf16[256,512]{1,0:T(8,128)(2,1)S(1)} %other.4), channel_id=1, source_target_pairs={{0,10},{4,14},{10,0},{14,4},{2,8},{6,12},{8,2},{12,6},{3,13},{7,1}... | collective-permute-start | bytes 786440 | tf_op jit(solution)/shard_map/ppermute | solution.py:391
  58.7 19.8 %collective-permute-start.4 = (bf16[256,512]{1,0:T(8,128)(2,1)S(1)}, bf16[256,512]{1,0:T(8,128)(2,1)S(1)}, u32[]{:S(2)}, u32[]{:S(2)}) collective-permute-start(bf16[256,512]{1,0:T(8,128)(2,1)S(1)} %get-tuple-element.15), channel_id=1, source_target_pairs={{0,14},{4,10},{10,4},{14,0},{2,12},{6,8},{8,6},{12,2},{3,1},{7,13}... | collective-permute-start | bytes 786440 | tf_op jit(solution)/shard_map/ppermute | solution.py:391
  58.8 20.0 %collective-permute-start.5 = (bf16[256,512]{1,0:T(8,128)(2,1)S(1)}, bf16[256,512]{1,0:T(8,128)(2,1)S(1)}, u32[]{:S(2)}, u32[]{:S(2)}) collective-permute-start(bf16[256,512]{1,0:T(8,128)(2,1)S(1)} %get-tuple-element.16), channel_id=1, source_target_pairs={{0,4},{4,0},{10,14},{14,10},{2,6},{6,2},{8,12},{12,8},{3,7},{7,3},... | collective-permute-start | bytes 786440 | tf_op jit(solution)/shard_map/ppermute | solution.py:391

commit v7 on v6

--- a/solution.py
+++ b/solution.py
@@ -115,10 +115,13 @@
         copy.wait()
 
 
-def query_kernel(now_ref, before_ref, taps_ref, out_ref, whole):
+def query_kernel(projected_hbm, before_ref, taps_ref, out_ref, now_ref, whole, sem):
     rows = out_ref.shape[0]
     halo = before_ref.shape[0]
+    copy = pltpu.make_async_copy(projected_hbm.at[0], now_ref, sem.at[0])
+    copy.start()
     whole[:halo] = before_ref[...].astype(F32)
+    copy.wait()
     whole[halo:] = now_ref[...].astype(F32)
     total = taps_ref[0, 0:1, :] * whole[halo:]
     for j in range(1, TAPS):
@@ -327,20 +330,24 @@
     recv = lax.all_to_all(send, "ctx", 0, 0, tiled=True)
     w_other = lax.ppermute(w_send, ("tp", "dp"), pair_route)
 
+    taps = jnp.concatenate([short_taps.reshape(3 * TAPS, width), skip_gain[None, :]], axis=0)
+    taps = lax.dynamic_slice_in_dim(taps, me_ctx * group, group, axis=1).T
     before = lax.ppermute(projected[0, rows - HALO :], "ctx", [(i, i + 1) for i in range(ctx - 1)])
+    taps, before = lax.optimization_barrier((taps, before))
     query = pl.pallas_call(
         query_kernel,
-        in_specs=[vmem] * 3,
+        in_specs=[hbm, vmem, vmem],
         out_specs=vmem,
         out_shape=jax.ShapeDtypeStruct((rows, width), F32),
-        scratch_shapes=[pltpu.VMEM((HALO + rows, width), F32)],
-        compiler_params=pltpu.CompilerParams(vmem_limit_bytes=48 * MIB),
+        scratch_shapes=[
+            pltpu.VMEM((rows, width), BF16),
+            pltpu.VMEM((HALO + rows, width), F32),
+            pltpu.SemaphoreType.DMA((1,)),
+        ],
+        compiler_params=pltpu.CompilerParams(vmem_limit_bytes=58 * MIB),
         name="query",
-    )(projected[0], before, short_taps)
-
-    taps = jnp.concatenate([short_taps.reshape(3 * TAPS, width), skip_gain[None, :]], axis=0)
-    taps = lax.dynamic_slice_in_dim(taps, me_ctx * group, group, axis=1).T
-    taps, query = lax.optimization_barrier((taps, query))
+    )(projected, before, short_taps)
+
     tables = lane_tables(rows)
     conv = pl.pallas_call(
         conv_kernel,
@@ -390,8 +397,8 @@
     def passed(block, step):
         return lax.ppermute(block, ("tp", "dp"), [(quad[i], quad[i ^ step]) for quad in quads for i in range(chunks)])
 
-    parts = [passed(block, step) for step, block in zip((2,), project((2,), BF16))]
-    parts += [passed(block, step) for step, block in zip((3, 1), project((3, 1), BF16))]
+    parts = [passed(block, step) for step, block in zip((3,), project((3,), BF16))]
+    parts += [passed(block, step) for step, block in zip((1, 2), project((1, 2), BF16))]
     (own,) = project((0,), F32)
     return pl.pallas_call(
         sum_kernel,

time: 80.2 us -> 79.8 us (level)
  the two profiles are of different devices: /device:TPU:8 before, /device:TPU:1 now
where the time goes in v7:
time: 79.8 us; the launch traced here: 78.5 us
  waiting for transfers between devices  32.6 us (41%)
  starting transfers between devices  25.3 us (32%)
  Pallas kernels  18.5 us (23%)
  local copies, waits for them, and re-layouts  1.87 us (2%)
    ppermute x3, waiting for transfers between devices, passed(): lax.ppermute(block, ('tp', 'dp'), [(quad[i], quad[i ^ step]) for quad in...  17.8 us
    all_to_all x1, starting transfers between devices, local(): recv = lax.all_to_all(send, 'ctx', 0, 0, tiled=True)  6.75 us
    ppermute x1, starting transfers between devices, local(): w_other = lax.ppermute(w_send, ('tp', 'dp'), pair_route)  6.49 us
    pallas_call x1, Pallas kernels, local(): pl.pallas_call(conv_kernel, in_specs=[vmem, vmem, vmem, hbm], out_specs=v...  6.25 us
    ppermute x3, starting transfers between devices, passed(): lax.ppermute(block, ('tp', 'dp'), [(quad[i], quad[i ^ step]) for quad in...  5.16 us
    all_to_all x1, waiting for transfers between devices, local(): recv = lax.all_to_all(send, 'ctx', 0, 0, tiled=True)  5.1 us
    all_to_all x1, waiting for transfers between devices, local(): conv = lax.all_to_all(conv, 'ctx', 0, 0, tiled=True)  4.49 us
    pallas_call x1, Pallas kernels, local(): pl.pallas_call(prep_kernel, in_specs=[smem, hbm, hbm, hbm, hbm], out_spec...  4.14 us
  transfers between devices with their start and end apart: 8, of which 7 were waited for; matrix products, arithmetic and copies ran while one was open for 1% of the time, Pallas kernels for 17%

profile of v7, /device:TPU:1, one launch (start us, length us, event | category | flops | bytes accessed | tf_op | source)
XLA Modules:
  0.0 78.5 jit_solution(18439265337769391889)
XLA Ops:
  0.0 4.1 %prep.1 = (bf16[16,32,640]{2,1,0:T(8,128)(2,1)}, bf16[512,2048]{1,0:T(8,128)(2,1)}) custom-call(s32[1]{0:T(128)} %bitcast.place_ref, bf16[3,256,512]{2,1,0:T(8,128)(2,1)} %projected_hbm.3, f32[256,512]{1,0:T(8,128)} %filter_hbm.1, f32[3,7,512]{2,1,0:T(8,128)} %taps_ref.1, bf16[512,4096]{1,0:T(8,128)(2,1)} %w_hbm.3), custom_call_target="tpu_custom_call" | custom-call | tf_op jit(solution)/shard_map/prep/pallas_call | solution.py:308
  4.2 6.5 %collective-permute-start.2 = (bf16[512,2048]{1,0:T(8,128)(2,1)}, bf16[512,2048]{1,0:T(8,128)(2,1)S(1)}, u32[]{:S(2)}, u32[]{:S(2)}) collective-permute-start(bf16[512,2048]{1,0:T(8,128)(2,1)} %get-tuple-element.14), channel_id=1, source_target_pairs={{0,2},{3,5},{2,0},{5,3},{4,6},{7,9},{6,4},{9,7},{8,10},{11,13},{10... | collective-permute-start | bytes 6291464 | tf_op jit(solution)/shard_map/ppermute | solution.py:331
  10.6 6.8 %all-to-all-start = ((bf16[16,32,640]{2,1,0:T(8,128)(2,1)}), bf16[16,32,640]{2,1,0:T(8,128)(2,1)S(1)}, u32[]{:S(2)}, u32[]{:S(2)}) async-start(bf16[16,32,640]{2,1,0:T(8,128)(2,1)} %get-tuple-element.11), calls=%async_computation | async-start | bytes 1310720 | tf_op jit(solution)/shard_map/all_to_all | solution.py:330
  17.4 0.7 slice_bitcast_fusion
  18.1 3.3 %collective-permute-start = (bf16[16,512]{1,0:T(8,128)(2,1)S(1)}, bf16[16,512]{1,0:T(8,128)(2,1)S(1)}, u32[]{:S(2)}, u32[]{:S(2)}) collective-permute-start(bf16[16,512]{1,0:T(8,128)(2,1)S(1)} %slice_bitcast_fusion), channel_id=1, source_target_pairs={{0,16},{16,32},{32,48},{48,64},{64,80},{80,96},{96,112},{112,128},... | collective-permute-start | bytes 49160 | tf_op jit(solution)/shard_map/ppermute | solution.py:335
  21.6 1.6 %collective-permute-done.before_ref = bf16[16,512]{1,0:T(8,128)(2,1)S(1)} collective-permute-done((bf16[16,512]{1,0:T(8,128)(2,1)S(1)}, bf16[16,512]{1,0:T(8,128)(2,1)S(1)}, u32[]{:S(2)}, u32[]{:S(2)}) %collective-permute-start) | collective-permute-done | bytes 16416 | tf_op jit(solution)/shard_map/ppermute | solution.py:335
  23.2 5.1 %all-to-all-done.recv_ref = bf16[16,32,640]{2,1,0:T(8,128)(2,1)S(1)} async-done(((bf16[16,32,640]{2,1,0:T(8,128)(2,1)}), bf16[16,32,640]{2,1,0:T(8,128)(2,1)S(1)}, u32[]{:S(2)}, u32[]{:S(2)}) %all-to-all-start) | async-done | bytes 655392 | tf_op jit(solution)/shard_map/all_to_all | solution.py:330
  28.3 6.3 %conv.1 = bf16[16,32,256]{2,1,0:T(8,128)(2,1)} custom-call(bf16[16,32,640]{2,1,0:T(8,128)(2,1)S(1)} %all-to-all-done.recv_ref, f32[32,22]{1,0:T(8,128)S(1)} %bitcast.5, f32[2,16,1,256]{3,2,1,0:T(1,128)S(1)} %copy-done.1, bf16[2048,512]{1,0:T(8,128)(2,1)} %constant.31.clone.tables_hbm), custom_call_target="tpu_custom_call" | custom-call | tf_op jit(solution)/shard_map/conv/pallas_call | solution.py:352
  34.6 3.5 %all-to-all-start.1 = ((bf16[16,32,256]{2,1,0:T(8,128)(2,1)}), bf16[16,32,256]{2,1,0:T(8,128)(2,1)S(1)}, u32[]{:S(2)}, u32[]{:S(2)}) async-start(bf16[16,32,256]{2,1,0:T(8,128)(2,1)} %conv.1), calls=%async_computation.1 | async-start | bytes 524288 | tf_op jit(solution)/shard_map/all_to_all | solution.py:369
  38.2 3.3 %query.1.query_ref = f32[256,512]{1,0:T(8,128)} custom-call(bf16[3,256,512]{2,1,0:T(8,128)(2,1)} %projected_hbm.3, bf16[16,512]{1,0:T(8,128)(2,1)} %copy-done.3, f32[3,7,512]{2,1,0:T(8,128)} %taps_ref.1), custom_call_target="tpu_custom_call" | custom-call | tf_op jit(solution)/shard_map/query/pallas_call | solution.py:337
  41.5 4.5 %all-to-all-done.1.conv_ref = bf16[16,32,256]{2,1,0:T(8,128)(2,1)S(1)} async-done(((bf16[16,32,256]{2,1,0:T(8,128)(2,1)}), bf16[16,32,256]{2,1,0:T(8,128)(2,1)S(1)}, u32[]{:S(2)}, u32[]{:S(2)}) %all-to-all-start.1) | async-done | bytes 262176 | tf_op jit(solution)/shard_map/all_to_all | solution.py:369
  46.0 1.0 %copy-done = f32[256,512]{1,0:T(8,128)S(1)} copy-done((f32[256,512]{1,0:T(8,128)S(1)}, f32[256,512]{1,0:T(8,128)}, u32[]{:S(2)}) %copy-start) | copy-done | bytes 524312
  47.0 0.1 mix.1.mixed_ref
  47.2 0.1 collective-permute-start.1
  47.3 2.8 %own.1.own_ref = f32[4,256,512]{2,1,0:T(8,128)S(1)} custom-call(s32[1]{0:T(128)} %bitcast.place_ref, bf16[256,512]{1,0:T(8,128)(2,1)S(1)} %mix.1.mixed_ref, bf16[512,4096]{1,0:T(8,128)(2,1)} %w_hbm.3), custom_call_target="tpu_custom_call" | custom-call | tf_op jit(solution)/shard_map/own/pallas_call | solution.py:377
  50.1 3.6 %collective-permute-done.1.mixed_ref = bf16[256,512]{1,0:T(8,128)(2,1)S(1)} collective-permute-done((bf16[256,512]{1,0:T(8,128)(2,1)S(1)}, bf16[256,512]{1,0:T(8,128)(2,1)S(1)}, u32[]{:S(2)}, u32[]{:S(2)}) %collective-permute-start.1) | collective-permute-done | bytes 262176 | tf_op jit(solution)/shard_map/ppermute | solution.py:376
  53.7 0.3 other.4
  54.1 0.5 other.5
  54.6 5.1 %collective-permute-start.4 = (bf16[256,512]{1,0:T(8,128)(2,1)S(1)}, bf16[256,512]{1,0:T(8,128)(2,1)S(1)}, u32[]{:S(2)}, u32[]{:S(2)}) collective-permute-start(bf16[256,512]{1,0:T(8,128)(2,1)S(1)} %get-tuple-element.15), channel_id=1, source_target_pairs={{0,4},{4,0},{10,14},{14,10},{2,6},{6,2},{8,12},{12,8},{3,7},{7,3},... | collective-permute-start | bytes 786440 | tf_op jit(solution)/shard_map/ppermute | solution.py:398
  59.6 0.3 other.3.own_ref
  59.9 2.5 %collective-permute-done.3.refs_0_ = bf16[256,512]{1,0:T(8,128)(2,1)S(1)} collective-permute-done((bf16[256,512]{1,0:T(8,128)(2,1)S(1)}, bf16[256,512]{1,0:T(8,128)(2,1)S(1)}, u32[]{:S(2)}, u32[]{:S(2)}) %collective-permute-start.3) | collective-permute-done | bytes 262176 | tf_op jit(solution)/shard_map/ppermute | solution.py:398
  62.5 12.4 %collective-permute-done.4.refs_1_ = bf16[256,512]{1,0:T(8,128)(2,1)S(1)} collective-permute-done((bf16[256,512]{1,0:T(8,128)(2,1)S(1)}, bf16[256,512]{1,0:T(8,128)(2,1)S(1)}, u32[]{:S(2)}, u32[]{:S(2)}) %collective-permute-start.4) | collective-permute-done | bytes 262176 | tf_op jit(solution)/shard_map/ppermute | solution.py:398
  74.8 2.9 %collective-permute-done.5.refs_2_ = bf16[256,512]{1,0:T(8,128)(2,1)S(1)} collective-permute-done((bf16[256,512]{1,0:T(8,128)(2,1)S(1)}, bf16[256,512]{1,0:T(8,128)(2,1)S(1)}, u32[]{:S(2)}, u32[]{:S(2)}) %collective-permute-start.5) | collective-permute-done | bytes 262176 | tf_op jit(solution)/shard_map/ppermute | solution.py:398
  77.7 0.8 %sum.1 = bf16[256,512]{1,0:T(8,128)(2,1)} custom-call(f32[256,512]{1,0:T(8,128)S(1)} %other.3.own_ref, bf16[256,512]{1,0:T(8,128)(2,1)S(1)} %collective-permute-done.3.refs_0_, bf16[256,512]{1,0:T(8,128)(2,1)S(1)} %collective-permute-done.4.refs_1_, bf16[256,512]{1,0:T(8,128)(2,1)S(1)} %collective-permute-done.5.refs_2_), custom_call_target="tpu_custom_call" | custom-call | tf_op jit(solution)/shard_map/sum/pallas_call | solution.py:403
  (15 shorter events, 0.3 us)
Async XLA Ops:
  0.0 21.4 %copy-start.2 = (f32[3,7,512]{2,1,0:T(8,128)S(1)}, f32[3,7,512]{2,1,0:T(8,128)}, u32[]{:S(2)}) copy-start(f32[3,7,512]{2,1,0:T(8,128)} %taps_ref.1) | copy-start | bytes 129028
  0.0 21.4 %copy-start.4 = (f32[512]{0:T(512)S(1)}, f32[512]{0:T(512)}, u32[]{:S(2)}) copy-start(f32[512]{0:T(512)} %param.10) | copy-start | bytes 6148
  0.0 28.3 %copy-start.1 = (f32[2,16,1,256]{3,2,1,0:T(1,128)S(1)}, f32[2,16,1,256]{3,2,1,0:T(1,128)}, u32[]{:S(2)}) copy-start(f32[2,16,1,256]{3,2,1,0:T(1,128)} %constant.30.clone.tw_ref) | copy-start | bytes 98308
  4.2 49.5 %collective-permute-start.2 = (bf16[512,2048]{1,0:T(8,128)(2,1)}, bf16[512,2048]{1,0:T(8,128)(2,1)S(1)}, u32[]{:S(2)}, u32[]{:S(2)}) collective-permute-start(bf16[512,2048]{1,0:T(8,128)(2,1)} %get-tuple-element.14), channel_id=1, source_target_pairs={{0,2},{3,5},{2,0},{5,3},{4,6},{7,9},{6,4},{9,7},{8,10},{11,13},{10... | collective-permute-start | bytes 6291464 | tf_op jit(solution)/shard_map/ppermute | solution.py:331
  10.6 17.7 %all-to-all-start = ((bf16[16,32,640]{2,1,0:T(8,128)(2,1)}), bf16[16,32,640]{2,1,0:T(8,128)(2,1)S(1)}, u32[]{:S(2)}, u32[]{:S(2)}) async-start(bf16[16,32,640]{2,1,0:T(8,128)(2,1)} %get-tuple-element.11), calls=%async_computation | async-start | bytes 1310720 | tf_op jit(solution)/shard_map/all_to_all | solution.py:330
  18.1 5.1 %collective-permute-start = (bf16[16,512]{1,0:T(8,128)(2,1)S(1)}, bf16[16,512]{1,0:T(8,128)(2,1)S(1)}, u32[]{:S(2)}, u32[]{:S(2)}) collective-permute-start(bf16[16,512]{1,0:T(8,128)(2,1)S(1)} %slice_bitcast_fusion), channel_id=1, source_target_pairs={{0,16},{16,32},{32,48},{48,64},{64,80},{80,96},{96,112},{112,128},... | collective-permute-start | bytes 49160 | tf_op jit(solution)/shard_map/ppermute | solution.py:335
  23.2 14.9 %copy-start.3 = (bf16[16,512]{1,0:T(8,128)(2,1)}, bf16[16,512]{1,0:T(8,128)(2,1)S(1)}, u32[]{:S(2)}) copy-start(bf16[16,512]{1,0:T(8,128)(2,1)S(1)} %collective-permute-done.before_ref) | copy-start | bytes 49156
  34.6 11.4 %all-to-all-start.1 = ((bf16[16,32,256]{2,1,0:T(8,128)(2,1)}), bf16[16,32,256]{2,1,0:T(8,128)(2,1)S(1)}, u32[]{:S(2)}, u32[]{:S(2)}) async-start(bf16[16,32,256]{2,1,0:T(8,128)(2,1)} %conv.1), calls=%async_computation.1 | async-start | bytes 524288 | tf_op jit(solution)/shard_map/all_to_all | solution.py:369
  46.0 1.0 %copy-start = (f32[256,512]{1,0:T(8,128)S(1)}, f32[256,512]{1,0:T(8,128)}, u32[]{:S(2)}) copy-start(f32[256,512]{1,0:T(8,128)} %query.1.query_ref) | copy-start | bytes 1572868
  47.2 6.5 %collective-permute-start.1 = (bf16[256,512]{1,0:T(8,128)(2,1)S(1)}, bf16[256,512]{1,0:T(8,128)(2,1)S(1)}, u32[]{:S(2)}, u32[]{:S(2)}) collective-permute-start(bf16[256,512]{1,0:T(8,128)(2,1)S(1)} %mix.1.mixed_ref), channel_id=1, source_target_pairs={{0,2},{3,5},{2,0},{5,3},{4,6},{7,9},{6,4},{9,7},{8,10},{11,13},{10... | collective-permute-start | bytes 786440 | tf_op jit(solution)/shard_map/ppermute | solution.py:376
  54.0 8.5 %collective-permute-start.3 = (bf16[256,512]{1,0:T(8,128)(2,1)S(1)}, bf16[256,512]{1,0:T(8,128)(2,1)S(1)}, u32[]{:S(2)}, u32[]{:S(2)}) collective-permute-start(bf16[256,512]{1,0:T(8,128)(2,1)S(1)} %other.4), channel_id=1, source_target_pairs={{0,14},{4,10},{10,4},{14,0},{2,12},{6,8},{8,6},{12,2},{3,1},{7,13}... | collective-permute-start | bytes 786440 | tf_op jit(solution)/shard_map/ppermute | solution.py:398
  54.6 20.3 %collective-permute-start.4 = (bf16[256,512]{1,0:T(8,128)(2,1)S(1)}, bf16[256,512]{1,0:T(8,128)(2,1)S(1)}, u32[]{:S(2)}, u32[]{:S(2)}) collective-permute-start(bf16[256,512]{1,0:T(8,128)(2,1)S(1)} %get-tuple-element.15), channel_id=1, source_target_pairs={{0,4},{4,0},{10,14},{14,10},{2,6},{6,2},{8,12},{12,8},{3,7},{7,3},... | collective-permute-start | bytes 786440 | tf_op jit(solution)/shard_map/ppermute | solution.py:398
  59.6 18.1 %collective-permute-start.5 = (bf16[256,512]{1,0:T(8,128)(2,1)S(1)}, bf16[256,512]{1,0:T(8,128)(2,1)S(1)}, u32[]{:S(2)}, u32[]{:S(2)}) collective-permute-start(bf16[256,512]{1,0:T(8,128)(2,1)S(1)} %get-tuple-element.16), channel_id=1, source_target_pairs={{0,10},{4,14},{10,0},{14,4},{2,8},{6,12},{8,2},{12,6},{3,13},{7,1}... | collective-permute-start | bytes 786440 | tf_op jit(solution)/shard_map/ppermute | solution.py:398

commit v8 on v4

--- a/solution.py
+++ b/solution.py
@@ -236,12 +236,13 @@
 def own_kernel(place_ref, mixed_ref, w_hbm, out_ref, own, sems):
     width = w_hbm.shape[0]
     index = place_ref[0] // 4
-    copies = []
-    for step in range(own.shape[0]):
+    order = list(reversed(range(own.shape[0])))
+    copies = {}
+    for step in order:
         start = column_start(place_ref, index ^ step, w_hbm)
-        copies.append(pltpu.make_async_copy(w_hbm.at[:, pl.ds(start, width)], own.at[step], sems.at[step]))
+        copies[step] = pltpu.make_async_copy(w_hbm.at[:, pl.ds(start, width)], own.at[step], sems.at[step])
         copies[step].start()
-    for step in reversed(range(own.shape[0])):
+    for step in order:
         copies[step].wait()
         out_ref[step] = dot(mixed_ref[...], own[step])
 

time: 80 us -> 80 us (level)
  no operation moved by 1% of the time
where the time goes in v8:
time: 80 us; the launch traced here: 79.6 us
  waiting for transfers between devices  28.9 us (36%)
  starting transfers between devices  20.6 us (26%)
  Pallas kernels  14.1 us (18%)
  blocking collectives  12.3 us (15%)
  local copies, waits for them, and re-layouts  3.46 us (4%)
    ppermute x3, waiting for transfers between devices, passed(): lax.ppermute(block, ('tp', 'dp'), [(quad[i], quad[i ^ step]) for quad in...  18.8 us
    all_to_all x1, blocking collectives, local(): conv = lax.all_to_all(conv, 'ctx', 0, 0, tiled=True)  12.3 us
    ppermute x3, starting transfers between devices, passed(): lax.ppermute(block, ('tp', 'dp'), [(quad[i], quad[i ^ step]) for quad in...  6.67 us
    pallas_call x1, Pallas kernels, local(): pl.pallas_call(conv_kernel, in_specs=[vmem, vmem, vmem, hbm], out_specs=v...  6.19 us
    all_to_all x1, starting transfers between devices, local(): recv = lax.all_to_all(send, 'ctx', 0, 0, tiled=True)  5.3 us
    ppermute x1, waiting for transfers between devices, local(): lax.ppermute(projected[0, rows - HALO:], 'ctx', [(i, i + 1) for i in rang...  4.15 us
    all_to_all x1, waiting for transfers between devices, local(): recv = lax.all_to_all(send, 'ctx', 0, 0, tiled=True)  3.87 us
    ppermute x1, starting transfers between devices, local(): lax.ppermute(projected[0, rows - HALO:], 'ctx', [(i, i + 1) for i in rang...  3.81 us
  transfers between devices with their start and end apart: 7, of which 6 were waited for; matrix products, arithmetic and copies ran while one was open for 3% of the time, Pallas kernels for 13%

profile of v8, /device:TPU:32, one launch (start us, length us, event | category | flops | bytes accessed | tf_op | source)
XLA Modules:
  0.0 79.6 jit_solution(6239158795991929438)
XLA Ops:
  0.0 2.9 %prep.1 = (bf16[16,96,256]{2,1,0:T(8,128)(2,1)}, bf16[512,2048]{1,0:T(8,128)(2,1)}) custom-call(s32[1]{0:T(128)} %bitcast.place_ref, bf16[3,256,512]{2,1,0:T(8,128)(2,1)} %projected_hbm.1, f32[256,512]{1,0:T(8,128)} %filter_hbm.1, bf16[512,4096]{1,0:T(8,128)(2,1)} %w_hbm.3), custom_call_target="tpu_custom_call" | custom-call | tf_op jit(solution)/shard_map/prep/pallas_call | solution.py:288
  2.9 1.9 %collective-permute-start.2 = (bf16[512,2048]{1,0:T(8,128)(2,1)}, bf16[512,2048]{1,0:T(8,128)(2,1)S(1)}, u32[]{:S(2)}, u32[]{:S(2)}) collective-permute-start(bf16[512,2048]{1,0:T(8,128)(2,1)} %get-tuple-element.14), channel_id=1, source_target_pairs={{0,2},{3,5},{2,0},{5,3},{4,6},{7,9},{6,4},{9,7},{8,10},{11,13},{10... | collective-permute-start | bytes 6291464 | tf_op jit(solution)/shard_map/ppermute | solution.py:308
  4.8 5.3 %all-to-all-start = ((bf16[16,96,256]{2,1,0:T(8,128)(2,1)}), bf16[16,96,256]{2,1,0:T(8,128)(2,1)S(1)}, u32[]{:S(2)}, u32[]{:S(2)}) async-start(bf16[16,96,256]{2,1,0:T(8,128)(2,1)} %get-tuple-element.11), calls=%async_computation | async-start | bytes 1572864 | tf_op jit(solution)/shard_map/all_to_all | solution.py:307
  10.1 0.7 slice_bitcast_fusion.1
  10.9 3.8 %collective-permute-start = (bf16[16,512]{1,0:T(8,128)(2,1)S(1)}, bf16[16,512]{1,0:T(8,128)(2,1)S(1)}, u32[]{:S(2)}, u32[]{:S(2)}) collective-permute-start(bf16[16,512]{1,0:T(8,128)(2,1)S(1)} %slice_bitcast_fusion.1), channel_id=1, source_target_pairs={{0,16},{16,32},{32,48},{48,64},{64,80},{80,96},{96,112},{112,128},... | collective-permute-start | bytes 49160 | tf_op jit(solution)/shard_map/ppermute | solution.py:310
  14.7 1.7 %slice_bitcast_fusion.now_ref = bf16[256,512]{1,0:T(8,128)(2,1)} fusion(bf16[3,256,512]{2,1,0:T(8,128)(2,1)} %projected_hbm.1), kind=kLoop, calls=%fused_computation | loop fusion | bytes 524288 | tf_op jit(solution)/shard_map/squeeze | solution.py:319
  16.5 4.2 %collective-permute-done.before_ref = bf16[16,512]{1,0:T(8,128)(2,1)S(1)} collective-permute-done((bf16[16,512]{1,0:T(8,128)(2,1)S(1)}, bf16[16,512]{1,0:T(8,128)(2,1)S(1)}, u32[]{:S(2)}, u32[]{:S(2)}) %collective-permute-start) | collective-permute-done | bytes 16416 | tf_op jit(solution)/shard_map/ppermute | solution.py:310
  20.7 0.9 %copy-done = bf16[256,512]{1,0:T(8,128)(2,1)S(1)} copy-done((bf16[256,512]{1,0:T(8,128)(2,1)S(1)}, bf16[256,512]{1,0:T(8,128)(2,1)}, u32[]{:S(2)}) %copy-start) | copy-done | bytes 262168
  21.6 0.7 query.1.query_ref
  22.4 3.9 %all-to-all-done.recv_ref = bf16[16,96,256]{2,1,0:T(8,128)(2,1)S(1)} async-done(((bf16[16,96,256]{2,1,0:T(8,128)(2,1)}), bf16[16,96,256]{2,1,0:T(8,128)(2,1)S(1)}, u32[]{:S(2)}, u32[]{:S(2)}) %all-to-all-start) | async-done | bytes 786464 | tf_op jit(solution)/shard_map/all_to_all | solution.py:307
  26.3 6.2 %conv.1 = bf16[16,32,256]{2,1,0:T(8,128)(2,1)S(1)} custom-call(bf16[16,96,256]{2,1,0:T(8,128)(2,1)S(1)} %all-to-all-done.recv_ref, f32[32,22]{1,0:T(8,128)S(1)} %bitcast.7, f32[2,16,1,256]{3,2,1,0:T(1,128)S(1)} %copy-done.2, bf16[2048,512]{1,0:T(8,128)(2,1)} %constant.31.clone.tables_hbm), custom_call_target="tpu_custom_call" | custom-call | tf_op jit(solution)/shard_map/conv/pallas_call | solution.py:325
  32.5 12.3 %all_to_all.10.conv_ref = bf16[16,32,256]{2,1,0:T(8,128)(2,1)S(1)} all-to-all(bf16[16,32,256]{2,1,0:T(8,128)(2,1)S(1)} %conv.1), channel_id=1, replica_groups=mesh['ctx'=16,'tp'=8,'dp'=2] {'ctx'}, dimensions={0} | all-to-all | bytes 524288 | tf_op jit(solution)/shard_map/all_to_all | solution.py:342
  44.9 2.9 %collective-permute-start.1 = (bf16[256,512]{1,0:T(8,128)(2,1)S(1)}, bf16[256,512]{1,0:T(8,128)(2,1)S(1)}, u32[]{:S(2)}, u32[]{:S(2)}) collective-permute-start(bf16[256,512]{1,0:T(8,128)(2,1)S(1)} %mix.1.mixed_ref), channel_id=1, source_target_pairs={{0,2},{3,5},{2,0},{5,3},{4,6},{7,9},{6,4},{9,7},{8,10},{11,13},{10... | collective-permute-start | bytes 786440 | tf_op jit(solution)/shard_map/ppermute | solution.py:349
  47.9 2.3 %own.1.own_ref = f32[4,256,512]{2,1,0:T(8,128)S(1)} custom-call(s32[1]{0:T(128)} %bitcast.place_ref, bf16[256,512]{1,0:T(8,128)(2,1)S(1)} %mix.1.mixed_ref, bf16[512,4096]{1,0:T(8,128)(2,1)} %w_hbm.3), custom_call_target="tpu_custom_call" | custom-call | tf_op jit(solution)/shard_map/own/pallas_call | solution.py:350
  50.1 2.1 %collective-permute-done.1.mixed_ref = bf16[256,512]{1,0:T(8,128)(2,1)S(1)} collective-permute-done((bf16[256,512]{1,0:T(8,128)(2,1)S(1)}, bf16[256,512]{1,0:T(8,128)(2,1)S(1)}, u32[]{:S(2)}, u32[]{:S(2)}) %collective-permute-start.1) | collective-permute-done | bytes 262176 | tf_op jit(solution)/shard_map/ppermute | solution.py:349
  52.2 0.3 other.4
  52.5 4.5 %collective-permute-start.3 = (bf16[256,512]{1,0:T(8,128)(2,1)S(1)}, bf16[256,512]{1,0:T(8,128)(2,1)S(1)}, u32[]{:S(2)}, u32[]{:S(2)}) collective-permute-start(bf16[256,512]{1,0:T(8,128)(2,1)S(1)} %other.4), channel_id=1, source_target_pairs={{0,14},{4,10},{10,4},{14,0},{2,12},{6,8},{8,6},{12,2},{3,1},{7,13}... | collective-permute-start | bytes 786440 | tf_op jit(solution)/shard_map/ppermute | solution.py:371
  57.0 0.4 other.5
  57.5 0.4 collective-permute-start.4
  57.8 1.8 %collective-permute-start.5 = (bf16[256,512]{1,0:T(8,128)(2,1)S(1)}, bf16[256,512]{1,0:T(8,128)(2,1)S(1)}, u32[]{:S(2)}, u32[]{:S(2)}) collective-permute-start(bf16[256,512]{1,0:T(8,128)(2,1)S(1)} %get-tuple-element.16), channel_id=1, source_target_pairs={{0,10},{4,14},{10,0},{14,4},{2,8},{6,12},{8,2},{12,6},{3,13},{7,1}... | collective-permute-start | bytes 786440 | tf_op jit(solution)/shard_map/ppermute | solution.py:371
  59.9 11.9 %collective-permute-done.3.refs_0_ = bf16[256,512]{1,0:T(8,128)(2,1)S(1)} collective-permute-done((bf16[256,512]{1,0:T(8,128)(2,1)S(1)}, bf16[256,512]{1,0:T(8,128)(2,1)S(1)}, u32[]{:S(2)}, u32[]{:S(2)}) %collective-permute-start.3) | collective-permute-done | bytes 262176 | tf_op jit(solution)/shard_map/ppermute | solution.py:371
  71.9 2.3 %collective-permute-done.4.refs_1_ = bf16[256,512]{1,0:T(8,128)(2,1)S(1)} collective-permute-done((bf16[256,512]{1,0:T(8,128)(2,1)S(1)}, bf16[256,512]{1,0:T(8,128)(2,1)S(1)}, u32[]{:S(2)}, u32[]{:S(2)}) %collective-permute-start.4) | collective-permute-done | bytes 262176 | tf_op jit(solution)/shard_map/ppermute | solution.py:371
  74.2 4.6 %collective-permute-done.5.refs_2_ = bf16[256,512]{1,0:T(8,128)(2,1)S(1)} collective-permute-done((bf16[256,512]{1,0:T(8,128)(2,1)S(1)}, bf16[256,512]{1,0:T(8,128)(2,1)S(1)}, u32[]{:S(2)}, u32[]{:S(2)}) %collective-permute-start.5) | collective-permute-done | bytes 262176 | tf_op jit(solution)/shard_map/ppermute | solution.py:371
  78.7 0.8 %sum.1 = bf16[256,512]{1,0:T(8,128)(2,1)} custom-call(f32[256,512]{1,0:T(8,128)S(1)} %other.3.own_ref, bf16[256,512]{1,0:T(8,128)(2,1)S(1)} %collective-permute-done.3.refs_0_, bf16[256,512]{1,0:T(8,128)(2,1)S(1)} %collective-permute-done.4.refs_1_, bf16[256,512]{1,0:T(8,128)(2,1)S(1)} %collective-permute-done.5.refs_2_), custom_call_target="tpu_custom_call" | custom-call | tf_op jit(solution)/shard_map/sum/pallas_call | solution.py:376
  (13 shorter events, 0.6 us)
Async XLA Ops:
  0.0 14.7 %copy-start.1 = (f32[3,7,512]{2,1,0:T(8,128)S(1)}, f32[3,7,512]{2,1,0:T(8,128)}, u32[]{:S(2)}) copy-start(f32[3,7,512]{2,1,0:T(8,128)} %taps_ref.1) | copy-start | bytes 129028
  2.9 13.5 %copy-start.3 = (f32[512]{0:T(512)S(1)}, f32[512]{0:T(512)}, u32[]{:S(2)}) copy-start(f32[512]{0:T(512)} %param.10) | copy-start | bytes 6148
  2.9 23.4 %copy-start.2 = (f32[2,16,1,256]{3,2,1,0:T(1,128)S(1)}, f32[2,16,1,256]{3,2,1,0:T(1,128)}, u32[]{:S(2)}) copy-start(f32[2,16,1,256]{3,2,1,0:T(1,128)} %constant.30.clone.tw_ref) | copy-start | bytes 98308
  2.9 49.3 %collective-permute-start.2 = (bf16[512,2048]{1,0:T(8,128)(2,1)}, bf16[512,2048]{1,0:T(8,128)(2,1)S(1)}, u32[]{:S(2)}, u32[]{:S(2)}) collective-permute-start(bf16[512,2048]{1,0:T(8,128)(2,1)} %get-tuple-element.14), channel_id=1, source_target_pairs={{0,2},{3,5},{2,0},{5,3},{4,6},{7,9},{6,4},{9,7},{8,10},{11,13},{10... | collective-permute-start | bytes 6291464 | tf_op jit(solution)/shard_map/ppermute | solution.py:308
  4.8 21.5 %all-to-all-start = ((bf16[16,96,256]{2,1,0:T(8,128)(2,1)}), bf16[16,96,256]{2,1,0:T(8,128)(2,1)S(1)}, u32[]{:S(2)}, u32[]{:S(2)}) async-start(bf16[16,96,256]{2,1,0:T(8,128)(2,1)} %get-tuple-element.11), calls=%async_computation | async-start | bytes 1572864 | tf_op jit(solution)/shard_map/all_to_all | solution.py:307
  10.9 9.8 %collective-permute-start = (bf16[16,512]{1,0:T(8,128)(2,1)S(1)}, bf16[16,512]{1,0:T(8,128)(2,1)S(1)}, u32[]{:S(2)}, u32[]{:S(2)}) collective-permute-start(bf16[16,512]{1,0:T(8,128)(2,1)S(1)} %slice_bitcast_fusion.1), channel_id=1, source_target_pairs={{0,16},{16,32},{32,48},{48,64},{64,80},{80,96},{96,112},{112,128},... | collective-permute-start | bytes 49160 | tf_op jit(solution)/shard_map/ppermute | solution.py:310
  20.7 0.9 %copy-start = (bf16[256,512]{1,0:T(8,128)(2,1)S(1)}, bf16[256,512]{1,0:T(8,128)(2,1)}, u32[]{:S(2)}) copy-start(bf16[256,512]{1,0:T(8,128)(2,1)} %slice_bitcast_fusion.now_ref) | copy-start | bytes 786436
  44.9 7.3 %collective-permute-start.1 = (bf16[256,512]{1,0:T(8,128)(2,1)S(1)}, bf16[256,512]{1,0:T(8,128)(2,1)S(1)}, u32[]{:S(2)}, u32[]{:S(2)}) collective-permute-start(bf16[256,512]{1,0:T(8,128)(2,1)S(1)} %mix.1.mixed_ref), channel_id=1, source_target_pairs={{0,2},{3,5},{2,0},{5,3},{4,6},{7,9},{6,4},{9,7},{8,10},{11,13},{10... | collective-permute-start | bytes 786440 | tf_op jit(solution)/shard_map/ppermute | solution.py:349
  52.5 19.4 %collective-permute-start.3 = (bf16[256,512]{1,0:T(8,128)(2,1)S(1)}, bf16[256,512]{1,0:T(8,128)(2,1)S(1)}, u32[]{:S(2)}, u32[]{:S(2)}) collective-permute-start(bf16[256,512]{1,0:T(8,128)(2,1)S(1)} %other.4), channel_id=1, source_target_pairs={{0,14},{4,10},{10,4},{14,0},{2,12},{6,8},{8,6},{12,2},{3,1},{7,13}... | collective-permute-start | bytes 786440 | tf_op jit(solution)/shard_map/ppermute | solution.py:371
  57.5 16.7 %collective-permute-start.4 = (bf16[256,512]{1,0:T(8,128)(2,1)S(1)}, bf16[256,512]{1,0:T(8,128)(2,1)S(1)}, u32[]{:S(2)}, u32[]{:S(2)}) collective-permute-start(bf16[256,512]{1,0:T(8,128)(2,1)S(1)} %get-tuple-element.15), channel_id=1, source_target_pairs={{0,4},{4,0},{10,14},{14,10},{2,6},{6,2},{8,12},{12,8},{3,7},{7,3},... | collective-permute-start | bytes 786440 | tf_op jit(solution)/shard_map/ppermute | solution.py:371
  57.8 20.9 %collective-permute-start.5 = (bf16[256,512]{1,0:T(8,128)(2,1)S(1)}, bf16[256,512]{1,0:T(8,128)(2,1)S(1)}, u32[]{:S(2)}, u32[]{:S(2)}) collective-permute-start(bf16[256,512]{1,0:T(8,128)(2,1)S(1)} %get-tuple-element.16), channel_id=1, source_target_pairs={{0,10},{4,14},{10,0},{14,4},{2,8},{6,12},{8,2},{12,6},{3,13},{7,1}... | collective-permute-start | bytes 786440 | tf_op jit(solution)/shard_map/ppermute | solution.py:371

commit v9 on v8

--- a/solution.py
+++ b/solution.py
@@ -370,8 +370,7 @@
     def passed(block, step):
         return lax.ppermute(block, ("tp", "dp"), [(quad[i], quad[i ^ step]) for quad in quads for i in range(chunks)])
 
-    parts = [passed(block, step) for step, block in zip((3,), project((3,), BF16))]
-    parts += [passed(block, step) for step, block in zip((1, 2), project((1, 2), BF16))]
+    parts = [passed(block, step) for step, block in zip((3, 1, 2), project((3, 1, 2), BF16))]
     (own,) = project((0,), F32)
     return pl.pallas_call(
         sum_kernel,

time: 80 us -> 79.7 us (level)
  transfers between devices with their start and end apart: 7 -> 7, of which waited for: 6 -> 5; matrix products, arithmetic and copies ran while one was open for 3% -> 3% of each run, Pallas kernels for 13% -> 12%
where the time goes in v9:
time: 79.7 us; the launch traced here: 79.3 us
  waiting for transfers between devices  28.9 us (36%)
  starting transfers between devices  20.6 us (26%)
  Pallas kernels  13.9 us (17%)
  blocking collectives  12.3 us (15%)
  local copies, waits for them, and re-layouts  3.46 us (4%)
    ppermute x3, waiting for transfers between devices, passed(): lax.ppermute(block, ('tp', 'dp'), [(quad[i], quad[i ^ step]) for quad in...  18.8 us
    all_to_all x1, blocking collectives, local(): conv = lax.all_to_all(conv, 'ctx', 0, 0, tiled=True)  12.3 us
    ppermute x3, starting transfers between devices, passed(): lax.ppermute(block, ('tp', 'dp'), [(quad[i], quad[i ^ step]) for quad in...  6.58 us
    pallas_call x1, Pallas kernels, local(): pl.pallas_call(conv_kernel, in_specs=[vmem, vmem, vmem, hbm], out_specs=v...  6.19 us
    all_to_all x1, starting transfers between devices, local(): recv = lax.all_to_all(send, 'ctx', 0, 0, tiled=True)  5.3 us
    ppermute x1, waiting for transfers between devices, local(): lax.ppermute(projected[0, rows - HALO:], 'ctx', [(i, i + 1) for i in rang...  4.15 us
    all_to_all x1, waiting for transfers between devices, local(): recv = lax.all_to_all(send, 'ctx', 0, 0, tiled=True)  3.87 us
    ppermute x1, starting transfers between devices, local(): lax.ppermute(projected[0, rows - HALO:], 'ctx', [(i, i + 1) for i in rang...  3.81 us
  transfers between devices with their start and end apart: 7, of which 5 were waited for; matrix products, arithmetic and copies ran while one was open for 3% of the time, Pallas kernels for 12%

profile of v9, /device:TPU:32, one launch (start us, length us, event | category | flops | bytes accessed | tf_op | source)
XLA Modules:
  0.0 79.3 jit_solution(13297620590960231214)
XLA Ops:
  0.0 2.9 %prep.1 = (bf16[16,96,256]{2,1,0:T(8,128)(2,1)}, bf16[512,2048]{1,0:T(8,128)(2,1)}) custom-call(s32[1]{0:T(128)} %bitcast.place_ref, bf16[3,256,512]{2,1,0:T(8,128)(2,1)} %projected_hbm.1, f32[256,512]{1,0:T(8,128)} %filter_hbm.1, bf16[512,4096]{1,0:T(8,128)(2,1)} %w_hbm.3), custom_call_target="tpu_custom_call" | custom-call | tf_op jit(solution)/shard_map/prep/pallas_call | solution.py:288
  2.9 1.9 %collective-permute-start.2 = (bf16[512,2048]{1,0:T(8,128)(2,1)}, bf16[512,2048]{1,0:T(8,128)(2,1)S(1)}, u32[]{:S(2)}, u32[]{:S(2)}) collective-permute-start(bf16[512,2048]{1,0:T(8,128)(2,1)} %get-tuple-element.15), channel_id=1, source_target_pairs={{0,2},{3,5},{2,0},{5,3},{4,6},{7,9},{6,4},{9,7},{8,10},{11,13},{10... | collective-permute-start | bytes 6291464 | tf_op jit(solution)/shard_map/ppermute | solution.py:308
  4.8 5.3 %all-to-all-start = ((bf16[16,96,256]{2,1,0:T(8,128)(2,1)}), bf16[16,96,256]{2,1,0:T(8,128)(2,1)S(1)}, u32[]{:S(2)}, u32[]{:S(2)}) async-start(bf16[16,96,256]{2,1,0:T(8,128)(2,1)} %get-tuple-element.12), calls=%async_computation | async-start | bytes 1572864 | tf_op jit(solution)/shard_map/all_to_all | solution.py:307
  10.1 0.7 slice_bitcast_fusion.1
  10.9 3.8 %collective-permute-start = (bf16[16,512]{1,0:T(8,128)(2,1)S(1)}, bf16[16,512]{1,0:T(8,128)(2,1)S(1)}, u32[]{:S(2)}, u32[]{:S(2)}) collective-permute-start(bf16[16,512]{1,0:T(8,128)(2,1)S(1)} %slice_bitcast_fusion.1), channel_id=1, source_target_pairs={{0,16},{16,32},{32,48},{48,64},{64,80},{80,96},{96,112},{112,128},... | collective-permute-start | bytes 49160 | tf_op jit(solution)/shard_map/ppermute | solution.py:310
  14.7 1.7 %slice_bitcast_fusion.now_ref = bf16[256,512]{1,0:T(8,128)(2,1)} fusion(bf16[3,256,512]{2,1,0:T(8,128)(2,1)} %projected_hbm.1), kind=kLoop, calls=%fused_computation | loop fusion | bytes 524288 | tf_op jit(solution)/shard_map/squeeze | solution.py:319
  16.5 4.2 %collective-permute-done.before_ref = bf16[16,512]{1,0:T(8,128)(2,1)S(1)} collective-permute-done((bf16[16,512]{1,0:T(8,128)(2,1)S(1)}, bf16[16,512]{1,0:T(8,128)(2,1)S(1)}, u32[]{:S(2)}, u32[]{:S(2)}) %collective-permute-start) | collective-permute-done | bytes 16416 | tf_op jit(solution)/shard_map/ppermute | solution.py:310
  20.7 0.9 %copy-done = bf16[256,512]{1,0:T(8,128)(2,1)S(1)} copy-done((bf16[256,512]{1,0:T(8,128)(2,1)S(1)}, bf16[256,512]{1,0:T(8,128)(2,1)}, u32[]{:S(2)}) %copy-start) | copy-done | bytes 262168
  21.6 0.7 query.1.query_ref
  22.4 3.9 %all-to-all-done.recv_ref = bf16[16,96,256]{2,1,0:T(8,128)(2,1)S(1)} async-done(((bf16[16,96,256]{2,1,0:T(8,128)(2,1)}), bf16[16,96,256]{2,1,0:T(8,128)(2,1)S(1)}, u32[]{:S(2)}, u32[]{:S(2)}) %all-to-all-start) | async-done | bytes 786464 | tf_op jit(solution)/shard_map/all_to_all | solution.py:307
  26.3 6.2 %conv.1 = bf16[16,32,256]{2,1,0:T(8,128)(2,1)S(1)} custom-call(bf16[16,96,256]{2,1,0:T(8,128)(2,1)S(1)} %all-to-all-done.recv_ref, f32[32,22]{1,0:T(8,128)S(1)} %bitcast.7, f32[2,16,1,256]{3,2,1,0:T(1,128)S(1)} %copy-done.2, bf16[2048,512]{1,0:T(8,128)(2,1)} %constant.31.clone.tables_hbm), custom_call_target="tpu_custom_call" | custom-call | tf_op jit(solution)/shard_map/conv/pallas_call | solution.py:325
  32.5 12.3 %all_to_all.10.conv_ref = bf16[16,32,256]{2,1,0:T(8,128)(2,1)S(1)} all-to-all(bf16[16,32,256]{2,1,0:T(8,128)(2,1)S(1)} %conv.1), channel_id=1, replica_groups=mesh['ctx'=16,'tp'=8,'dp'=2] {'ctx'}, dimensions={0} | all-to-all | bytes 524288 | tf_op jit(solution)/shard_map/all_to_all | solution.py:342
  44.8 0.1 mix.1.mixed_ref
  44.9 2.9 %collective-permute-start.1 = (bf16[256,512]{1,0:T(8,128)(2,1)S(1)}, bf16[256,512]{1,0:T(8,128)(2,1)S(1)}, u32[]{:S(2)}, u32[]{:S(2)}) collective-permute-start(bf16[256,512]{1,0:T(8,128)(2,1)S(1)} %mix.1.mixed_ref), channel_id=1, source_target_pairs={{0,2},{3,5},{2,0},{5,3},{4,6},{7,9},{6,4},{9,7},{8,10},{11,13},{10... | collective-permute-start | bytes 786440 | tf_op jit(solution)/shard_map/ppermute | solution.py:349
  47.9 2.3 %own.1.own_ref = f32[4,256,512]{2,1,0:T(8,128)S(1)} custom-call(s32[1]{0:T(128)} %bitcast.place_ref, bf16[256,512]{1,0:T(8,128)(2,1)S(1)} %mix.1.mixed_ref, bf16[512,4096]{1,0:T(8,128)(2,1)} %w_hbm.3), custom_call_target="tpu_custom_call" | custom-call | tf_op jit(solution)/shard_map/own/pallas_call | solution.py:350
  50.1 2.1 %collective-permute-done.1.mixed_ref = bf16[256,512]{1,0:T(8,128)(2,1)S(1)} collective-permute-done((bf16[256,512]{1,0:T(8,128)(2,1)S(1)}, bf16[256,512]{1,0:T(8,128)(2,1)S(1)}, u32[]{:S(2)}, u32[]{:S(2)}) %collective-permute-start.1) | collective-permute-done | bytes 262176 | tf_op jit(solution)/shard_map/ppermute | solution.py:349
  52.2 0.6 other.3
  52.8 4.5 %collective-permute-start.3 = (bf16[256,512]{1,0:T(8,128)(2,1)S(1)}, bf16[256,512]{1,0:T(8,128)(2,1)S(1)}, u32[]{:S(2)}, u32[]{:S(2)}) collective-permute-start(bf16[256,512]{1,0:T(8,128)(2,1)S(1)} %get-tuple-element.16), channel_id=1, source_target_pairs={{0,14},{4,10},{10,4},{14,0},{2,12},{6,8},{8,6},{12,2},{3,1},{7,13}... | collective-permute-start | bytes 786440 | tf_op jit(solution)/shard_map/ppermute | solution.py:371
  57.3 0.3 collective-permute-start.4
  57.6 1.8 %collective-permute-start.5 = (bf16[256,512]{1,0:T(8,128)(2,1)S(1)}, bf16[256,512]{1,0:T(8,128)(2,1)S(1)}, u32[]{:S(2)}, u32[]{:S(2)}) collective-permute-start(bf16[256,512]{1,0:T(8,128)(2,1)S(1)} %get-tuple-element.18), channel_id=1, source_target_pairs={{0,10},{4,14},{10,0},{14,4},{2,8},{6,12},{8,2},{12,6},{3,13},{7,1}... | collective-permute-start | bytes 786440 | tf_op jit(solution)/shard_map/ppermute | solution.py:371
  59.4 0.3 other.2.own_ref
  59.7 13.6 %collective-permute-done.3.refs_0_ = bf16[256,512]{1,0:T(8,128)(2,1)S(1)} collective-permute-done((bf16[256,512]{1,0:T(8,128)(2,1)S(1)}, bf16[256,512]{1,0:T(8,128)(2,1)S(1)}, u32[]{:S(2)}, u32[]{:S(2)}) %collective-permute-start.3) | collective-permute-done | bytes 262176 | tf_op jit(solution)/shard_map/ppermute | solution.py:371
  73.3 5.2 %collective-permute-done.5.refs_2_ = bf16[256,512]{1,0:T(8,128)(2,1)S(1)} collective-permute-done((bf16[256,512]{1,0:T(8,128)(2,1)S(1)}, bf16[256,512]{1,0:T(8,128)(2,1)S(1)}, u32[]{:S(2)}, u32[]{:S(2)}) %collective-permute-start.5) | collective-permute-done | bytes 262176 | tf_op jit(solution)/shard_map/ppermute | solution.py:371
  78.5 0.8 %sum.1 = bf16[256,512]{1,0:T(8,128)(2,1)} custom-call(f32[256,512]{1,0:T(8,128)S(1)} %other.2.own_ref, bf16[256,512]{1,0:T(8,128)(2,1)S(1)} %collective-permute-done.3.refs_0_, bf16[256,512]{1,0:T(8,128)(2,1)S(1)} %collective-permute-done.4.refs_1_, bf16[256,512]{1,0:T(8,128)(2,1)S(1)} %collective-permute-done.5.refs_2_), custom_call_target="tpu_custom_call" | custom-call | tf_op jit(solution)/shard_map/sum/pallas_call | solution.py:375
  (12 shorter events, 0.2 us)
Async XLA Ops:
  0.0 14.7 %copy-start.1 = (f32[3,7,512]{2,1,0:T(8,128)S(1)}, f32[3,7,512]{2,1,0:T(8,128)}, u32[]{:S(2)}) copy-start(f32[3,7,512]{2,1,0:T(8,128)} %taps_ref.1) | copy-start | bytes 129028
  2.9 13.5 %copy-start.3 = (f32[512]{0:T(512)S(1)}, f32[512]{0:T(512)}, u32[]{:S(2)}) copy-start(f32[512]{0:T(512)} %param.10) | copy-start | bytes 6148
  2.9 23.4 %copy-start.2 = (f32[2,16,1,256]{3,2,1,0:T(1,128)S(1)}, f32[2,16,1,256]{3,2,1,0:T(1,128)}, u32[]{:S(2)}) copy-start(f32[2,16,1,256]{3,2,1,0:T(1,128)} %constant.30.clone.tw_ref) | copy-start | bytes 98308
  2.9 49.3 %collective-permute-start.2 = (bf16[512,2048]{1,0:T(8,128)(2,1)}, bf16[512,2048]{1,0:T(8,128)(2,1)S(1)}, u32[]{:S(2)}, u32[]{:S(2)}) collective-permute-start(bf16[512,2048]{1,0:T(8,128)(2,1)} %get-tuple-element.15), channel_id=1, source_target_pairs={{0,2},{3,5},{2,0},{5,3},{4,6},{7,9},{6,4},{9,7},{8,10},{11,13},{10... | collective-permute-start | bytes 6291464 | tf_op jit(solution)/shard_map/ppermute | solution.py:308
  4.8 21.5 %all-to-all-start = ((bf16[16,96,256]{2,1,0:T(8,128)(2,1)}), bf16[16,96,256]{2,1,0:T(8,128)(2,1)S(1)}, u32[]{:S(2)}, u32[]{:S(2)}) async-start(bf16[16,96,256]{2,1,0:T(8,128)(2,1)} %get-tuple-element.12), calls=%async_computation | async-start | bytes 1572864 | tf_op jit(solution)/shard_map/all_to_all | solution.py:307
  10.9 9.8 %collective-permute-start = (bf16[16,512]{1,0:T(8,128)(2,1)S(1)}, bf16[16,512]{1,0:T(8,128)(2,1)S(1)}, u32[]{:S(2)}, u32[]{:S(2)}) collective-permute-start(bf16[16,512]{1,0:T(8,128)(2,1)S(1)} %slice_bitcast_fusion.1), channel_id=1, source_target_pairs={{0,16},{16,32},{32,48},{48,64},{64,80},{80,96},{96,112},{112,128},... | collective-permute-start | bytes 49160 | tf_op jit(solution)/shard_map/ppermute | solution.py:310
  20.7 0.9 %copy-start = (bf16[256,512]{1,0:T(8,128)(2,1)S(1)}, bf16[256,512]{1,0:T(8,128)(2,1)}, u32[]{:S(2)}) copy-start(bf16[256,512]{1,0:T(8,128)(2,1)} %slice_bitcast_fusion.now_ref) | copy-start | bytes 786436
  44.9 7.3 %collective-permute-start.1 = (bf16[256,512]{1,0:T(8,128)(2,1)S(1)}, bf16[256,512]{1,0:T(8,128)(2,1)S(1)}, u32[]{:S(2)}, u32[]{:S(2)}) collective-permute-start(bf16[256,512]{1,0:T(8,128)(2,1)S(1)} %mix.1.mixed_ref), channel_id=1, source_target_pairs={{0,2},{3,5},{2,0},{5,3},{4,6},{7,9},{6,4},{9,7},{8,10},{11,13},{10... | collective-permute-start | bytes 786440 | tf_op jit(solution)/shard_map/ppermute | solution.py:349
  52.8 20.5 %collective-permute-start.3 = (bf16[256,512]{1,0:T(8,128)(2,1)S(1)}, bf16[256,512]{1,0:T(8,128)(2,1)S(1)}, u32[]{:S(2)}, u32[]{:S(2)}) collective-permute-start(bf16[256,512]{1,0:T(8,128)(2,1)S(1)} %get-tuple-element.16), channel_id=1, source_target_pairs={{0,14},{4,10},{10,4},{14,0},{2,12},{6,8},{8,6},{12,2},{3,1},{7,13}... | collective-permute-start | bytes 786440 | tf_op jit(solution)/shard_map/ppermute | solution.py:371
  57.3 16.0 %collective-permute-start.4 = (bf16[256,512]{1,0:T(8,128)(2,1)S(1)}, bf16[256,512]{1,0:T(8,128)(2,1)S(1)}, u32[]{:S(2)}, u32[]{:S(2)}) collective-permute-start(bf16[256,512]{1,0:T(8,128)(2,1)S(1)} %get-tuple-element.17), channel_id=1, source_target_pairs={{0,4},{4,0},{10,14},{14,10},{2,6},{6,2},{8,12},{12,8},{3,7},{7,3},... | collective-permute-start | bytes 786440 | tf_op jit(solution)/shard_map/ppermute | solution.py:371
  57.6 20.9 %collective-permute-start.5 = (bf16[256,512]{1,0:T(8,128)(2,1)S(1)}, bf16[256,512]{1,0:T(8,128)(2,1)S(1)}, u32[]{:S(2)}, u32[]{:S(2)}) collective-permute-start(bf16[256,512]{1,0:T(8,128)(2,1)S(1)} %get-tuple-element.18), channel_id=1, source_target_pairs={{0,10},{4,14},{10,0},{14,4},{2,8},{6,12},{8,2},{12,6},{3,13},{7,1}... | collective-permute-start | bytes 786440 | tf_op jit(solution)/shard_map/ppermute | solution.py:371
